TPU v7x, 128 devices: a whole 4x4x4 slice. The times are simulated.
128 devices in a mesh: ctx: 16 (over z, x_lo, core), head: 8 (over y, x_hi).
Axes of the slice: x: 4 (x_hi: 2, x_lo: 2; x = x_hi * 2 + x_lo), y: 4, z: 4, core: 2. Of those that a mesh axis runs over, the one named last changes fastest.
Arguments:
- queries: bfloat16 [8192, 4096], P('ctx', 'head'), may hold values from -5 to 5
- key_rows: bfloat16 [8192, 4096], P('ctx', 'head'), may hold values from -5 to 5
- value_rows: bfloat16 [8192, 4096], P('ctx', 'head'), may hold values from -6 to 6
- out_weight: bfloat16 [4096, 4096], P('head'), may hold values from -0.125 to 0.125
- output_grad: bfloat16 [8192, 4096], P('ctx'), may hold values from -6 to 6
Outputs:
- layer_output: bfloat16 [8192, 4096], P('ctx', 'head')
- query_grad: bfloat16 [8192, 4096], P('ctx', 'head')
- key_grad: bfloat16 [8192, 4096], P('ctx', 'head')
- value_grad: bfloat16 [8192, 4096], P('ctx', 'head')
- weight_grad: bfloat16 [4096, 4096], P('head', 'ctx')
All inputs are finite; a program needn't handle non-finite values.
Results may differ from a plain program's by a relative error of at most 0.023.
Values may be sent and summed in bfloat16 or wider, within the bound.
No kernel may reach another device: no remote copies, remote signals or barrier semaphores. Data moves between devices by JAX's collectives and lax.ppermute only.
A program may use at most 192 MiB of HBM per device.

v0:
```python
import functools
import math

import jax
import jax.numpy as jnp
from jax import lax
from jax.experimental import pallas as pl
from jax.experimental.pallas import tpu as pltpu
from jax.sharding import PartitionSpec as P

HD = 128
BF = jnp.bfloat16
F32 = jnp.float32
SCALE = 1.0 / math.sqrt(HD)
LOG2E = math.log2(math.e)
VMEM_LIMIT = 56 * 1024 * 1024


def params(**kw):
    return pltpu.CompilerParams(vmem_limit_bytes=VMEM_LIMIT, **kw)


def mm(a, b, dims):
    return lax.dot_general(a, b, (dims, ((), ())), preferred_element_type=F32)


NN = ((1,), (0,))
NT = ((1,), (1,))
TN = ((0,), (0,))


def swap(value, axis, mask):
    size = lax.axis_size(axis)
    return lax.ppermute(value, axis, [(i, i ^ mask) for i in range(size)])


def shape(dims, dtype=BF):
    return jax.ShapeDtypeStruct(dims, dtype)


def grad_attention_kernel(pos, w_ref, g_ref, keep_ref, send_ref, other_ref, acc):
    step = pl.program_id(0)
    core = pos[0]

    @pl.when(step == 0)
    def _():
        acc[...] = jnp.zeros_like(acc)

    acc[...] += mm(w_ref[...], g_ref[...], NT)
    half = g_ref.shape[1] // 2
    for part in range(2):
        away = pl.multiple_of((1 - core) * 256 + part * 512, 256)
        other_ref[:, part * 256 : (part + 1) * 256] = g_ref[:, pl.ds(away, 256)]
    del half

    @pl.when(step == pl.num_programs(0) - 1)
    def _():
        keep_ref[...] = acc[pl.ds(pl.multiple_of(core * 256, 256), 256), :].astype(BF)
        send_ref[...] = acc[pl.ds(pl.multiple_of((1 - core) * 256, 256), 256), :].astype(BF)


def grad_attention_call(pos, out_weight, output_grad):
    width = output_grad.shape[1]
    step = 1024
    return pl.pallas_call(
        grad_attention_kernel,
        grid_spec=pltpu.PrefetchScalarGridSpec(
            num_scalar_prefetch=1,
            grid=(width // step,),
            in_specs=[
                pl.BlockSpec((512, step), lambda i, pos: (0, i)),
                pl.BlockSpec((512, step), lambda i, pos: (0, i)),
            ],
            out_specs=[
                pl.BlockSpec((256, 512), lambda i, pos: (0, 0)),
                pl.BlockSpec((256, 512), lambda i, pos: (0, 0)),
                pl.BlockSpec((512, step // 2), lambda i, pos: (0, i)),
            ],
            scratch_shapes=[pltpu.VMEM((512, 512), F32)],
        ),
        out_shape=[shape((256, 512)), shape((256, 512)), shape((512, width // 2))],
        compiler_params=params(),
        name="grad_attention",
    )(pos, out_weight, output_grad)


def band(rows, cols, ratio, weight, row_major):
    r = lax.broadcasted_iota(jnp.int32, (rows, cols), 0)
    c = lax.broadcasted_iota(jnp.int32, (rows, cols), 1)
    hit = (c // ratio == r) if row_major else (r // ratio == c)
    return jnp.where(hit, weight, 0.0).astype(BF)


def pool_kernel(pos, q_ref, k_ref, v_ref, recv_ref, qt_ref, kv_ref, l1_ref, l2_ref, l3_ref):
    kv_ref[:512, :256] = k_ref[...]
    kv_ref[:512, 256:] = v_ref[...]
    kv_ref[512:, :256] = recv_ref[1]
    kv_ref[512:, 256:] = recv_ref[2]
    fold = band(256, 512, 2, 0.5, True)
    l1_ref[:256, :] = mm(fold, kv_ref[:512, :], NN).astype(BF)
    l1_ref[256:, :] = mm(fold, kv_ref[512:, :], NN).astype(BF)
    l2_ref[...] = mm(fold, l1_ref[...], NN).astype(BF)
    l3_ref[...] = mm(fold[:128, :256], l2_ref[...], NN).astype(BF)
    qt_ref[:, :512] = q_ref[...].T
    qt_ref[:, 512:] = recv_ref[0].T


def pool_call(pos, queries, keys, values, recv):
    own = pl.BlockSpec((512, 256), lambda i, pos: (0, pos[0]))

    def whole(*dims):
        return pl.BlockSpec(dims, lambda i, pos: (0,) * len(dims))

    return pl.pallas_call(
        pool_kernel,
        grid_spec=pltpu.PrefetchScalarGridSpec(
            num_scalar_prefetch=1,
            grid=(1,),
            in_specs=[own, own, own, whole(3, 512, 256)],
            out_specs=[
                whole(256, 1024),
                whole(1024, 512),
                whole(512, 512),
                whole(256, 512),
                whole(128, 512),
            ],
        ),
        out_shape=[
            shape((256, 1024)),
            shape((1024, 512)),
            shape((512, 512)),
            shape((256, 512)),
            shape((128, 512)),
        ],
        compiler_params=params(),
        name="pool",
    )(pos, queries, keys, values, recv)


def score_block(key, value, qt_ref, e_ref, slot, carry):
    new = []
    for c, (m_run, l_run, acc) in enumerate(carry):
        cols = slice(c * QC, (c + 1) * QC)
        s = mm(key, qt_ref[:, cols], NN)
        m = jnp.max(s, axis=0, keepdims=True) * (SCALE * LOG2E)
        e = jnp.exp2(s * (SCALE * LOG2E) - m)
        l = jnp.sum(e, axis=0, keepdims=True)
        e_low = e.astype(BF)
        e_ref[0, slot, :, cols] = e_low
        u = mm(value, e_low, TN)
        if m_run is None:
            new.append((m, l, u, m))
        else:
            top = jnp.maximum(m_run, m)
            f_run, f_new = jnp.exp2(m_run - top), jnp.exp2(m - top)
            new.append((top, l_run * f_run + l * f_new, acc * f_run + u * f_new, m))
    return new


QC = 512
NQ = 2


def near_kernel(qt_ref, kv_k, kv_v, e_ref, acc_ref, st_ref):
    carry = [(None, None, None)] * NQ
    tops = []
    for j in range(2):
        rows = slice(j * 512, (j + 1) * 512)
        got = score_block(kv_k[rows, :], kv_v[rows, :], qt_ref, e_ref, j, carry)
        carry = [g[:3] for g in got]
        tops.append([g[3] for g in got])
    for c in range(NQ):
        cols = slice(c * QC, (c + 1) * QC)
        m, l, acc = carry[c]
        acc_ref[:, cols] = acc
        st_ref[0, 0:1, cols] = m
        st_ref[0, 1:2, cols] = l
        st_ref[0, 2:3, cols] = tops[0][c]
        st_ref[0, 3:4, cols] = tops[1][c]


def near_call(qt, kv):
    return pl.pallas_call(
        near_kernel,
        grid=(2,),
        in_specs=[
            pl.BlockSpec((128, 1024), lambda h: (h, 0)),
            pl.BlockSpec((1024, 128), lambda h: (0, h)),
            pl.BlockSpec((1024, 128), lambda h: (0, h + 2)),
        ],
        out_specs=[
            pl.BlockSpec((1, 2, 512, 1024), lambda h: (h, 0, 0, 0)),
            pl.BlockSpec((128, 1024), lambda h: (h, 0)),
            pl.BlockSpec((1, 8, 1024), lambda h: (h, 0, 0)),
        ],
        out_shape=[
            shape((2, 2, 512, 1024)),
            shape((256, 1024), F32),
            shape((2, 8, 1024), F32),
        ],
        compiler_params=params(),
        name="near_scores",
    )(qt, kv, kv)


FAR_ROWS = (512, 256, 256, 128, 128, 128, 128)


def gather_far(refs, dst):
    at = 0
    for ref, rows in zip(refs, FAR_ROWS):
        dst[at : at + rows, :] = ref[...]
        at += rows


def far_kernel(qt_ref, *refs):
    keys, values = refs[:7], refs[7:14]
    acc_ref, st_ref, e_ref, o_ref, s_ref, k_all, v_all = refs[14:]
    gather_far(keys, k_all)
    gather_far(values, v_all)
    carry = []
    for c in range(NQ):
        cols = slice(c * QC, (c + 1) * QC)
        carry.append((st_ref[0, 0:1, cols], st_ref[0, 1:2, cols], acc_ref[:, cols]))
    tops = [[st_ref[0, 2 + j : 3 + j, c * QC : (c + 1) * QC] for c in range(NQ)] for j in range(2)]
    for j in range(3):
        rows = slice(j * 512, (j + 1) * 512)
        got = score_block(k_all[rows, :], v_all[rows, :], qt_ref, e_ref, j, carry)
        carry = [g[:3] for g in got]
        tops.append([g[3] for g in got])
    for c in range(NQ):
        cols = slice(c * QC, (c + 1) * QC)
        m, l, acc = carry[c]
        inv = 1.0 / l
        o_ref[:, cols] = (acc * inv).astype(BF)
        for j in range(5):
            s_ref[0, j : j + 1, cols] = jnp.exp2(tops[j][c] - m) * inv


def far_specs(offset):
    return [pl.BlockSpec((rows, 128), functools.partial(lambda o, h: (0, h + o), offset)) for rows in FAR_ROWS]


def far_call(qt, far, acc, stats):
    return pl.pallas_call(
        far_kernel,
        grid=(2,),
        in_specs=[
            pl.BlockSpec((128, 1024), lambda h: (h, 0)),
            *far_specs(0),
            *far_specs(2),
            pl.BlockSpec((128, 1024), lambda h: (h, 0)),
            pl.BlockSpec((1, 8, 1024), lambda h: (h, 0, 0)),
        ],
        out_specs=[
            pl.BlockSpec((1, 3, 512, 1024), lambda h: (h, 0, 0, 0)),
            pl.BlockSpec((128, 1024), lambda h: (h, 0)),
            pl.BlockSpec((1, 8, 1024), lambda h: (h, 0, 0)),
        ],
        out_shape=[
            shape((2, 3, 512, 1024)),
            shape((256, 1024)),
            shape((2, 8, 1024), F32),
        ],
        scratch_shapes=[pltpu.VMEM((1536, 128), BF), pltpu.VMEM((1536, 128), BF)],
        compiler_params=params(),
        name="far_scores",
    )(qt, *far, *far, acc, stats)


def project_kernel(pos, o_ref, r_ref, w_mine, w_other, a0, a1, a2, a3, b0, b1, mine, other):
    step = pl.program_id(0)

    @pl.when(step == 0)
    def _():
        mine[...] = o_ref[:, :512].T
        other[...] = r_ref[:, 512:].T

    out = (mm(mine[...], w_mine[...], NN) + mm(other[...], w_other[...], NN)).astype(BF)
    for dy, a in enumerate((a0, a1, a2, a3)):
        for dx, b in enumerate((b0, b1)):

            @pl.when(step == ORDER.index((dy, dx)))
            def _():
                a[:, dx * 512 : (dx + 1) * 512] = out[:256]
                b[dy] = out[256:]


ORDER = [(2, 1), (1, 1), (3, 1), (0, 1), (2, 0), (1, 0), (3, 0), (0, 0)]


def project_target(i):
    dy = jnp.where(i % 4 == 0, 2, jnp.where(i % 4 == 1, 1, jnp.where(i % 4 == 2, 3, 0)))
    dx = 1 - i // 4
    return dy * 2 + dx


def project_call(pos, attn, attn_other, out_weight):
    def whole(*dims):
        return pl.BlockSpec(dims, lambda i, pos: (0,) * len(dims))

    def weight(flip):
        return pl.BlockSpec(
            (256, 512), lambda i, pos: (pos[0] ^ flip, pos[1] ^ project_target(i))
        )

    return pl.pallas_call(
        project_kernel,
        grid_spec=pltpu.PrefetchScalarGridSpec(
            num_scalar_prefetch=1,
            grid=(8,),
            in_specs=[whole(256, 1024), whole(256, 1024), weight(0), weight(1)],
            out_specs=[whole(256, 1024)] * 4 + [whole(4, 256, 512)] * 2,
            scratch_shapes=[pltpu.VMEM((512, 256), BF), pltpu.VMEM((512, 256), BF)],
        ),
        out_shape=[shape((256, 1024))] * 4 + [shape((4, 256, 512))] * 2,
        compiler_params=params(),
        name="project",
    )(pos, attn, attn_other, out_weight, out_weight)


def weight_kernel(pos, o_ref, r_ref, g_own, g_recv, w0, w1, w2, w3):
    step = pl.program_id(0)
    core = pos[0]
    own, far = g_own[...], g_recv[...]
    up = (mm(o_ref[:, :512], own, NN) + mm(o_ref[:, 512:], far, NN)).astype(BF)
    down = (mm(r_ref[:, 512:], own, NN) + mm(r_ref[:, :512], far, NN)).astype(BF)
    first = pl.ds(pl.multiple_of(core * 256, 256), 256)
    second = pl.ds(pl.multiple_of((1 - core) * 256, 256), 256)
    for dz, w in enumerate((w0, w1, w2, w3)):

        @pl.when(step // 2 == dz)
        def _():
            w[step % 2, first, :] = up
            w[step % 2, second, :] = down


def weight_call(pos, attn, attn_other, output_grad, grad_recv):
    def whole(*dims):
        return pl.BlockSpec(dims, lambda i, pos: (0,) * len(dims))

    return pl.pallas_call(
        weight_kernel,
        grid_spec=pltpu.PrefetchScalarGridSpec(
            num_scalar_prefetch=1,
            grid=(8,),
            in_specs=[
                whole(256, 1024),
                whole(256, 1024),
                pl.BlockSpec((512, 256), lambda i, pos: (0, (pos[2] ^ i) * 2 + pos[0])),
                pl.BlockSpec((512, 256), lambda i, pos: (0, pos[2] ^ i)),
            ],
            out_specs=[whole(2, 512, 256)] * 4,
        ),
        out_shape=[shape((2, 512, 256))] * 4,
        compiler_params=params(),
        name="weight_term",
    )(pos, attn, attn_other, output_grad, grad_recv)


def grad_block(key, value, qt, da, row_dot, s, e_ref, slot, ds_ref, dq_ref, first):
    da_low = (da * s).astype(BF)
    dot_scaled = row_dot * s
    for c in range(NQ):
        cols = slice(c * QC, (c + 1) * QC)
        dp = mm(value, da_low[:, cols], NN)
        ds = (e_ref[0, slot, :, cols].astype(F32) * (dp - dot_scaled[:, cols])).astype(BF)
        ds_ref[:, cols] = ds
        part = mm(key, ds, TN)
        if first:
            dq_ref[:, cols] = part
        else:
            dq_ref[:, cols] += part
    dk = mm(ds_ref[...], qt, NT) * SCALE
    dv = mm(e_ref[0, slot], da_low, NT)
    return dk, dv


def grad_rows(da_own, da_recv, o_ref):
    da = jnp.concatenate([da_own[...], da_recv[...]], axis=1).astype(F32)
    return da, jnp.sum(da * o_ref[...].astype(F32), axis=0, keepdims=True)


def far_grad_kernel(qt_ref, da_own, da_recv, o_ref, s_ref, e_ref, *refs):
    keys, values = refs[:7], refs[7:14]
    outs = refs[14:21]
    dq_ref, k_all, v_all, ds_ref = refs[21:]
    head = pl.program_id(0)
    gather_far(keys, k_all)
    gather_far(values, v_all)
    da, row_dot = grad_rows(da_own, da_recv, o_ref)
    k_cols = pl.ds(pl.multiple_of(head * 128, 128), 128)
    v_cols = pl.ds(pl.multiple_of(head * 128 + 256, 128), 128)
    qt = qt_ref[...]
    at = 0
    for j in range(3):
        rows = slice(j * 512, (j + 1) * 512)
        s = s_ref[0, 2 + j : 3 + j, :]
        dk, dv = grad_block(
            k_all[rows, :], v_all[rows, :], qt, da, row_dot, s, e_ref, j, ds_ref, dq_ref, j == 0
        )
        lo = 0
        while lo < 512:
            n = FAR_ROWS[at]
            outs[at][:, k_cols] = dk[lo : lo + n].astype(BF)
            outs[at][:, v_cols] = dv[lo : lo + n].astype(BF)
            lo += n
            at += 1


def common_specs():
    return [
        pl.BlockSpec((128, 1024), lambda h: (h, 0)),
        pl.BlockSpec((128, 512), lambda h: (h, 0)),
        pl.BlockSpec((128, 512), lambda h: (h, 0)),
        pl.BlockSpec((128, 1024), lambda h: (h, 0)),
        pl.BlockSpec((1, 8, 1024), lambda h: (h, 0, 0)),
    ]


def far_grad_call(qt, da_own, da_recv, attn, scales, e_far, far):
    return pl.pallas_call(
        far_grad_kernel,
        grid=(2,),
        in_specs=[
            *common_specs(),
            pl.BlockSpec((1, 3, 512, 1024), lambda h: (h, 0, 0, 0)),
            *far_specs(0),
            *far_specs(2),
        ],
        out_specs=[pl.BlockSpec((rows, 512), lambda h: (0, 0)) for rows in FAR_ROWS]
        + [pl.BlockSpec((128, 1024), lambda h: (h, 0))],
        out_shape=[shape((rows, 512)) for rows in FAR_ROWS] + [shape((256, 1024), F32)],
        scratch_shapes=[
            pltpu.VMEM((1536, 128), BF),
            pltpu.VMEM((1536, 128), BF),
            pltpu.VMEM((512, 1024), BF),
        ],
        compiler_params=params(),
        name="far_grads",
    )(qt, da_own, da_recv, attn, scales, e_far, *far, *far)


def near_grad_kernel(
    qt_ref, da_own, da_recv, o_ref, s_ref, e_ref, kv_k, kv_v, dq_in, kv_ref, q_own, q_send, ds_ref, dq_ref
):
    head = pl.program_id(0)
    da, row_dot = grad_rows(da_own, da_recv, o_ref)
    k_cols = pl.ds(pl.multiple_of(head * 128, 128), 128)
    v_cols = pl.ds(pl.multiple_of(head * 128 + 256, 128), 128)
    qt = qt_ref[...]
    dq_ref[...] = dq_in[...]
    for j in range(2):
        rows = slice(j * 512, (j + 1) * 512)
        s = s_ref[0, j : j + 1, :]
        dk, dv = grad_block(
            kv_k[rows, :], kv_v[rows, :], qt, da, row_dot, s, e_ref, j, ds_ref, dq_ref, False
        )
        kv_ref[rows, k_cols] = dk
        kv_ref[rows, v_cols] = dv
    q_own[...] = (dq_ref[:, :512] * SCALE).T.astype(BF)
    q_send[...] = (dq_ref[:, 512:] * SCALE).T.astype(BF)


def near_grad_call(qt, da_own, da_recv, attn, scales, e_near, kv, dq):
    return pl.pallas_call(
        near_grad_kernel,
        grid=(2,),
        in_specs=[
            *common_specs(),
            pl.BlockSpec((1, 2, 512, 1024), lambda h: (h, 0, 0, 0)),
            pl.BlockSpec((1024, 128), lambda h: (0, h)),
            pl.BlockSpec((1024, 128), lambda h: (0, h + 2)),
            pl.BlockSpec((128, 1024), lambda h: (h, 0)),
        ],
        out_specs=[
            pl.BlockSpec((1024, 512), lambda h: (0, 0)),
            pl.BlockSpec((512, 128), lambda h: (0, h)),
            pl.BlockSpec((512, 128), lambda h: (0, h)),
        ],
        out_shape=[shape((1024, 512), F32), shape((512, 256)), shape((512, 256))],
        scratch_shapes=[pltpu.VMEM((512, 1024), BF), pltpu.VMEM((128, 1024), F32)],
        compiler_params=params(),
        name="near_grads",
    )(qt, da_own, da_recv, attn, scales, e_near, kv, kv, dq)


def collect_kernel(kv_ref, *refs):
    back, own_ref, send_ref = refs[:7], refs[7], refs[8]
    for part, out in ((1, send_ref), (0, own_ref)):
        total = kv_ref[part * 512 : (part + 1) * 512, :]
        for level, group in ((1, back[:1]), (2, back[1:3]), (3, back[3:])):
            n = 512 >> level
            rows = slice(part * n, (part + 1) * n)
            spread = band(512, n, 1 << level, 0.5**level, False)
            for ref in group:
                total = total + mm(spread, ref[rows, :], NN)
        out[...] = total.astype(BF)


def collect_call(kv_grad, back):
    def whole(*dims):
        return pl.BlockSpec(dims, lambda i: (0,) * len(dims))

    return pl.pallas_call(
        collect_kernel,
        grid=(1,),
        in_specs=[whole(1024, 512)] + [whole(rows, 512) for rows in FAR_ROWS],
        out_specs=[whole(512, 512)] * 2,
        out_shape=[shape((512, 512))] * 2,
        compiler_params=params(),
        name="collect",
    )(kv_grad, *back)


def place_kernel(pos, q_own, q_recv, kv_own, kv_recv, q_out, k_out, v_out):
    mine = pl.ds(pl.multiple_of(pos[0] * 256, 256), 256)
    other = pl.ds(pl.multiple_of((1 - pos[0]) * 256, 256), 256)
    q_out[:, mine] = q_own[...]
    q_out[:, other] = q_recv[...]
    k_out[:, mine] = kv_own[:, :256]
    k_out[:, other] = kv_recv[:, :256]
    v_out[:, mine] = kv_own[:, 256:]
    v_out[:, other] = kv_recv[:, 256:]


def place_call(pos, q_own, q_recv, kv_own, kv_recv):
    def whole(*dims):
        return pl.BlockSpec(dims, lambda i, pos: (0,) * len(dims))

    return pl.pallas_call(
        place_kernel,
        grid_spec=pltpu.PrefetchScalarGridSpec(
            num_scalar_prefetch=1,
            grid=(1,),
            in_specs=[whole(512, 256)] * 2 + [whole(512, 512)] * 2,
            out_specs=[whole(512, 512)] * 3,
        ),
        out_shape=[shape((512, 512))] * 3,
        compiler_params=params(),
        name="place",
    )(pos, q_own, q_recv, kv_own, kv_recv)


FAR_MASKS = (2, 4, 6, 8, 10, 12, 14)


def add(*terms):
    return functools.reduce(jnp.add, [t.astype(F32) for t in terms])


def shards(queries, key_rows, value_rows, out_weight, output_grad):
    ctx = lax.axis_index("ctx")
    core = ctx % 2
    pos = jnp.stack([core, lax.axis_index("head"), ctx // 2]).astype(jnp.int32)

    away = [
        lax.dynamic_slice_in_dim(a, (1 - core) * 256, 256, axis=1)
        for a in (queries, key_rows, value_rows)
    ]
    recv = swap(jnp.stack(away), "ctx", 1)
    da_own, da_send, grad_send = grad_attention_call(pos, out_weight, output_grad)
    da_recv = swap(da_send, "ctx", 1)
    grad_recv = swap(grad_send, "ctx", 1)

    qt, kv, l1, l2, l3 = pool_call(pos, queries, key_rows, value_rows, recv)
    pooled = (l1, l2, l2, l3, l3, l3, l3)
    far = [swap(a, "ctx", mask) for a, mask in zip(pooled, FAR_MASKS)]
    e_near, acc, stats = near_call(qt, kv)
    e_far, attn, scales = far_call(qt, far, acc, stats)

    attn_other = swap(attn, "ctx", 1)
    a0, a1, a2, a3, b0, b1 = project_call(pos, attn, attn_other, out_weight)
    b_recv = swap(b1, "head", 1)
    a_recv = [swap(a, "head", 2 * dy) for dy, a in ((1, a1), (2, a2), (3, a3))]

    w_parts = weight_call(pos, attn, attn_other, output_grad, grad_recv)
    w_recv = [swap(w_parts[dz], "ctx", 4 * dz) for dz in (1, 2, 3)]

    *level_grads, dq = far_grad_call(qt, da_own, da_recv, attn, scales, e_far, far)
    back = [swap(g, "ctx", mask) for g, mask in zip(level_grads, FAR_MASKS)]
    kv_grad, q_own, q_send = near_grad_call(qt, da_own, da_recv, attn, scales, e_near, kv, dq)
    q_recv = swap(q_send, "ctx", 1)

    b_sum = add(b0, b_recv)
    b_back = [swap(b_sum[dy].astype(BF), "head", 2 * dy) for dy in (1, 2, 3)]
    a_sum = add(a0, *a_recv)
    a_back = swap(a_sum[:, 512:].astype(BF), "head", 1)
    w_sum = add(w_parts[0], *w_recv)
    w_back = swap(w_sum[1].astype(BF), "ctx", 2)

    layer_output = jnp.concatenate(
        [add(a_sum[:, :512], a_back), add(b_sum[0], *b_back)], axis=0
    ).astype(BF)
    weight_grad = add(w_sum[0], w_back).astype(BF)

    kv_own, kv_send = collect_call(kv_grad, back)
    kv_recv = swap(kv_send, "ctx", 1)
    query_grad, key_grad, value_grad = place_call(pos, q_own, q_recv, kv_own, kv_recv)
    return (layer_output, query_grad, key_grad, value_grad, weight_grad)


def solution(mesh):
    placed = (P("ctx", "head"), P("ctx", "head"), P("ctx", "head"), P("head", None), P("ctx", None))
    return jax.shard_map(
        shards,
        mesh=mesh,
        in_specs=placed,
        out_specs=(
            P("ctx", "head"),
            P("ctx", "head"),
            P("ctx", "head"),
            P("ctx", "head"),
            P("head", "ctx"),
        ),
        check_vma=False,
    )
```

profile of v0, /device:TPU:0, one launch (start us, length us, event | category | flops | bytes accessed | tf_op | source)
XLA Modules:
  0.0 194.0 jit_solution(4312691890821698539)
XLA Ops:
  3.5 7.6 %grad_attention.1 = (bf16[256,512]{1,0:T(8,128)(2,1)}, bf16[256,512]{1,0:T(8,128)(2,1)}, bf16[512,2048]{1,0:T(8,128)(2,1)}) custom-call(s32[3]{0:T(128)} %pad_add_fusion.pos, bf16[512,4096]{1,0:T(8,128)(2,1)} %w_ref.1, bf16[512,4096]{1,0:T(8,128)(2,1)} %g_own.1), custom_call_target="tpu_custom_call" | custom-call | tf_op jit(solution)/shard_map/grad_attention/pallas_call | solution.py:65
  12.5 3.6 %pool.1 = (bf16[256,1024]{1,0:T(8,128)(2,1)}, bf16[1024,512]{1,0:T(8,128)(2,1)}, bf16[512,512]{1,0:T(8,128)(2,1)}, bf16[256,512]{1,0:T(8,128)(2,1)}, bf16[128,512]{1,0:T(8,128)(2,1)}) custom-call(s32[3]{0:T(128)} %pad_add_fusion.pos, bf16[512,512]{1,0:T(8,128)(2,1)} %q_ref.1, bf16[512,512]{1,0:T(8,128)(2,1)} %k_ref.1, bf16[512,512]{1,0:T(8,128)(2,1)} %v_ref.1, ...), custom_call_target="tpu_custom_call" | custom-call | tf_op jit(solution)/shard_map/pool/pallas_call | solution.py:114
  17.7 4.0 %collective-permute-start.7 = (bf16[128,512]{1,0:T(8,128)(2,1)}, bf16[128,512]{1,0:T(8,128)(2,1)S(1)}, u32[]{:S(2)}, u32[]{:S(2)}) collective-permute-start(bf16[128,512]{1,0:T(8,128)(2,1)} %get-tuple-element.48), channel_id=1, source_target_pairs={{0,112},{8,120},{16,96},{24,104},{32,80},{40,88},{48,64},{56,72},{... | collective-permute-start | bytes 393224 | tf_op jit(solution)/shard_map/ppermute | solution.py:34
  21.8 2.8 %collective-permute-start.5 = (bf16[128,512]{1,0:T(8,128)(2,1)}, bf16[128,512]{1,0:T(8,128)(2,1)S(1)}, u32[]{:S(2)}, u32[]{:S(2)}) collective-permute-start(bf16[128,512]{1,0:T(8,128)(2,1)} %get-tuple-element.48), channel_id=1, source_target_pairs={{0,80},{8,88},{16,64},{24,72},{32,112},{40,120},{48,96},{56,104},{... | collective-permute-start | bytes 393224 | tf_op jit(solution)/shard_map/ppermute | solution.py:34
  24.5 13.1 %collective-permute-done.7.refs_6_.refs_13_ = bf16[128,512]{1,0:T(8,128)(2,1)S(1)} collective-permute-done((bf16[128,512]{1,0:T(8,128)(2,1)}, bf16[128,512]{1,0:T(8,128)(2,1)S(1)}, u32[]{:S(2)}, u32[]{:S(2)}) %collective-permute-start.7) | collective-permute-done | bytes 131104 | tf_op jit(solution)/shard_map/ppermute | solution.py:34
  38.2 2.4 %collective-permute-start.2 = (bf16[256,512]{1,0:T(8,128)(2,1)}, bf16[256,512]{1,0:T(8,128)(2,1)S(1)}, u32[]{:S(2)}, u32[]{:S(2)}) collective-permute-start(bf16[256,512]{1,0:T(8,128)(2,1)} %get-tuple-element.47), channel_id=1, source_target_pairs={{0,32},{8,40},{16,48},{24,56},{32,0},{40,8},{48,16},{56,24},{64,96... | collective-permute-start | bytes 786440 | tf_op jit(solution)/shard_map/ppermute | solution.py:34
  40.9 12.5 %collective-permute-done.4.refs_3_.refs_10_ = bf16[128,512]{1,0:T(8,128)(2,1)S(1)} collective-permute-done((bf16[128,512]{1,0:T(8,128)(2,1)}, bf16[128,512]{1,0:T(8,128)(2,1)S(1)}, u32[]{:S(2)}, u32[]{:S(2)}) %collective-permute-start.4) | collective-permute-done | bytes 131104 | tf_op jit(solution)/shard_map/ppermute | solution.py:34
  53.4 7.2 %near_scores.1 = (bf16[2,2,512,1024]{3,2,1,0:T(8,128)(2,1)}, f32[256,1024]{1,0:T(8,128)}, f32[2,8,1024]{2,1,0:T(8,128)}) custom-call(bf16[256,1024]{1,0:T(8,128)(2,1)} %get-tuple-element.45.qt_ref, bf16[1024,512]{1,0:T(8,128)(2,1)} %get-tuple-element.49.kv_k.kv_v, bf16[1024,512]{1,0:T(8,128)(2,1)} %get-tuple-element.49.kv_k.kv_v), custom_call_target="tpu_custom_call" | custom-call | tf_op jit(solution)/shard_map/near_scores/pallas_call | solution.py:183
  61.6 10.0 %far_scores.1 = (bf16[2,3,512,1024]{3,2,1,0:T(8,128)(2,1)}, bf16[256,1024]{1,0:T(8,128)(2,1)}, f32[2,8,1024]{2,1,0:T(8,128)}) custom-call(bf16[256,1024]{1,0:T(8,128)(2,1)} %get-tuple-element.45.qt_ref, bf16[512,512]{1,0:T(8,128)(2,1)} %copy-done, bf16[256,512]{1,0:T(8,128)(2,1)} %copy-done.2, bf16[256,512]{1,0:T(8,128)(2,1)} %copy-done.1, ...), custom_call_target="tpu_custom_call" | custom-call | tf_op jit(solution)/shard_map/far_scores/pallas_call | solution.py:245
  73.0 10.9 %far_grads.1 = (bf16[512,512]{1,0:T(8,128)(2,1)}, bf16[256,512]{1,0:T(8,128)(2,1)}, bf16[256,512]{1,0:T(8,128)(2,1)}, bf16[128,512]{1,0:T(8,128)(2,1)}, bf16[128...) custom-call(bf16[256,1024]{1,0:T(8,128)(2,1)} %get-tuple-element.45.qt_ref, ...), custom_call_target="tpu_custom_call" | custom-call | tf_op jit(solution)/shard_map/far_grads/pallas_call | solution.py:422
  83.9 2.0 %collective-permute-start.22 = (bf16[128,512]{1,0:T(8,128)(2,1)}, bf16[128,512]{1,0:T(8,128)(2,1)S(1)}, u32[]{:S(2)}, u32[]{:S(2)}) collective-permute-start(bf16[128,512]{1,0:T(8,128)(2,1)} %get-tuple-element.71), channel_id=1, source_target_pairs={{0,64},{8,72},{16,80},{24,88},{32,96},{40,104},{48,112},{56,120},{... | collective-permute-start | bytes 393224 | tf_op jit(solution)/shard_map/ppermute | solution.py:34
  85.9 2.4 %collective-permute-start.23 = (bf16[128,512]{1,0:T(8,128)(2,1)}, bf16[128,512]{1,0:T(8,128)(2,1)S(1)}, u32[]{:S(2)}, u32[]{:S(2)}) collective-permute-start(bf16[128,512]{1,0:T(8,128)(2,1)} %get-tuple-element.72), channel_id=1, source_target_pairs={{0,80},{8,88},{16,64},{24,72},{32,112},{40,120},{48,96},{56,104},{... | collective-permute-start | bytes 393224 | tf_op jit(solution)/shard_map/ppermute | solution.py:34
  88.3 2.1 %collective-permute-start.24 = (bf16[128,512]{1,0:T(8,128)(2,1)}, bf16[128,512]{1,0:T(8,128)(2,1)S(1)}, u32[]{:S(2)}, u32[]{:S(2)}) collective-permute-start(bf16[128,512]{1,0:T(8,128)(2,1)} %get-tuple-element.73), channel_id=1, source_target_pairs={{0,96},{8,104},{16,112},{24,120},{32,64},{40,72},{48,80},{56,88},{... | collective-permute-start | bytes 393224 | tf_op jit(solution)/shard_map/ppermute | solution.py:34
  90.5 3.6 %collective-permute-done.22.refs_3_ = bf16[128,512]{1,0:T(8,128)(2,1)S(1)} collective-permute-done((bf16[128,512]{1,0:T(8,128)(2,1)}, bf16[128,512]{1,0:T(8,128)(2,1)S(1)}, u32[]{:S(2)}, u32[]{:S(2)}) %collective-permute-start.22) | collective-permute-done | bytes 131104 | tf_op jit(solution)/shard_map/ppermute | solution.py:34
  96.8 1.8 collective-permute-start.21
  98.6 1.9 collective-permute-start.25
  100.5 10.3 %project.1 = (bf16[256,1024]{1,0:T(8,128)(2,1)}, bf16[256,1024]{1,0:T(8,128)(2,1)}, bf16[256,1024]{1,0:T(8,128)(2,1)}, bf16[256,1024]{1,0:T(8,128)(2,1)}, bf16[4...) custom-call(s32[3]{0:T(128)} %pad_add_fusion.pos, bf16[256,1024]{1,0:T(8,128)(2,1)} %get-tuple-element.52.o_ref, ...), custom_call_target="tpu_custom_call" | custom-call | tf_op jit(solution)/shard_map/project/pallas_call | solution.py:307
  110.8 7.2 %collective-permute-done.25.refs_6_ = bf16[128,512]{1,0:T(8,128)(2,1)S(1)} collective-permute-done((bf16[128,512]{1,0:T(8,128)(2,1)}, bf16[128,512]{1,0:T(8,128)(2,1)S(1)}, u32[]{:S(2)}, u32[]{:S(2)}) %collective-permute-start.25) | collective-permute-done | bytes 131104 | tf_op jit(solution)/shard_map/ppermute | solution.py:34
  119.5 2.9 %collective-permute-start.10 = (bf16[256,1024]{1,0:T(8,128)(2,1)}, bf16[256,1024]{1,0:T(8,128)(2,1)S(1)}, u32[]{:S(2)}, u32[]{:S(2)}) collective-permute-start(bf16[256,1024]{1,0:T(8,128)(2,1)} %get-tuple-element.55), channel_id=1, source_target_pairs={{0,4},{1,5},{2,6},{3,7},{4,0},{5,1},{6,2},{7,3},{8,12},{9,13},{10,... | collective-permute-start | bytes 1572872 | tf_op jit(solution)/shard_map/ppermute | solution.py:34
  122.7 8.8 %near_grads.1 = (f32[1024,512]{1,0:T(8,128)}, bf16[512,256]{1,0:T(8,128)(2,1)}, bf16[512,256]{1,0:T(8,128)(2,1)}) custom-call(bf16[256,1024]{1,0:T(8,128)(2,1)} %get-tuple-element.45.qt_ref, bf16[256,512]{1,0:T(8,128)(2,1)} %get-tuple-element.59.da_own, bf16[256,512]{1,0:T(8,128)(2,1)} %copy-done.10, bf16[256,1024]{1,0:T(8,128)(2,1)} %get-tuple-element.52.o_ref, ...), custom_call_target="tpu_custom_call" | custom-call | tf_op jit(solution)/shard_map/near_grads/pallas_call | solution.py:466
  132.3 4.8 %collect.1 = (bf16[512,512]{1,0:T(8,128)(2,1)}, bf16[512,512]{1,0:T(8,128)(2,1)}) custom-call(f32[1024,512]{1,0:T(8,128)} %get-tuple-element.67.kv_ref, bf16[512,512]{1,0:T(8,128)(2,1)} %copy-done.12, bf16[256,512]{1,0:T(8,128)(2,1)} %copy-done.16, bf16[256,512]{1,0:T(8,128)(2,1)} %copy-done.17, bf16[128,512]{1,0:T(8,128)(2,1)} %copy-done.19, ...), custom_call_target="tpu_custom_call" | custom-call | tf_op jit(solution)/shard_map/collect/pallas_call | solution.py:505
  138.5 9.1 %weight_term.1 = (bf16[2,512,256]{2,1,0:T(8,128)(2,1)}, bf16[2,512,256]{2,1,0:T(8,128)(2,1)}, bf16[2,512,256]{2,1,0:T(8,128)(2,1)}, bf16[2,512,256]{2,1,0:T(8,128)(2,1)}) custom-call(s32[3]{0:T(128)} %pad_add_fusion.pos, bf16[256,1024]{1,0:T(8,128)(2,1)} %get-tuple-element.52.o_ref, bf16[256,1024]{1,0:T(8,128)(2,1)} %copy-done.8, bf16[512,4096]{1,0:T(8,128)(2,1)} %g_own.1, ...), custom_call_target="tpu_custom_call" | custom-call | tf_op jit(solution)/shard_map/weight_term/pallas_call | solution.py:342
  147.8 4.6 %collective-permute-start.30 = (bf16[2,512,256]{2,1,0:T(8,128)(2,1)}, bf16[2,512,256]{2,1,0:T(8,128)(2,1)S(1)}, u32[]{:S(2)}, u32[]{:S(2)}) collective-permute-start(bf16[2,512,256]{2,1,0:T(8,128)(2,1)} %get-tuple-element.84), channel_id=1, source_target_pairs={{0,96},{8,104},{16,112},{24,120},{32,64},{40,72},{48,80},{56,88},{... | collective-permute-start | bytes 1572872 | tf_op jit(solution)/shard_map/ppermute | solution.py:34
  152.4 2.8 %collective-permute-start.13 = (bf16[4,256,512]{2,1,0:T(8,128)(2,1)}, bf16[4,256,512]{2,1,0:T(8,128)(2,1)S(1)}, u32[]{:S(2)}, u32[]{:S(2)}) collective-permute-start(bf16[4,256,512]{2,1,0:T(8,128)(2,1)} %get-tuple-element.58), channel_id=1, source_target_pairs={{0,1},{1,0},{2,3},{3,2},{4,5},{5,4},{6,7},{7,6},{8,9},{9,8},{10,11... | collective-permute-start | bytes 3145736 | tf_op jit(solution)/shard_map/ppermute | solution.py:34
  156.4 3.2 %place.1 = (bf16[512,512]{1,0:T(8,128)(2,1)}, bf16[512,512]{1,0:T(8,128)(2,1)}, bf16[512,512]{1,0:T(8,128)(2,1)}) custom-call(s32[3]{0:T(128)} %pad_add_fusion.pos, bf16[512,256]{1,0:T(8,128)(2,1)} %get-tuple-element.65.q_own, bf16[512,256]{1,0:T(8,128)(2,1)} %copy-done.18, bf16[512,512]{1,0:T(8,128)(2,1)} %get-tuple-element.75.kv_own, ...), custom_call_target="tpu_custom_call" | custom-call | tf_op jit(solution)/shard_map/place/pallas_call | solution.py:531
  159.6 3.1 %collective-permute-done.28 = bf16[2,512,256]{2,1,0:T(8,128)(2,1)S(1)} collective-permute-done((bf16[2,512,256]{2,1,0:T(8,128)(2,1)}, bf16[2,512,256]{2,1,0:T(8,128)(2,1)S(1)}, u32[]{:S(2)}, u32[]{:S(2)}) %collective-permute-start.28) | collective-permute-done | bytes 524320 | tf_op jit(solution)/shard_map/ppermute | solution.py:34
  162.7 8.1 %collective-permute-done.29 = bf16[2,512,256]{2,1,0:T(8,128)(2,1)S(1)} collective-permute-done((bf16[2,512,256]{2,1,0:T(8,128)(2,1)}, bf16[2,512,256]{2,1,0:T(8,128)(2,1)S(1)}, u32[]{:S(2)}, u32[]{:S(2)}) %collective-permute-start.29) | collective-permute-done | bytes 524320 | tf_op jit(solution)/shard_map/ppermute | solution.py:34
  170.8 4.4 %collective-permute-done.30 = bf16[2,512,256]{2,1,0:T(8,128)(2,1)S(1)} collective-permute-done((bf16[2,512,256]{2,1,0:T(8,128)(2,1)}, bf16[2,512,256]{2,1,0:T(8,128)(2,1)S(1)}, u32[]{:S(2)}, u32[]{:S(2)}) %collective-permute-start.30) | collective-permute-done | bytes 524320 | tf_op jit(solution)/shard_map/ppermute | solution.py:34
  175.8 4.4 %collective-permute-done.13 = bf16[4,256,512]{2,1,0:T(8,128)(2,1)S(1)} collective-permute-done((bf16[4,256,512]{2,1,0:T(8,128)(2,1)}, bf16[4,256,512]{2,1,0:T(8,128)(2,1)S(1)}, u32[]{:S(2)}, u32[]{:S(2)}) %collective-permute-start.13) | collective-permute-done | bytes 1048608 | tf_op jit(solution)/shard_map/ppermute | solution.py:34
  181.1 2.7 %collective-permute-start.16 = (bf16[256,512]{1,0:T(8,128)(2,1)S(1)}, bf16[256,512]{1,0:T(8,128)(2,1)S(1)}, u32[]{:S(2)}, u32[]{:S(2)}) collective-permute-start(bf16[256,512]{1,0:T(8,128)(2,1)S(1)} %get-tuple-element.88), channel_id=1, source_target_pairs={{0,6},{1,7},{2,4},{3,5},{4,2},{5,3},{6,0},{7,1},{8,14},{9,15},{10,... | collective-permute-start | bytes 786440 | tf_op jit(solution)/shard_map/ppermute | solution.py:34
  185.9 2.4 %collective-permute-done.31 = bf16[512,256]{1,0:T(8,128)(2,1)S(1)} collective-permute-done((bf16[512,256]{1,0:T(8,128)(2,1)S(1)}, bf16[512,256]{1,0:T(8,128)(2,1)S(1)}, u32[]{:S(2)}, u32[]{:S(2)}) %collective-permute-start.31) | collective-permute-done | bytes 262176 | tf_op jit(solution)/shard_map/ppermute | solution.py:34
  189.1 2.1 %collective-permute-done.16 = bf16[256,512]{1,0:T(8,128)(2,1)S(1)} collective-permute-done((bf16[256,512]{1,0:T(8,128)(2,1)S(1)}, bf16[256,512]{1,0:T(8,128)(2,1)S(1)}, u32[]{:S(2)}, u32[]{:S(2)}) %collective-permute-start.16) | collective-permute-done | bytes 262176 | tf_op jit(solution)/shard_map/ppermute | solution.py:34
  (104 shorter events, 24.1 us)
Async XLA Ops:
  2.8 8.8 %collective-permute-start = (bf16[3,512,256]{2,1,0:T(8,128)(2,1)S(1)}, bf16[3,512,256]{2,1,0:T(8,128)(2,1)S(1)}, u32[]{:S(2)}, u32[]{:S(2)}) collective-permute-start(bf16[3,512,256]{2,1,0:T(8,128)(2,1)S(1)} %pad_maximum_fusion), channel_id=1, source_target_pairs={{0,8},{8,0},{16,24},{24,16},{32,40},{40,32},{48,56},{56,48},{64,72... | collective-permute-start | bytes 2359304 | tf_op jit(solution)/shard_map/ppermute | solution.py:34
  11.1 126.0 %collective-permute-start.27 = (bf16[512,2048]{1,0:T(8,128)(2,1)}, bf16[512,2048]{1,0:T(8,128)(2,1)S(1)}, u32[]{:S(2)}, u32[]{:S(2)}) collective-permute-start(bf16[512,2048]{1,0:T(8,128)(2,1)} %get-tuple-element.80), channel_id=1, source_target_pairs={{0,8},{8,0},{16,24},{24,16},{32,40},{40,32},{48,56},{56,48},{64,72... | collective-permute-start | bytes 6291464 | tf_op jit(solution)/shard_map/ppermute | solution.py:34
  16.1 44.5 %collective-permute-start.1 = (bf16[512,512]{1,0:T(8,128)(2,1)}, bf16[512,512]{1,0:T(8,128)(2,1)S(1)}, u32[]{:S(2)}, u32[]{:S(2)}) collective-permute-start(bf16[512,512]{1,0:T(8,128)(2,1)} %get-tuple-element.46), channel_id=1, source_target_pairs={{0,16},{8,24},{16,0},{24,8},{32,48},{40,56},{48,32},{56,40},{64,80... | collective-permute-start | bytes 1572872 | tf_op jit(solution)/shard_map/ppermute | solution.py:34
  17.7 20.0 %collective-permute-start.7 = (bf16[128,512]{1,0:T(8,128)(2,1)}, bf16[128,512]{1,0:T(8,128)(2,1)S(1)}, u32[]{:S(2)}, u32[]{:S(2)}) collective-permute-start(bf16[128,512]{1,0:T(8,128)(2,1)} %get-tuple-element.48), channel_id=1, source_target_pairs={{0,112},{8,120},{16,96},{24,104},{32,80},{40,88},{48,64},{56,72},{... | collective-permute-start | bytes 393224 | tf_op jit(solution)/shard_map/ppermute | solution.py:34
  21.7 16.5 %collective-permute-start.6 = (bf16[128,512]{1,0:T(8,128)(2,1)}, bf16[128,512]{1,0:T(8,128)(2,1)S(1)}, u32[]{:S(2)}, u32[]{:S(2)}) collective-permute-start(bf16[128,512]{1,0:T(8,128)(2,1)} %get-tuple-element.48), channel_id=1, source_target_pairs={{0,96},{8,104},{16,112},{24,120},{32,64},{40,72},{48,80},{56,88},{... | collective-permute-start | bytes 393224 | tf_op jit(solution)/shard_map/ppermute | solution.py:34
  21.8 18.9 %collective-permute-start.5 = (bf16[128,512]{1,0:T(8,128)(2,1)}, bf16[128,512]{1,0:T(8,128)(2,1)S(1)}, u32[]{:S(2)}, u32[]{:S(2)}) collective-permute-start(bf16[128,512]{1,0:T(8,128)(2,1)} %get-tuple-element.48), channel_id=1, source_target_pairs={{0,80},{8,88},{16,64},{24,72},{32,112},{40,120},{48,96},{56,104},{... | collective-permute-start | bytes 393224 | tf_op jit(solution)/shard_map/ppermute | solution.py:34
  37.7 22.9 %collective-permute-start.3 = (bf16[256,512]{1,0:T(8,128)(2,1)}, bf16[256,512]{1,0:T(8,128)(2,1)S(1)}, u32[]{:S(2)}, u32[]{:S(2)}) collective-permute-start(bf16[256,512]{1,0:T(8,128)(2,1)} %get-tuple-element.47), channel_id=1, source_target_pairs={{0,48},{8,56},{16,32},{24,40},{32,16},{40,24},{48,0},{56,8},{64,11... | collective-permute-start | bytes 786440 | tf_op jit(solution)/shard_map/ppermute | solution.py:34
  38.2 22.4 %collective-permute-start.2 = (bf16[256,512]{1,0:T(8,128)(2,1)}, bf16[256,512]{1,0:T(8,128)(2,1)S(1)}, u32[]{:S(2)}, u32[]{:S(2)}) collective-permute-start(bf16[256,512]{1,0:T(8,128)(2,1)} %get-tuple-element.47), channel_id=1, source_target_pairs={{0,32},{8,40},{16,48},{24,56},{32,0},{40,8},{48,16},{56,24},{64,96... | collective-permute-start | bytes 786440 | tf_op jit(solution)/shard_map/ppermute | solution.py:34
  40.6 12.8 %collective-permute-start.4 = (bf16[128,512]{1,0:T(8,128)(2,1)}, bf16[128,512]{1,0:T(8,128)(2,1)S(1)}, u32[]{:S(2)}, u32[]{:S(2)}) collective-permute-start(bf16[128,512]{1,0:T(8,128)(2,1)} %get-tuple-element.48), channel_id=1, source_target_pairs={{0,64},{8,72},{16,80},{24,88},{32,96},{40,104},{48,112},{56,120},{... | collective-permute-start | bytes 393224 | tf_op jit(solution)/shard_map/ppermute | solution.py:34
  53.4 18.9 %collective-permute-start.17 = (bf16[256,512]{1,0:T(8,128)(2,1)S(1)}, bf16[256,512]{1,0:T(8,128)(2,1)S(1)}, u32[]{:S(2)}, u32[]{:S(2)}) collective-permute-start(bf16[256,512]{1,0:T(8,128)(2,1)S(1)} %copy-done.23), channel_id=1, source_target_pairs={{0,8},{8,0},{16,24},{24,16},{32,40},{40,32},{48,56},{56,48},{64,72... | collective-permute-start | bytes 786440 | tf_op jit(solution)/shard_map/ppermute | solution.py:34
  71.6 27.0 %collective-permute-start.8 = (bf16[256,1024]{1,0:T(8,128)(2,1)}, bf16[256,1024]{1,0:T(8,128)(2,1)S(1)}, u32[]{:S(2)}, u32[]{:S(2)}) collective-permute-start(bf16[256,1024]{1,0:T(8,128)(2,1)} %get-tuple-element.52.o_ref), channel_id=1, source_target_pairs={{0,8},{8,0},{16,24},{24,16},{32,40},{40,32},{48,56},{56,48},{64,72... | collective-permute-start | bytes 1572872 | tf_op jit(solution)/shard_map/ppermute | solution.py:34
  83.9 10.2 %collective-permute-start.22 = (bf16[128,512]{1,0:T(8,128)(2,1)}, bf16[128,512]{1,0:T(8,128)(2,1)S(1)}, u32[]{:S(2)}, u32[]{:S(2)}) collective-permute-start(bf16[128,512]{1,0:T(8,128)(2,1)} %get-tuple-element.71), channel_id=1, source_target_pairs={{0,64},{8,72},{16,80},{24,88},{32,96},{40,104},{48,112},{56,120},{... | collective-permute-start | bytes 393224 | tf_op jit(solution)/shard_map/ppermute | solution.py:34
  85.9 9.5 %collective-permute-start.23 = (bf16[128,512]{1,0:T(8,128)(2,1)}, bf16[128,512]{1,0:T(8,128)(2,1)S(1)}, u32[]{:S(2)}, u32[]{:S(2)}) collective-permute-start(bf16[128,512]{1,0:T(8,128)(2,1)} %get-tuple-element.72), channel_id=1, source_target_pairs={{0,80},{8,88},{16,64},{24,72},{32,112},{40,120},{48,96},{56,104},{... | collective-permute-start | bytes 393224 | tf_op jit(solution)/shard_map/ppermute | solution.py:34
  88.3 8.4 %collective-permute-start.24 = (bf16[128,512]{1,0:T(8,128)(2,1)}, bf16[128,512]{1,0:T(8,128)(2,1)S(1)}, u32[]{:S(2)}, u32[]{:S(2)}) collective-permute-start(bf16[128,512]{1,0:T(8,128)(2,1)} %get-tuple-element.73), channel_id=1, source_target_pairs={{0,96},{8,104},{16,112},{24,120},{32,64},{40,72},{48,80},{56,88},{... | collective-permute-start | bytes 393224 | tf_op jit(solution)/shard_map/ppermute | solution.py:34
  94.1 37.4 %collective-permute-start.19 = (bf16[512,512]{1,0:T(8,128)(2,1)}, bf16[512,512]{1,0:T(8,128)(2,1)S(1)}, u32[]{:S(2)}, u32[]{:S(2)}) collective-permute-start(bf16[512,512]{1,0:T(8,128)(2,1)} %get-tuple-element.68), channel_id=1, source_target_pairs={{0,16},{8,24},{16,0},{24,8},{32,48},{40,56},{48,32},{56,40},{64,80... | collective-permute-start | bytes 1572872 | tf_op jit(solution)/shard_map/ppermute | solution.py:34
  95.4 24.1 %collective-permute-start.20 = (bf16[256,512]{1,0:T(8,128)(2,1)}, bf16[256,512]{1,0:T(8,128)(2,1)S(1)}, u32[]{:S(2)}, u32[]{:S(2)}) collective-permute-start(bf16[256,512]{1,0:T(8,128)(2,1)} %get-tuple-element.69), channel_id=1, source_target_pairs={{0,32},{8,40},{16,48},{24,56},{32,0},{40,8},{48,16},{56,24},{64,96... | collective-permute-start | bytes 786440 | tf_op jit(solution)/shard_map/ppermute | solution.py:34
  96.8 25.7 %collective-permute-start.21 = (bf16[256,512]{1,0:T(8,128)(2,1)}, bf16[256,512]{1,0:T(8,128)(2,1)S(1)}, u32[]{:S(2)}, u32[]{:S(2)}) collective-permute-start(bf16[256,512]{1,0:T(8,128)(2,1)} %get-tuple-element.70), channel_id=1, source_target_pairs={{0,48},{8,56},{16,32},{24,40},{32,16},{40,24},{48,0},{56,8},{64,11... | collective-permute-start | bytes 786440 | tf_op jit(solution)/shard_map/ppermute | solution.py:34
  98.6 19.4 %collective-permute-start.25 = (bf16[128,512]{1,0:T(8,128)(2,1)}, bf16[128,512]{1,0:T(8,128)(2,1)S(1)}, u32[]{:S(2)}, u32[]{:S(2)}) collective-permute-start(bf16[128,512]{1,0:T(8,128)(2,1)} %get-tuple-element.74), channel_id=1, source_target_pairs={{0,112},{8,120},{16,96},{24,104},{32,80},{40,88},{48,64},{56,72},{... | collective-permute-start | bytes 393224 | tf_op jit(solution)/shard_map/ppermute | solution.py:34
  118.0 29.7 %collective-permute-start.9 = (bf16[256,1024]{1,0:T(8,128)(2,1)}, bf16[256,1024]{1,0:T(8,128)(2,1)S(1)}, u32[]{:S(2)}, u32[]{:S(2)}) collective-permute-start(bf16[256,1024]{1,0:T(8,128)(2,1)} %get-tuple-element.54), channel_id=1, source_target_pairs={{0,2},{1,3},{2,0},{3,1},{4,6},{5,7},{6,4},{7,5},{8,10},{9,11},{10,... | collective-permute-start | bytes 1572872 | tf_op jit(solution)/shard_map/ppermute | solution.py:34
  119.5 28.3 %collective-permute-start.10 = (bf16[256,1024]{1,0:T(8,128)(2,1)}, bf16[256,1024]{1,0:T(8,128)(2,1)S(1)}, u32[]{:S(2)}, u32[]{:S(2)}) collective-permute-start(bf16[256,1024]{1,0:T(8,128)(2,1)} %get-tuple-element.55), channel_id=1, source_target_pairs={{0,4},{1,5},{2,6},{3,7},{4,0},{5,1},{6,2},{7,3},{8,12},{9,13},{10,... | collective-permute-start | bytes 1572872 | tf_op jit(solution)/shard_map/ppermute | solution.py:34
  122.4 30.0 %collective-permute-start.11 = (bf16[256,1024]{1,0:T(8,128)(2,1)}, bf16[256,1024]{1,0:T(8,128)(2,1)S(1)}, u32[]{:S(2)}, u32[]{:S(2)}) collective-permute-start(bf16[256,1024]{1,0:T(8,128)(2,1)} %get-tuple-element.56), channel_id=1, source_target_pairs={{0,6},{1,7},{2,4},{3,5},{4,2},{5,3},{6,0},{7,1},{8,14},{9,15},{10,... | collective-permute-start | bytes 1572872 | tf_op jit(solution)/shard_map/ppermute | solution.py:34
  131.5 16.1 %collective-permute-start.18 = (bf16[512,256]{1,0:T(8,128)(2,1)}, bf16[512,256]{1,0:T(8,128)(2,1)S(1)}, u32[]{:S(2)}, u32[]{:S(2)}) collective-permute-start(bf16[512,256]{1,0:T(8,128)(2,1)} %get-tuple-element.66), channel_id=1, source_target_pairs={{0,8},{8,0},{16,24},{24,16},{32,40},{40,32},{48,56},{56,48},{64,72... | collective-permute-start | bytes 786440 | tf_op jit(solution)/shard_map/ppermute | solution.py:34
  137.2 18.4 %collective-permute-start.26 = (bf16[512,512]{1,0:T(8,128)(2,1)}, bf16[512,512]{1,0:T(8,128)(2,1)S(1)}, u32[]{:S(2)}, u32[]{:S(2)}) collective-permute-start(bf16[512,512]{1,0:T(8,128)(2,1)} %get-tuple-element.76), channel_id=1, source_target_pairs={{0,8},{8,0},{16,24},{24,16},{32,40},{40,32},{48,56},{56,48},{64,72... | collective-permute-start | bytes 1572872 | tf_op jit(solution)/shard_map/ppermute | solution.py:34
  147.6 15.1 %collective-permute-start.28 = (bf16[2,512,256]{2,1,0:T(8,128)(2,1)}, bf16[2,512,256]{2,1,0:T(8,128)(2,1)S(1)}, u32[]{:S(2)}, u32[]{:S(2)}) collective-permute-start(bf16[2,512,256]{2,1,0:T(8,128)(2,1)} %get-tuple-element.82), channel_id=1, source_target_pairs={{0,32},{8,40},{16,48},{24,56},{32,0},{40,8},{48,16},{56,24},{64,96... | collective-permute-start | bytes 1572872 | tf_op jit(solution)/shard_map/ppermute | solution.py:34
  147.7 23.1 %collective-permute-start.29 = (bf16[2,512,256]{2,1,0:T(8,128)(2,1)}, bf16[2,512,256]{2,1,0:T(8,128)(2,1)S(1)}, u32[]{:S(2)}, u32[]{:S(2)}) collective-permute-start(bf16[2,512,256]{2,1,0:T(8,128)(2,1)} %get-tuple-element.83), channel_id=1, source_target_pairs={{0,64},{8,72},{16,80},{24,88},{32,96},{40,104},{48,112},{56,120},{... | collective-permute-start | bytes 1572872 | tf_op jit(solution)/shard_map/ppermute | solution.py:34
  147.8 27.4 %collective-permute-start.30 = (bf16[2,512,256]{2,1,0:T(8,128)(2,1)}, bf16[2,512,256]{2,1,0:T(8,128)(2,1)S(1)}, u32[]{:S(2)}, u32[]{:S(2)}) collective-permute-start(bf16[2,512,256]{2,1,0:T(8,128)(2,1)} %get-tuple-element.84), channel_id=1, source_target_pairs={{0,96},{8,104},{16,112},{24,120},{32,64},{40,72},{48,80},{56,88},{... | collective-permute-start | bytes 1572872 | tf_op jit(solution)/shard_map/ppermute | solution.py:34
  152.4 27.8 %collective-permute-start.13 = (bf16[4,256,512]{2,1,0:T(8,128)(2,1)}, bf16[4,256,512]{2,1,0:T(8,128)(2,1)S(1)}, u32[]{:S(2)}, u32[]{:S(2)}) collective-permute-start(bf16[4,256,512]{2,1,0:T(8,128)(2,1)} %get-tuple-element.58), channel_id=1, source_target_pairs={{0,1},{1,0},{2,3},{3,2},{4,5},{5,4},{6,7},{7,6},{8,9},{9,8},{10,11... | collective-permute-start | bytes 3145736 | tf_op jit(solution)/shard_map/ppermute | solution.py:34
  155.6 30.2 %collective-permute-start.12 = (bf16[256,512]{1,0:T(8,128)(2,1)S(1)}, bf16[256,512]{1,0:T(8,128)(2,1)S(1)}, u32[]{:S(2)}, u32[]{:S(2)}) collective-permute-start(bf16[256,512]{1,0:T(8,128)(2,1)S(1)} %slice.69), channel_id=1, source_target_pairs={{0,1},{1,0},{2,3},{3,2},{4,5},{5,4},{6,7},{7,6},{8,9},{9,8},{10,11... | collective-permute-start | bytes 786440 | tf_op jit(solution)/shard_map/ppermute | solution.py:34
  175.5 12.9 %collective-permute-start.31 = (bf16[512,256]{1,0:T(8,128)(2,1)S(1)}, bf16[512,256]{1,0:T(8,128)(2,1)S(1)}, u32[]{:S(2)}, u32[]{:S(2)}) collective-permute-start(bf16[512,256]{1,0:T(8,128)(2,1)S(1)} %fusion.7), channel_id=1, source_target_pairs={{0,16},{8,24},{16,0},{24,8},{32,48},{40,56},{48,32},{56,40},{64,80... | collective-permute-start | bytes 786440 | tf_op jit(solution)/shard_map/ppermute | solution.py:34
  180.7 8.4 %collective-permute-start.14 = (bf16[256,512]{1,0:T(8,128)(2,1)S(1)}, bf16[256,512]{1,0:T(8,128)(2,1)S(1)}, u32[]{:S(2)}, u32[]{:S(2)}) collective-permute-start(bf16[256,512]{1,0:T(8,128)(2,1)S(1)} %get-tuple-element.87), channel_id=1, source_target_pairs={{0,2},{1,3},{2,0},{3,1},{4,6},{5,7},{6,4},{7,5},{8,10},{9,11},{10,... | collective-permute-start | bytes 786440 | tf_op jit(solution)/shard_map/ppermute | solution.py:34
  181.1 10.1 %collective-permute-start.16 = (bf16[256,512]{1,0:T(8,128)(2,1)S(1)}, bf16[256,512]{1,0:T(8,128)(2,1)S(1)}, u32[]{:S(2)}, u32[]{:S(2)}) collective-permute-start(bf16[256,512]{1,0:T(8,128)(2,1)S(1)} %get-tuple-element.88), channel_id=1, source_target_pairs={{0,6},{1,7},{2,4},{3,5},{4,2},{5,3},{6,0},{7,1},{8,14},{9,15},{10,... | collective-permute-start | bytes 786440 | tf_op jit(solution)/shard_map/ppermute | solution.py:34
  183.9 9.2 %collective-permute-start.15 = (bf16[256,512]{1,0:T(8,128)(2,1)S(1)}, bf16[256,512]{1,0:T(8,128)(2,1)S(1)}, u32[]{:S(2)}, u32[]{:S(2)}) collective-permute-start(bf16[256,512]{1,0:T(8,128)(2,1)S(1)} %get-tuple-element.89), channel_id=1, source_target_pairs={{0,4},{1,5},{2,6},{3,7},{4,0},{5,1},{6,2},{7,3},{8,12},{9,13},{10,... | collective-permute-start | bytes 786440 | tf_op jit(solution)/shard_map/ppermute | solution.py:34
  (24 other events, 334.1 us)
where the time goes:
time: 195 us; the launch traced here: 194 us
  Pallas kernels  75.5 us (39%)
  waiting for transfers between devices  63.7 us (33%)
  starting transfers between devices  43.7 us (22%)
  local copies, waits for them, and re-layouts  6.67 us (3%)
  other arithmetic  3.48 us (2%)
    ppermute x32, waiting for transfers between devices, swap(): return lax.ppermute(value, axis, [(i, i ^ mask) for i in range(size)])  63.7 us
    ppermute x32, starting transfers between devices, swap(): return lax.ppermute(value, axis, [(i, i ^ mask) for i in range(size)])  43.7 us
    pallas_call x1, Pallas kernels, far_grad_call(): pl.pallas_call(far_grad_kernel, grid=(2,), in_specs=[*common_specs(), pl....  10.9 us
    pallas_call x1, Pallas kernels, project_call(): pl.pallas_call(project_kernel, grid_spec=pltpu.PrefetchScalarGridSpec(num...  10.3 us
    pallas_call x1, Pallas kernels, far_call(): pl.pallas_call(far_kernel, grid=(2,), in_specs=[pl.BlockSpec((128, 1024),...  10 us
    pallas_call x1, Pallas kernels, weight_call(): pl.pallas_call(weight_kernel, grid_spec=pltpu.PrefetchScalarGridSpec(num_...  9.12 us
    pallas_call x1, Pallas kernels, near_grad_call(): pl.pallas_call(near_grad_kernel, grid=(2,), in_specs=[*common_specs(), pl...  8.76 us
    pallas_call x1, Pallas kernels, grad_attention_call(): pl.pallas_call(grad_attention_kernel, grid_spec=pltpu.PrefetchScalarGridS...  7.57 us
  transfers between devices with their start and end apart: 32, of which 13 were waited for; matrix products, arithmetic and copies ran while one was open for 1% of the time, Pallas kernels for 39%

commit v1 on v0

v1 whole, which is shorter than its diff:
```python
import functools
import math

import jax
import jax.numpy as jnp
from jax import lax
from jax.experimental import pallas as pl
from jax.experimental.pallas import tpu as pltpu
from jax.sharding import PartitionSpec as P

HD = 128
BF = jnp.bfloat16
F32 = jnp.float32
SCALE = 1.0 / math.sqrt(HD)
LOG2E = math.log2(math.e)
VMEM_LIMIT = 16 * 1024 * 1024


def cost(us):
    return pl.CostEstimate(flops=0, bytes_accessed=int(us * 1.20e+06), transcendentals=0)


def params(**kw):
    return pltpu.CompilerParams(vmem_limit_bytes=VMEM_LIMIT, **kw)


def mm(a, b, dims):
    return lax.dot_general(a, b, (dims, ((), ())), preferred_element_type=F32)


NN = ((1,), (0,))
NT = ((1,), (1,))
TN = ((0,), (0,))


def swap(value, axis, mask):
    size = lax.axis_size(axis)
    return lax.ppermute(value, axis, [(i, i ^ mask) for i in range(size)])


def shape(dims, dtype=BF):
    return jax.ShapeDtypeStruct(dims, dtype)


def grad_attention_kernel(pos, w_ref, g_ref, keep_ref, send_ref, other_ref, acc):
    step = pl.program_id(0)
    core = pos[0]

    @pl.when(step == 0)
    def _():
        acc[...] = jnp.zeros_like(acc)

    acc[...] += mm(w_ref[...], g_ref[...], NT)
    for part in range(2):
        away = pl.multiple_of((1 - core) * 256 + part * 512, 256)
        other_ref[:, part * 256 : (part + 1) * 256] = g_ref[:, pl.ds(away, 256)]

    @pl.when(step == pl.num_programs(0) - 1)
    def _():
        keep_ref[...] = acc[pl.ds(pl.multiple_of(core * 256, 256), 256), :].astype(BF)
        send_ref[...] = acc[pl.ds(pl.multiple_of((1 - core) * 256, 256), 256), :].astype(BF)


def grad_attention_call(pos, out_weight, output_grad):
    width = output_grad.shape[1]
    step = 1024
    return pl.pallas_call(
        grad_attention_kernel,
        grid_spec=pltpu.PrefetchScalarGridSpec(
            num_scalar_prefetch=1,
            grid=(width // step,),
            in_specs=[
                pl.BlockSpec((512, step), lambda i, pos: (0, i)),
                pl.BlockSpec((512, step), lambda i, pos: (0, i)),
            ],
            out_specs=[
                pl.BlockSpec((256, 512), lambda i, pos: (0, 0)),
                pl.BlockSpec((256, 512), lambda i, pos: (0, 0)),
                pl.BlockSpec((512, step // 2), lambda i, pos: (0, i)),
            ],
            scratch_shapes=[pltpu.VMEM((512, 512), F32)],
        ),
        out_shape=[shape((256, 512)), shape((256, 512)), shape((512, width // 2))],
        compiler_params=params(),
        cost_estimate=cost(4.5),
        name="grad_attention",
    )(pos, out_weight, output_grad)


def band(rows, cols, ratio, weight, row_major):
    r = lax.broadcasted_iota(jnp.int32, (rows, cols), 0)
    c = lax.broadcasted_iota(jnp.int32, (rows, cols), 1)
    hit = (c // ratio == r) if row_major else (r // ratio == c)
    return jnp.where(hit, weight, 0.0).astype(BF)


def prepare_kernel(pos, q_ref, k_ref, v_ref, qt_ref, kv_ref, l1_ref):
    fold = band(256, 512, 2, 0.5, True)
    for at, ref in enumerate((k_ref, v_ref)):
        cols = slice(at * 256, (at + 1) * 256)
        kv_ref[:, cols] = ref[...]
        l1_ref[:, cols] = mm(fold, ref[...], NN).astype(BF)
    qt_ref[...] = q_ref[...].T


def pool_kernel(pos, k_ref, v_ref, own_ref, kv_ref, l1_ref):
    fold = band(256, 512, 2, 0.5, True)
    l1_ref[:256, :] = own_ref[...]
    for at, ref in enumerate((k_ref, v_ref)):
        cols = slice(at * 256, (at + 1) * 256)
        kv_ref[:, cols] = ref[...]
        l1_ref[256:, cols] = mm(fold, ref[...], NN).astype(BF)


def whole(*dims):
    return pl.BlockSpec(dims, lambda i, pos: (0,) * len(dims))


def half_cols():
    return pl.BlockSpec((512, 256), lambda i, pos: (0, pos[0]))


def prepare_call(pos, queries, keys, values):
    return pl.pallas_call(
        prepare_kernel,
        grid_spec=pltpu.PrefetchScalarGridSpec(
            num_scalar_prefetch=1,
            grid=(1,),
            in_specs=[half_cols()] * 3,
            out_specs=[whole(256, 512), whole(512, 512), whole(256, 512)],
        ),
        out_shape=[shape((256, 512)), shape((512, 512)), shape((256, 512))],
        compiler_params=params(),
        cost_estimate=cost(1.0),
        name="prepare",
    )(pos, queries, keys, values)


def pool_call(pos, keys, values, l1_own):
    return pl.pallas_call(
        pool_kernel,
        grid_spec=pltpu.PrefetchScalarGridSpec(
            num_scalar_prefetch=1,
            grid=(1,),
            in_specs=[half_cols(), half_cols(), whole(256, 512)],
            out_specs=[whole(512, 512), whole(512, 512)],
        ),
        out_shape=[shape((512, 512)), shape((512, 512))],
        compiler_params=params(),
        cost_estimate=cost(1.0),
        name="pool",
    )(pos, keys, values, l1_own)


def pool_more_kernel(pos, l1_ref, own_ref, q_ref, l2_ref, l3_ref, qt_ref):
    fold = band(256, 512, 2, 0.5, True)
    l2 = mm(fold, l1_ref[...], NN).astype(BF)
    l2_ref[...] = l2
    l3_ref[...] = mm(fold[:128, :256], l2, NN).astype(BF)
    qt_ref[:, :512] = own_ref[...]
    qt_ref[:, 512:] = q_ref[...].T


def pool_more_call(pos, l1, qt_own, queries):
    return pl.pallas_call(
        pool_more_kernel,
        grid_spec=pltpu.PrefetchScalarGridSpec(
            num_scalar_prefetch=1,
            grid=(1,),
            in_specs=[whole(512, 512), whole(256, 512), half_cols()],
            out_specs=[whole(256, 512), whole(128, 512), whole(256, 1024)],
        ),
        out_shape=[shape((256, 512)), shape((128, 512)), shape((256, 1024))],
        compiler_params=params(),
        cost_estimate=cost(1.0),
        name="pool_more",
    )(pos, l1, qt_own, queries)


def score_block(key, value, qt_ref, e_ref, slot, carry):
    new = []
    for c, (m_run, l_run, acc) in enumerate(carry):
        cols = slice(c * QC, (c + 1) * QC)
        s = mm(key, qt_ref[:, cols], NN)
        m = jnp.max(s, axis=0, keepdims=True) * (SCALE * LOG2E)
        e = jnp.exp2(s * (SCALE * LOG2E) - m)
        l = jnp.sum(e, axis=0, keepdims=True)
        e_low = e.astype(BF)
        e_ref[0, slot, :, cols] = e_low
        u = mm(value, e_low, TN)
        if m_run is None:
            new.append((m, l, u, m))
        else:
            top = jnp.maximum(m_run, m)
            f_run, f_new = jnp.exp2(m_run - top), jnp.exp2(m - top)
            new.append((top, l_run * f_run + l * f_new, acc * f_run + u * f_new, m))
    return new


QC = 1024
NQ = 1


def near_kernel(qt_ref, *refs):
    keys, values = refs[:2], refs[2:4]
    e_ref, acc_ref, st_ref = refs[4:]
    carry = [(None, None, None)] * NQ
    for j in range(2):
        got = score_block(keys[j][...], values[j][...], qt_ref, e_ref, j, carry)
        carry = [g[:3] for g in got]
        for c in range(NQ):
            st_ref[0, 2 + j : 3 + j, c * QC : (c + 1) * QC] = got[c][3]
    put_carry(carry, acc_ref, st_ref)


def put_carry(carry, acc_ref, st_ref):
    for c, (m, l, acc) in enumerate(carry):
        cols = slice(c * QC, (c + 1) * QC)
        acc_ref[:, cols] = acc
        st_ref[0, 0:1, cols] = m
        st_ref[0, 1:2, cols] = l


def get_carry(acc_ref, st_ref):
    parts = [slice(c * QC, (c + 1) * QC) for c in range(NQ)]
    return [(st_ref[0, 0:1, p], st_ref[0, 1:2, p], acc_ref[:, p]) for p in parts]


def middle_kernel(qt_ref, *refs):
    keys, values = refs[:2], refs[2:4]
    acc_in, st_in, e_ref, acc_ref, st_ref = refs[4:]
    carry = get_carry(acc_in, st_in)
    st_ref[0, 2:4, :] = st_in[0, 2:4, :]
    for j in range(2):
        got = score_block(keys[j][...], values[j][...], qt_ref, e_ref, j, carry)
        carry = [g[:3] for g in got]
        for c in range(NQ):
            st_ref[0, 4 + j : 5 + j, c * QC : (c + 1) * QC] = got[c][3]
    put_carry(carry, acc_ref, st_ref)


def last_kernel(qt_ref, key, value, acc_in, st_in, e_ref, o_ref, s_ref):
    got = score_block(key[...], value[...], qt_ref, e_ref, 0, get_carry(acc_in, st_in))
    for c, (m, l, acc, top) in enumerate(got):
        cols = slice(c * QC, (c + 1) * QC)
        inv = 1.0 / l
        o_ref[:, cols] = (acc * inv).astype(BF)
        s_ref[0, :4, cols] = jnp.exp2(st_in[0, 2:6, cols] - m) * inv
        s_ref[0, 4:5, cols] = jnp.exp2(top - m) * inv


def per_head(*dims):
    return pl.BlockSpec(dims, lambda h: (h,) + (0,) * (len(dims) - 1))


def kv_specs(count):
    def spec(offset):
        return pl.BlockSpec((512, 128), lambda h: (0, h + offset))

    return [spec(0)] * count + [spec(2)] * count


CARRY_SPECS = [per_head(128, 1024), per_head(1, 8, 1024)]
CARRY = [shape((256, 1024), F32), shape((2, 8, 1024), F32)]


def score_call(kernel, name, us, qt, blocks, carry, last=False):
    n = len(blocks)
    return pl.pallas_call(
        kernel,
        grid=(2,),
        in_specs=[per_head(128, 1024), *kv_specs(n), *CARRY_SPECS[: len(carry)]],
        out_specs=[per_head(1, n, 512, 1024), *CARRY_SPECS],
        out_shape=[
            shape((2, n, 512, 1024)),
            shape((256, 1024)) if last else CARRY[0],
            CARRY[1],
        ],
        compiler_params=params(),
        cost_estimate=cost(us),
        name=name,
    )(qt, *blocks, *blocks, *carry)


def project_kernel(
    pos, o_ref, r_ref, w_mine, w_other, keep, first_1, first_3, late_1, late_3, mine, other
):
    step = pl.program_id(0)

    @pl.when(step == 0)
    def _():
        mine[...] = o_ref[:, :512].T
        other[...] = r_ref[:, 512:].T

    out = (mm(mine[...], w_mine[...], NN) + mm(other[...], w_other[...], NN)).astype(BF)
    top, low = out[:256], out[256:]

    @pl.when(step == 0)
    def _():
        keep[...] = out

    @pl.when(step == 1)
    def _():
        first_1[256:] = top
        late_1[...] = low

    @pl.when(step == 2)
    def _():
        first_1[:256] = top
        first_3[:256] = low

    @pl.when(step == 3)
    def _():
        first_3[256:] = low
        late_3[...] = top


def project_call(pos, attn, attn_other, out_weight, dx):
    def weight(flip):
        return pl.BlockSpec((256, 512), lambda i, pos: (pos[0] ^ flip, pos[1] ^ (i * 2 + dx)))

    return pl.pallas_call(
        project_kernel,
        grid_spec=pltpu.PrefetchScalarGridSpec(
            num_scalar_prefetch=1,
            grid=(4,),
            in_specs=[whole(256, 1024), whole(256, 1024), weight(0), weight(1)],
            out_specs=[whole(512, 512)] * 3 + [whole(256, 512)] * 2,
            scratch_shapes=[pltpu.VMEM((512, 256), BF), pltpu.VMEM((512, 256), BF)],
        ),
        out_shape=[shape((512, 512))] * 3 + [shape((256, 512))] * 2,
        compiler_params=params(),
        cost_estimate=cost(3.0),
        name="project",
    )(pos, attn, attn_other, out_weight, out_weight)


def weight_kernel(
    pos, o_ref, r_ref, g_own, g_recv, keep, first_1, first_3, late_1, late_3
):
    dz, dx = pl.program_id(0) // 2, pl.program_id(0) % 2
    own, far = g_own[...], g_recv[...]
    up = (mm(o_ref[:, :512], own, NN) + mm(o_ref[:, 512:], far, NN)).astype(BF)
    down = (mm(r_ref[:, 512:], own, NN) + mm(r_ref[:, :512], far, NN)).astype(BF)

    @pl.when(dz == 0)
    def _():
        keep[0, dx] = up
        keep[1, dx] = down

    @pl.when(dz == 1)
    def _():
        first_1[1, dx] = up
        late_1[dx] = down

    @pl.when(dz == 2)
    def _():
        first_1[0, dx] = up
        first_3[0, dx] = down

    @pl.when(dz == 3)
    def _():
        first_3[1, dx] = down
        late_3[dx] = up


def weight_call(pos, attn, attn_other, output_grad, grad_recv):
    return pl.pallas_call(
        weight_kernel,
        grid_spec=pltpu.PrefetchScalarGridSpec(
            num_scalar_prefetch=1,
            grid=(8,),
            in_specs=[
                whole(256, 1024),
                whole(256, 1024),
                pl.BlockSpec((512, 256), lambda i, pos: (0, (pos[2] ^ i) * 2 + pos[0])),
                pl.BlockSpec((512, 256), lambda i, pos: (0, pos[2] ^ i)),
            ],
            out_specs=[whole(2, 2, 256, 256)] * 3 + [whole(2, 256, 256)] * 2,
        ),
        out_shape=[shape((2, 2, 256, 256))] * 3 + [shape((2, 256, 256))] * 2,
        compiler_params=params(),
        cost_estimate=cost(5.0),
        name="weight_term",
    )(pos, attn, attn_other, output_grad, grad_recv)


def grad_block(key, value, qt, da, row_dot, s, e_ref, slot, ds_ref, dq_ref, first):
    da_low = (da * s).astype(BF)
    dot_scaled = row_dot * s
    for c in range(NQ):
        cols = slice(c * QC, (c + 1) * QC)
        dp = mm(value, da_low[:, cols], NN)
        ds = (e_ref[0, slot, :, cols].astype(F32) * (dp - dot_scaled[:, cols])).astype(BF)
        ds_ref[:, cols] = ds
        part = mm(key, ds, TN)
        if first:
            dq_ref[:, cols] = part
        else:
            dq_ref[:, cols] += part
    dk = mm(ds_ref[...], qt, NT) * SCALE
    dv = mm(e_ref[0, slot], da_low, NT)
    return dk, dv


def grad_rows(da_own, da_recv, o_ref):
    da = jnp.concatenate([da_own[...], da_recv[...]], axis=1).astype(F32)
    return da, jnp.sum(da * o_ref[...].astype(F32), axis=0, keepdims=True)


def far_grad_kernel(qt_ref, da_own, da_recv, o_ref, s_ref, e_middle, e_last, *refs):
    keys, values = refs[:3], refs[3:6]
    side_ref, z1_ref, z3_ref, z2_ref, dq_ref, ds_ref = refs[6:]
    head = pl.program_id(0)
    da, row_dot = grad_rows(da_own, da_recv, o_ref)
    k_cols = pl.ds(pl.multiple_of(head * 128, 128), 128)
    v_cols = pl.ds(pl.multiple_of(head * 128 + 256, 128), 128)
    qt = qt_ref[...]
    for j in range(3):
        s = s_ref[0, 2 + j : 3 + j, :]
        both = grad_block(
            keys[j][...],
            values[j][...],
            qt,
            da,
            row_dot,
            s,
            e_last if j == 2 else e_middle,
            j % 2,
            ds_ref,
            dq_ref,
            j == 0,
        )
        for cols, grad in zip((k_cols, v_cols), both):
            grad = grad.astype(BF)
            if j == 0:
                side_ref[:, cols] = grad
            else:
                at = j - 1
                z1_ref[at * 256 : at * 256 + 256, cols] = grad[:256]
                z3_ref[at * 128 : at * 128 + 128, cols] = grad[256:384]
                z2_ref[at * 128 : at * 128 + 128, cols] = grad[384:]


def common_specs():
    return [
        pl.BlockSpec((128, 1024), lambda h: (h, 0)),
        pl.BlockSpec((128, 512), lambda h: (h, 0)),
        pl.BlockSpec((128, 512), lambda h: (h, 0)),
        pl.BlockSpec((128, 1024), lambda h: (h, 0)),
        pl.BlockSpec((1, 8, 1024), lambda h: (h, 0, 0)),
    ]


def far_grad_call(qt, da_own, da_recv, attn, scales, e_middle, e_last, far):
    return pl.pallas_call(
        far_grad_kernel,
        grid=(2,),
        in_specs=[
            *common_specs(),
            per_head(1, 2, 512, 1024),
            per_head(1, 1, 512, 1024),
            *kv_specs(3),
        ],
        out_specs=[pl.BlockSpec((rows, 512), lambda h: (0, 0)) for rows in (512, 512, 256, 256)]
        + [pl.BlockSpec((128, 1024), lambda h: (h, 0))],
        out_shape=[shape((rows, 512)) for rows in (512, 512, 256, 256)] + [shape((256, 1024), F32)],
        scratch_shapes=[pltpu.VMEM((512, 1024), BF)],
        compiler_params=params(),
        cost_estimate=cost(6.7),
        name="far_grads",
    )(qt, da_own, da_recv, attn, scales, e_middle, e_last, *far, *far)


def near_grad_kernel(
    qt_ref,
    da_own,
    da_recv,
    o_ref,
    s_ref,
    e_ref,
    k_own,
    k_sib,
    v_own,
    v_sib,
    dq_in,
    kv_ref,
    q_own,
    q_send,
    ds_ref,
    dq_ref,
):
    keys, values = (k_own, k_sib), (v_own, v_sib)
    head = pl.program_id(0)
    da, row_dot = grad_rows(da_own, da_recv, o_ref)
    k_cols = pl.ds(pl.multiple_of(head * 128, 128), 128)
    v_cols = pl.ds(pl.multiple_of(head * 128 + 256, 128), 128)
    qt = qt_ref[...]
    dq_ref[...] = dq_in[...]
    for j in range(2):
        rows = slice(j * 512, (j + 1) * 512)
        s = s_ref[0, j : j + 1, :]
        dk, dv = grad_block(
            keys[j][...], values[j][...], qt, da, row_dot, s, e_ref, j, ds_ref, dq_ref, False
        )
        kv_ref[rows, k_cols] = dk
        kv_ref[rows, v_cols] = dv
    q_own[...] = (dq_ref[:, :512] * SCALE).T.astype(BF)
    q_send[...] = (dq_ref[:, 512:] * SCALE).T.astype(BF)


def near_grad_call(qt, da_own, da_recv, attn, scales, e_near, own, sib, dq):
    return pl.pallas_call(
        near_grad_kernel,
        grid=(2,),
        in_specs=[
            *common_specs(),
            pl.BlockSpec((1, 2, 512, 1024), lambda h: (h, 0, 0, 0)),
            *kv_specs(2),
            pl.BlockSpec((128, 1024), lambda h: (h, 0)),
        ],
        out_specs=[
            pl.BlockSpec((1024, 512), lambda h: (0, 0)),
            pl.BlockSpec((512, 128), lambda h: (0, h)),
            pl.BlockSpec((512, 128), lambda h: (0, h)),
        ],
        out_shape=[shape((1024, 512), F32), shape((512, 256)), shape((512, 256))],
        scratch_shapes=[pltpu.VMEM((512, 1024), BF), pltpu.VMEM((128, 1024), F32)],
        compiler_params=params(),
        cost_estimate=cost(4.8),
        name="near_grads",
    )(qt, da_own, da_recv, attn, scales, e_near, own, sib, own, sib, dq)


def spread(rows, level, refs, part):
    n = rows >> level
    wide = band(rows, n, 1 << level, 0.5**level, False)
    return [mm(wide, ref[part * n : (part + 1) * n, :], NN) for ref in refs]


def relay_kernel(side_ref, z1_ref, z3_ref, z2_ref, out_ref):
    parts = spread(512, 1, [z1_ref], 1) + spread(512, 2, [z3_ref, z2_ref], 1)
    out_ref[...] = functools.reduce(jnp.add, parts, side_ref[...].astype(F32)).astype(BF)


def relay_call(side, *along):
    return pl.pallas_call(
        relay_kernel,
        out_shape=shape((512, 512)),
        compiler_params=params(),
        cost_estimate=cost(0.6),
        name="relay",
    )(side, *along)


def collect_kernel(kv_ref, q_ref, side_ref, z1_ref, z3_ref, z2_ref, own_ref, send_ref):
    send_ref[:, 512:] = q_ref[...]
    for part, out in ((1, send_ref), (0, own_ref)):
        total = kv_ref[part * 512 : (part + 1) * 512, :]
        parts = spread(512, 1, [side_ref], part)
        parts += spread(512, 2, [z1_ref.at[:256]], part)
        parts += spread(512, 3, [z3_ref.at[:128], z2_ref.at[:128]], part)
        out[:, :512] = functools.reduce(jnp.add, parts, total).astype(BF)


def collect_call(kv_grad, q_send, side, *along):
    return pl.pallas_call(
        collect_kernel,
        out_shape=[shape((512, 512)), shape((512, 768))],
        compiler_params=params(),
        cost_estimate=cost(1.3),
        name="collect",
    )(kv_grad, q_send, side, *along)


def place_kernel(pos, q_own, kv_own, recv, q_out, k_out, v_out):
    mine = pl.ds(pl.multiple_of(pos[0] * 256, 256), 256)
    other = pl.ds(pl.multiple_of((1 - pos[0]) * 256, 256), 256)
    q_out[:, mine] = q_own[...]
    q_out[:, other] = recv[:, 512:]
    k_out[:, mine] = kv_own[:, :256]
    k_out[:, other] = recv[:, :256]
    v_out[:, mine] = kv_own[:, 256:]
    v_out[:, other] = recv[:, 256:512]


def place_call(pos, q_own, kv_own, recv):
    return pl.pallas_call(
        place_kernel,
        grid_spec=pltpu.PrefetchScalarGridSpec(
            num_scalar_prefetch=1,
            grid=(1,),
            in_specs=[whole(512, 256), whole(512, 512), whole(512, 768)],
            out_specs=[whole(512, 512)] * 3,
        ),
        out_shape=[shape((512, 512))] * 3,
        compiler_params=params(),
        cost_estimate=cost(1.0),
        name="place",
    )(pos, q_own, kv_own, recv)


def total(*terms):
    return functools.reduce(jnp.add, [t.astype(F32) for t in terms])


def cross_kernel(keep, c1, c3, o1, o3, out_ref):
    out_ref[:256, :] = total(keep[:256, :], c1[256:, :], o3[:256, :]).astype(BF)
    out_ref[256:, :] = total(keep[256:, :], c3[256:, :], o1[:256, :]).astype(BF)


def output_kernel(keep, o1, o3, end_1, end_3, cross, out_ref):
    out_ref[:256, :] = total(keep[:256, :], o1[512:, :], end_3[...], cross[:256, :]).astype(BF)
    out_ref[256:, :] = total(keep[256:, :], o3[512:, :], end_1[...], cross[256:, :]).astype(BF)


def weight_sum_kernel(keep, w1, w3, end_1, end_3, own_ref, send_ref):
    up = total(keep[0], w1[1], end_3[...])
    down = total(keep[1], w3[1], end_1[...])
    own_ref[0] = up[0]
    own_ref[1] = down[0]
    send_ref[0] = up[1].astype(BF)
    send_ref[1] = down[1].astype(BF)


def weight_out_kernel(pos, own, back, out_ref):
    for part in range(2):
        row = pos[0] * 256 if part == 0 else (1 - pos[0]) * 256
        rows = pl.ds(pl.multiple_of(row, 256), 256)
        out_ref[rows, :] = total(own[part], back[part]).astype(BF)


def plain_call(kernel, out_shape, us, name, *args):
    return pl.pallas_call(
        kernel,
        out_shape=out_shape,
        compiler_params=params(),
        cost_estimate=cost(us),
        name=name,
    )(*args)


def weight_out_call(pos, own, back):
    return pl.pallas_call(
        weight_out_kernel,
        grid_spec=pltpu.PrefetchScalarGridSpec(
            num_scalar_prefetch=1,
            grid=(1,),
            in_specs=[whole(2, 256, 256)] * 2,
            out_specs=whole(512, 256),
        ),
        out_shape=shape((512, 256)),
        compiler_params=params(),
        cost_estimate=cost(1.0),
        name="weight_out",
    )(pos, own, back)


def add(*terms):
    return functools.reduce(jnp.add, [t.astype(F32) for t in terms])


def after(values, *done):
    return lax.optimization_barrier((values, done))[0]


def low(*terms):
    return add(*terms).astype(BF)


def shards(queries, key_rows, value_rows, out_weight, output_grad):
    ctx = lax.axis_index("ctx")
    core = ctx % 2
    pos = jnp.stack([core, lax.axis_index("head"), ctx // 2]).astype(jnp.int32)

    k_recv, v_recv, q_recv = [swap(a, "ctx", 1) for a in (key_rows, value_rows, queries)]
    qt_own, kv_own, l1_own = prepare_call(pos, queries, key_rows, value_rows)
    k_recv, v_recv = after((k_recv, v_recv), q_recv)
    kv_sib, l1 = pool_call(pos, k_recv, v_recv, l1_own)
    side = swap(l1, "ctx", 2)
    l2, l3, qt = pool_more_call(pos, l1, qt_own, q_recv)
    along = [swap(a, "ctx", mask) for a, mask in ((l2, 4), (l3, 12), (l3, 8))]
    e_near, *carry = score_call(near_kernel, "near_scores", 4.2, qt, (kv_own, kv_sib), ())
    level = after(jnp.concatenate(along, axis=0), e_near, side)
    cross_level = swap(level, "ctx", 2)
    e_middle, *carry = score_call(
        middle_kernel, "middle_scores", 4.2, qt, (side, level), carry
    )
    da_own, da_send, grad_send = grad_attention_call(
        pos, *after((out_weight, output_grad), level)
    )
    cross_level = after(cross_level, da_own, e_middle)
    da_recv, grad_recv = [swap(a, "ctx", 1) for a in after((da_send, grad_send), cross_level)]
    e_last, attn, scales = score_call(
        last_kernel, "last_scores", 2.2, qt, (cross_level,), carry, True
    )
    far = (side, level, cross_level)

    attn_other = after(swap(attn, "ctx", 1), da_recv, grad_recv)
    keep_c, first_c1, first_c3, late_c1, late_c3 = project_call(
        pos, attn, attn_other, out_weight, 1
    )
    got_c1, got_c3 = swap(first_c1, "head", 2), swap(first_c3, "head", 6)

    attn_g, qt_g = after((attn, qt), keep_c)
    side_grad, *level_grads, dq = far_grad_call(
        qt_g, da_own, da_recv, attn_g, scales, e_middle, e_last, far
    )
    back = [swap(g, "ctx", mask) for g, mask in zip(level_grads, (4, 12, 8))]

    attn_p, other_p = after((attn, attn_other), side_grad)
    keep_o, first_o1, first_o3, late_o1, late_o3 = project_call(
        pos, attn_p, other_p, out_weight, 0
    )
    attn_w, other_w = after((attn, attn_other), keep_o)
    keep_w, first_w1, first_w3, late_w1, late_w3 = weight_call(
        pos, attn_w, other_w, output_grad, grad_recv
    )
    qt_n, da_n = after((qt, da_own), keep_w)
    kv_grad, q_own, q_send = near_grad_call(qt_n, da_n, da_recv, attn, scales, e_near, kv_own, kv_sib, dq)

    send_1 = jnp.concatenate([low(late_c1, got_c3[:256]), first_o1], axis=0)
    send_3 = jnp.concatenate([low(late_c3, got_c1[:256]), first_o3], axis=0)
    send_1, send_3 = after((send_1, send_3))
    got_o1, got_o3 = swap(send_1, "head", 2), swap(send_3, "head", 6)

    relayed = relay_call(after(side_grad, send_1, send_3, kv_grad), *back)
    side_back = swap(relayed, "ctx", 2)
    first_w1, first_w3 = after((first_w1, first_w3), back[1:])
    got_w1, got_w3 = swap(first_w1, "ctx", 4), swap(first_w3, "ctx", 12)

    cross = plain_call(
        cross_kernel, shape((512, 512)), 1.0, "cross", keep_c, got_c1, got_c3, got_o1, got_o3
    )
    got_w1, got_w3 = after((got_w1, got_w3), relayed)
    cross_back = swap(cross, "head", 1)
    end_1 = swap(low(late_o1, got_o3[256:512]), "head", 2)
    end_3 = swap(low(late_o3, got_o1[256:512]), "head", 6)
    layer_output = plain_call(
        output_kernel, shape((512, 512)), 1.0, "output", keep_o, got_o1, got_o3, end_1, end_3, cross_back
    )

    end_w1 = swap(low(late_w1, got_w3[0]), "ctx", 4)
    end_w3 = swap(low(late_w3, got_w1[0]), "ctx", 12)
    w_own, w_send = plain_call(
        weight_sum_kernel,
        [shape((2, 256, 256), F32), shape((2, 256, 256))],
        1.0,
        "weight_sum",
        *(after(keep_w, cross), got_w1, got_w3, end_w1, end_w3),
    )
    weight_grad = weight_out_call(pos, w_own, swap(w_send, "ctx", 2))

    kv_done, send = collect_call(after(kv_grad, got_w1), q_send, side_back, *back)
    query_grad, key_grad, value_grad = place_call(pos, q_own, kv_done, swap(send, "ctx", 1))
    return (layer_output, query_grad, key_grad, value_grad, weight_grad)


def solution(mesh):
    placed = (P("ctx", "head"), P("ctx", "head"), P("ctx", "head"), P("head", None), P("ctx", None))
    return jax.shard_map(
        shards,
        mesh=mesh,
        in_specs=placed,
        out_specs=(
            P("ctx", "head"),
            P("ctx", "head"),
            P("ctx", "head"),
            P("ctx", "head"),
            P("head", "ctx"),
        ),
        check_vma=False,
    )
```

time: 195 us -> 117 us (0.60)
  waiting for transfers between devices: 63.7 us -> 33.4 us
  Pallas kernels: 75.5 us -> 47 us
  starting transfers between devices: 43.7 us -> 30 us
  other arithmetic: 3.48 us -> 0.61 us
    ppermute x32 -> x28, waiting for transfers between devices: 63.7 us -> 33.4 us  [swap(): return lax.ppermute(value, axis, [(i, i ^ mask) for i in range(size)])]
    ppermute x32 -> x28, starting transfers between devices: 43.7 us -> 30 us  [swap(): return lax.ppermute(value, axis, [(i, i ^ mask) for i in range(size)])]
    pallas_call x4 -> x12, Pallas kernels: 32.9 us -> 24 us  [the longest x3 11 us: score_call(): pl.pallas_call(kernel, grid=(2,), in_specs=[per_head(128, 1024), *kv_spec...]
    pallas_call x1 -> x2, Pallas kernels: 10.3 us -> 5.98 us  [project_call(): pl.pallas_call(project_kernel, grid_spec=pltpu.PrefetchScalarGridSpec(num...]
    pallas_call x1, Pallas kernels: 9.12 us -> 5.1 us  [weight_call(): pl.pallas_call(weight_kernel, grid_spec=pltpu.PrefetchScalarGridSpec(num_...]
    pallas_call x1, Pallas kernels: 8.76 us -> 4.76 us  [near_grad_call(): pl.pallas_call(near_grad_kernel, grid=(2,), in_specs=[*common_specs(), pl...]
    pallas_call x1, Pallas kernels: 7.57 us -> 4.53 us  [grad_attention_call(): pl.pallas_call(grad_attention_kernel, grid_spec=pltpu.PrefetchScalarGridS...]
    pallas_call x1, Pallas kernels: 3.65 us -> 0.87 us  [pool_call(): pl.pallas_call(pool_kernel, grid_spec=pltpu.PrefetchScalarGridSpec(num_sc...]
  transfers between devices with their start and end apart: 32 -> 28, of which waited for: 13 -> 10; matrix products, arithmetic and copies ran while one was open for 1% -> 1% of each run, Pallas kernels for 39% -> 36%
where the time goes in v1:
time: 117 us
  Pallas kernels  47 us (40%)
  waiting for transfers between devices  33.4 us (29%)
  starting transfers between devices  30 us (26%)
  local copies, waits for them, and re-layouts  5.32 us (5%)
    ppermute x28, waiting for transfers between devices, swap(): return lax.ppermute(value, axis, [(i, i ^ mask) for i in range(size)])  33.4 us
    ppermute x28, starting transfers between devices, swap(): return lax.ppermute(value, axis, [(i, i ^ mask) for i in range(size)])  30 us
    pallas_call x3, Pallas kernels, score_call(): pl.pallas_call(kernel, grid=(2,), in_specs=[per_head(128, 1024), *kv_spec...  11 us
    pallas_call x1, Pallas kernels, far_grad_call(): pl.pallas_call(far_grad_kernel, grid=(2,), in_specs=[*common_specs(), per...  6.6 us
    pallas_call x2, Pallas kernels, project_call(): pl.pallas_call(project_kernel, grid_spec=pltpu.PrefetchScalarGridSpec(num...  5.98 us
    unnamed x12, local copies, waits for them, and re-layouts  5.32 us
    pallas_call x1, Pallas kernels, weight_call(): pl.pallas_call(weight_kernel, grid_spec=pltpu.PrefetchScalarGridSpec(num_...  5.1 us
    pallas_call x1, Pallas kernels, near_grad_call(): pl.pallas_call(near_grad_kernel, grid=(2,), in_specs=[*common_specs(), pl...  4.76 us
  transfers between devices with their start and end apart: 28, of which 10 were waited for; matrix products, arithmetic and copies ran while one was open for 1% of the time, Pallas kernels for 36%

profile of v1, /device:TPU:0, one launch (start us, length us, event | category | flops | bytes accessed | tf_op | source)
XLA Modules:
  0.0 117.2 jit_solution(11783739543614137407)
XLA Ops:
  6.3 1.6 %collective-permute-start.6 = (bf16[512,512]{1,0:T(8,128)(2,1)S(1)}, bf16[512,512]{1,0:T(8,128)(2,1)S(1)}, u32[]{:S(2)}, u32[]{:S(2)}) collective-permute-start(bf16[512,512]{1,0:T(8,128)(2,1)S(1)} %get-tuple-element.84.l1_ref), channel_id=1, source_target_pairs={{0,16},{8,24},{16,0},{24,8},{32,48},{40,56},{48,32},{56,40},{64,80... | collective-permute-start | bytes 1572872 | tf_op jit(solution)/shard_map/ppermute | solution.py:38
  8.9 2.0 %collective-permute-start.3 = (bf16[256,512]{1,0:T(8,128)(2,1)S(1)}, bf16[256,512]{1,0:T(8,128)(2,1)S(1)}, u32[]{:S(2)}, u32[]{:S(2)}) collective-permute-start(bf16[256,512]{1,0:T(8,128)(2,1)S(1)} %get-tuple-element.87), channel_id=1, source_target_pairs={{0,32},{8,40},{16,48},{24,56},{32,0},{40,8},{48,16},{56,24},{64,96... | collective-permute-start | bytes 786440 | tf_op jit(solution)/shard_map/ppermute | solution.py:38
  11.0 3.6 %collective-permute-start.5 = (bf16[128,512]{1,0:T(8,128)(2,1)S(1)}, bf16[128,512]{1,0:T(8,128)(2,1)S(1)}, u32[]{:S(2)}, u32[]{:S(2)}) collective-permute-start(bf16[128,512]{1,0:T(8,128)(2,1)S(1)} %get-tuple-element.88), channel_id=1, source_target_pairs={{0,64},{8,72},{16,80},{24,88},{32,96},{40,104},{48,112},{56,120},{... | collective-permute-start | bytes 393224 | tf_op jit(solution)/shard_map/ppermute | solution.py:38
  14.5 4.2 %near_scores.1 = (bf16[2,2,512,1024]{3,2,1,0:T(8,128)(2,1)S(1)}, f32[256,1024]{1,0:T(8,128)S(1)}, f32[2,8,1024]{2,1,0:T(8,128)S(1)}) custom-call(bf16[256,1024]{1,0:T(8,128)(2,1)S(1)} %get-tuple-element.130.qt_ref, bf16[512,512]{1,0:T(8,128)(2,1)S(1)} %get-tuple-element.89.refs_0_.refs_2_.k_own.v_own, ...), custom_call_target="tpu_custom_call" | custom-call | bytes 5040000 | tf_op jit(solution)/shard_map/near_scores/pallas_call | solution.py:269
  18.8 4.9 %collective-permute-done.5 = bf16[128,512]{1,0:T(8,128)(2,1)S(1)} collective-permute-done((bf16[128,512]{1,0:T(8,128)(2,1)S(1)}, bf16[128,512]{1,0:T(8,128)(2,1)S(1)}, u32[]{:S(2)}, u32[]{:S(2)}) %collective-permute-start.5) | collective-permute-done | bytes 131104 | tf_op jit(solution)/shard_map/ppermute | solution.py:38
  24.3 2.2 %copy-done.1 = bf16[512,4096]{1,0:T(8,128)(2,1)S(1)} copy-done((bf16[512,4096]{1,0:T(8,128)(2,1)S(1)}, bf16[512,4096]{1,0:T(8,128)(2,1)}, u32[]{:S(2)}) %copy-start.1) | copy-done | bytes 4194328
  26.5 4.5 %grad_attention.1 = (bf16[256,512]{1,0:T(8,128)(2,1)S(1)}, bf16[256,512]{1,0:T(8,128)(2,1)S(1)}, bf16[512,2048]{1,0:T(8,128)(2,1)S(1)}) custom-call(s32[3]{0:T(128)S(1)} %pad_add_fusion.pos, bf16[512,4096]{1,0:T(8,128)(2,1)S(1)} %copy-done, bf16[512,4096]{1,0:T(8,128)(2,1)S(1)} %copy-done.1), custom_call_target="tpu_custom_call" | custom-call | bytes 5400000 | tf_op jit(solution)/shard_map/grad_attention/pallas_call | solution.py:67
  31.1 4.4 %middle_scores.1 = (bf16[2,2,512,1024]{3,2,1,0:T(8,128)(2,1)S(1)}, f32[256,1024]{1,0:T(8,128)S(1)}, f32[2,8,1024]{2,1,0:T(8,128)S(1)}) custom-call(bf16[256,1024]{1,0:T(8,128)(2,1)S(1)} %get-tuple-element.130.qt_ref, bf16[512,512]{1,0:T(8,128)(2,1)S(1)} %collective-permute-done.6.refs_0_.refs_2_.refs_3_, ...), custom_call_target="tpu_custom_call" | custom-call | bytes 5040000 | tf_op jit(solution)/shard_map/middle_scores/pallas_call | solution.py:269
  35.5 1.5 %collective-permute-done.7.key.value.refs_2_.refs_5_ = bf16[512,512]{1,0:T(8,128)(2,1)S(1)} collective-permute-done((bf16[512,512]{1,0:T(8,128)(2,1)S(1)}, bf16[512,512]{1,0:T(8,128)(2,1)S(1)}, u32[]{:S(2)}, u32[]{:S(2)}) %collective-permute-start.7) | collective-permute-done | bytes 524320 | tf_op jit(solution)/shard_map/ppermute | solution.py:38
  37.0 2.4 %last_scores.1 = (bf16[2,1,512,1024]{3,2,1,0:T(8,128)(2,1)S(1)}, bf16[256,1024]{1,0:T(8,128)(2,1)S(1)}, f32[2,8,1024]{2,1,0:T(8,128)S(1)}) custom-call(bf16[256,1024]{1,0:T(8,128)(2,1)S(1)} %get-tuple-element.130.qt_ref, bf16[512,512]{1,0:T(8,128)(2,1)S(1)} %collective-permute-done.7.key.value.refs_2_.refs_5_, ...), custom_call_target="tpu_custom_call" | custom-call | bytes 2640000 | tf_op jit(solution)/shard_map/last_scores/pallas_call | solution.py:269
  40.0 2.2 %collective-permute-done.9.da_recv = bf16[256,512]{1,0:T(8,128)(2,1)S(1)} collective-permute-done((bf16[256,512]{1,0:T(8,128)(2,1)S(1)}, bf16[256,512]{1,0:T(8,128)(2,1)S(1)}, u32[]{:S(2)}, u32[]{:S(2)}) %collective-permute-start.9) | collective-permute-done | bytes 262176 | tf_op jit(solution)/shard_map/ppermute | solution.py:38
  42.3 3.0 %project.2 = (bf16[512,512]{1,0:T(8,128)(2,1)S(1)}, bf16[512,512]{1,0:T(8,128)(2,1)S(1)}, bf16[512,512]{1,0:T(8,128)(2,1)S(1)}, bf16[256,512]{1,0:T(8,128)(2,1)S(1)}, bf16[256,512]{1,0:T(8,128)(2,1)S(1)}) custom-call(s32[3]{0:T(128)S(1)} %pad_add_fusion.pos, bf16[256,1024]{1,0:T(8,128)(2,1)S(1)} %get-tuple-element.127.o_ref, ...), custom_call_target="tpu_custom_call" | custom-call | bytes 3600000 | tf_op jit(solution)/shard_map/project/pallas_call | solution.py:322
  45.3 3.1 %collective-permute-start.11 = (bf16[512,512]{1,0:T(8,128)(2,1)S(1)}, bf16[512,512]{1,0:T(8,128)(2,1)S(1)}, u32[]{:S(2)}, u32[]{:S(2)}) collective-permute-start(bf16[512,512]{1,0:T(8,128)(2,1)S(1)} %get-tuple-element.118), channel_id=1, source_target_pairs={{0,6},{1,7},{2,4},{3,5},{4,2},{5,3},{6,0},{7,1},{8,14},{9,15},{10,... | collective-permute-start | bytes 1572872 | tf_op jit(solution)/shard_map/ppermute | solution.py:38
  48.5 6.6 %far_grads.1 = (bf16[512,512]{1,0:T(8,128)(2,1)S(1)}, bf16[512,512]{1,0:T(8,128)(2,1)S(1)}, bf16[256,512]{1,0:T(8,128)(2,1)S(1)}, bf16[256,512]{1,0:T(8,128)(2,1)S(1)}, f32[256,1024]{1,0:T(8,128)S(1)}) custom-call(bf16[256,1024]{1,0:T(8,128)(2,1)S(1)} %get-tuple-element.130.qt_ref, bf16[256,512]{1,0:T(8,128)(2,1)S(1)} %get-tuple-element.131.da_own, ...), custom_call_target="tpu_custom_call" | custom-call | bytes 8040000 | tf_op jit(solution)/shard_map/far_grads/pallas_call | solution.py:456
  55.1 1.3 %collective-permute-start.18 = (bf16[256,512]{1,0:T(8,128)(2,1)S(1)}, bf16[256,512]{1,0:T(8,128)(2,1)S(1)}, u32[]{:S(2)}, u32[]{:S(2)}) collective-permute-start(bf16[256,512]{1,0:T(8,128)(2,1)S(1)} %get-tuple-element.137), channel_id=1, source_target_pairs={{0,96},{8,104},{16,112},{24,120},{32,64},{40,72},{48,80},{56,88},{... | collective-permute-start | bytes 786440 | tf_op jit(solution)/shard_map/ppermute | solution.py:38
  57.1 2.2 %collective-permute-start.22 = (bf16[512,512]{1,0:T(8,128)(2,1)S(1)}, bf16[512,512]{1,0:T(8,128)(2,1)S(1)}, u32[]{:S(2)}, u32[]{:S(2)}) collective-permute-start(bf16[512,512]{1,0:T(8,128)(2,1)S(1)} %get-tuple-element.142), channel_id=1, source_target_pairs={{0,32},{8,40},{16,48},{24,56},{32,0},{40,8},{48,16},{56,24},{64,96... | collective-permute-start | bytes 1572872 | tf_op jit(solution)/shard_map/ppermute | solution.py:38
  59.3 3.0 %project.3 = (bf16[512,512]{1,0:T(8,128)(2,1)S(1)}, bf16[512,512]{1,0:T(8,128)(2,1)S(1)}, bf16[512,512]{1,0:T(8,128)(2,1)S(1)}, bf16[256,512]{1,0:T(8,128)(2,1)S(1)}, bf16[256,512]{1,0:T(8,128)(2,1)S(1)}) custom-call(s32[3]{0:T(128)S(1)} %pad_add_fusion.pos, bf16[256,1024]{1,0:T(8,128)(2,1)S(1)} %get-tuple-element.127.o_ref, ...), custom_call_target="tpu_custom_call" | custom-call | bytes 3600000 | tf_op jit(solution)/shard_map/project/pallas_call | solution.py:322
  62.3 5.1 %weight_term.1 = (bf16[2,2,256,256]{3,2,1,0:T(8,128)(2,1)S(1)}, bf16[2,2,256,256]{3,2,1,0:T(8,128)(2,1)S(1)}, bf16[2,2,256,256]{3,2,1,0:T(8,128)(2,1)S(1)}, bf16...) custom-call(s32[3]{0:T(128)S(1)} %pad_add_fusion.pos, bf16[256,1024]{1,0:T(8,128)(2,1)S(1)} %get-tuple-element.127.o_ref, ...), custom_call_target="tpu_custom_call" | custom-call | bytes 6000000 | tf_op jit(solution)/shard_map/weight_term/pallas_call | solution.py:368
  67.4 4.8 %near_grads.1 = (f32[1024,512]{1,0:T(8,128)S(1)}, bf16[512,256]{1,0:T(8,128)(2,1)S(1)}, bf16[512,256]{1,0:T(8,128)(2,1)S(1)}) custom-call(bf16[256,1024]{1,0:T(8,128)(2,1)S(1)} %get-tuple-element.130.qt_ref, bf16[256,512]{1,0:T(8,128)(2,1)S(1)} %get-tuple-element.131.da_own, bf16[256,512]{1,0:T(8,128)(2,1)S(1)} %collective-permute-done.9.da_recv, ...), custom_call_target="tpu_custom_call" | custom-call | bytes 5760000 | tf_op jit(solution)/shard_map/near_grads/pallas_call | solution.py:513
  72.3 1.7 %collective-permute-start.21 = (bf16[2,2,256,256]{3,2,1,0:T(8,128)(2,1)S(1)}, bf16[2,2,256,256]{3,2,1,0:T(8,128)(2,1)S(1)}, u32[]{:S(2)}, u32[]{:S(2)}) collective-permute-start(bf16[2,2,256,256]{3,2,1,0:T(8,128)(2,1)S(1)} %get-tuple-element.140), channel_id=1, source_target_pairs={{0,96},{8,104},{16,112},{24,120},{32,64},{40,72},{48,80},{56,88},{... | collective-permute-start | bytes 1572872 | tf_op jit(solution)/shard_map/ppermute | solution.py:38
  74.2 2.0 %collective-permute-start.13 = (bf16[768,512]{1,0:T(8,128)(2,1)S(1)}, bf16[768,512]{1,0:T(8,128)(2,1)S(1)}, u32[]{:S(2)}, u32[]{:S(2)}) collective-permute-start(bf16[768,512]{1,0:T(8,128)(2,1)S(1)} %pad_maximum_fusion), channel_id=1, source_target_pairs={{0,2},{1,3},{2,0},{3,1},{4,6},{5,7},{6,4},{7,5},{8,10},{9,11},{10,... | collective-permute-start | bytes 2359304 | tf_op jit(solution)/shard_map/ppermute | solution.py:38
  76.4 1.3 %collective-permute-done.22.z1_ref = bf16[512,512]{1,0:T(8,128)(2,1)S(1)} collective-permute-done((bf16[512,512]{1,0:T(8,128)(2,1)S(1)}, bf16[512,512]{1,0:T(8,128)(2,1)S(1)}, u32[]{:S(2)}, u32[]{:S(2)}) %collective-permute-start.22) | collective-permute-done | bytes 524320 | tf_op jit(solution)/shard_map/ppermute | solution.py:38
  78.9 8.5 %collective-permute-done.20.w1 = bf16[2,2,256,256]{3,2,1,0:T(8,128)(2,1)S(1)} collective-permute-done((bf16[2,2,256,256]{3,2,1,0:T(8,128)(2,1)S(1)}, bf16[2,2,256,256]{3,2,1,0:T(8,128)(2,1)S(1)}, u32[]{:S(2)}, u32[]{:S(2)}) %collective-permute-start.20) | collective-permute-done | bytes 524320 | tf_op jit(solution)/shard_map/ppermute | solution.py:38
  87.5 1.3 %collective-permute-start.26 = (bf16[2,256,256]{2,1,0:T(8,128)(2,1)S(1)}, bf16[2,256,256]{2,1,0:T(8,128)(2,1)S(1)}, u32[]{:S(2)}, u32[]{:S(2)}) collective-permute-start(bf16[2,256,256]{2,1,0:T(8,128)(2,1)S(1)} %fusion), channel_id=1, source_target_pairs={{0,96},{8,104},{16,112},{24,120},{32,64},{40,72},{48,80},{56,88},{... | collective-permute-start | bytes 786440 | tf_op jit(solution)/shard_map/ppermute | solution.py:38
  89.2 1.2 %collect.1 = (bf16[512,512]{1,0:T(8,128)(2,1)S(1)}, bf16[512,768]{1,0:T(8,128)(2,1)S(1)}) custom-call(f32[1024,512]{1,0:T(8,128)S(1)} %get-tuple-element.144.kv_ref, bf16[512,256]{1,0:T(8,128)(2,1)S(1)} %get-tuple-element.145.q_ref, bf16[512,512]{1,0:T(8,128)(2,1)S(1)} %collective-permute-done.23.side_ref, ...), custom_call_target="tpu_custom_call" | custom-call | bytes 1560000 | tf_op jit(solution)/shard_map/collect/pallas_call | solution.py:567
  92.1 2.7 %collective-permute-done.14.o3 = bf16[768,512]{1,0:T(8,128)(2,1)S(1)} collective-permute-done((bf16[768,512]{1,0:T(8,128)(2,1)S(1)}, bf16[768,512]{1,0:T(8,128)(2,1)S(1)}, u32[]{:S(2)}, u32[]{:S(2)}) %collective-permute-start.14) | collective-permute-done | bytes 786464 | tf_op jit(solution)/shard_map/ppermute | solution.py:38
  94.9 3.1 %collective-permute-start.17 = (bf16[512,512]{1,0:T(8,128)(2,1)S(1)}, bf16[512,512]{1,0:T(8,128)(2,1)S(1)}, u32[]{:S(2)}, u32[]{:S(2)}) collective-permute-start(bf16[512,512]{1,0:T(8,128)(2,1)S(1)} %cross.1), channel_id=1, source_target_pairs={{0,1},{1,0},{2,3},{3,2},{4,5},{5,4},{6,7},{7,6},{8,9},{9,8},{10,11... | collective-permute-start | bytes 1572872 | tf_op jit(solution)/shard_map/ppermute | solution.py:38
  99.6 1.2 collective-permute-start.27
  100.8 1.8 %collective-permute-start.15 = (bf16[256,512]{1,0:T(8,128)(2,1)S(1)}, bf16[256,512]{1,0:T(8,128)(2,1)S(1)}, u32[]{:S(2)}, u32[]{:S(2)}) collective-permute-start(bf16[256,512]{1,0:T(8,128)(2,1)S(1)} %add_convert_fusion.1), channel_id=1, source_target_pairs={{0,2},{1,3},{2,0},{3,1},{4,6},{5,7},{6,4},{7,5},{8,10},{9,11},{10,... | collective-permute-start | bytes 786440 | tf_op jit(solution)/shard_map/ppermute | solution.py:38
  102.7 10.3 %collective-permute-done.27.back = bf16[2,256,256]{2,1,0:T(8,128)(2,1)S(1)} collective-permute-done((bf16[2,256,256]{2,1,0:T(8,128)(2,1)S(1)}, bf16[2,256,256]{2,1,0:T(8,128)(2,1)S(1)}, u32[]{:S(2)}, u32[]{:S(2)}) %collective-permute-start.27) | collective-permute-done | bytes 262176 | tf_op jit(solution)/shard_map/ppermute | solution.py:38
  113.0 1.3 %weight_out.1 = bf16[512,256]{1,0:T(8,128)(2,1)} custom-call(s32[3]{0:T(128)S(1)} %pad_add_fusion.pos, f32[2,256,256]{2,1,0:T(8,128)S(1)} %get-tuple-element.155.own, bf16[2,256,256]{2,1,0:T(8,128)(2,1)S(1)} %collective-permute-done.27.back), custom_call_target="tpu_custom_call" | custom-call | bytes 1200000 | tf_op jit(solution)/shard_map/weight_out/pallas_call | solution.py:644
  114.3 1.8 %place.1 = (bf16[512,512]{1,0:T(8,128)(2,1)}, bf16[512,512]{1,0:T(8,128)(2,1)}, bf16[512,512]{1,0:T(8,128)(2,1)}) custom-call(s32[3]{0:T(128)S(1)} %pad_add_fusion.pos, bf16[512,256]{1,0:T(8,128)(2,1)S(1)} %get-tuple-element.133.q_own, bf16[512,512]{1,0:T(8,128)(2,1)S(1)} %get-tuple-element.146.kv_own, bf16[512,768]{1,0:T(8,128)(2,1)S(1)} %collective-permute-done.24.recv), custom_call_target="tpu_custom_call" | custom-call | bytes 1200000 | tf_op jit(solution)/shard_map/place/pallas_call | solution.py:588
  (65 shorter events, 15.4 us)
Async XLA Ops:
  0.6 4.8 %collective-permute-start.2 = (bf16[512,512]{1,0:T(8,128)(2,1)}, bf16[512,512]{1,0:T(8,128)(2,1)S(1)}, u32[]{:S(2)}, u32[]{:S(2)}) collective-permute-start(bf16[512,512]{1,0:T(8,128)(2,1)} %q_ref.1), channel_id=1, source_target_pairs={{0,8},{8,0},{16,24},{24,16},{32,40},{40,32},{48,56},{56,48},{64,72... | collective-permute-start | bytes 1572872 | tf_op jit(solution)/shard_map/ppermute | solution.py:38
  0.7 4.7 %collective-permute-start = (bf16[512,512]{1,0:T(8,128)(2,1)}, bf16[512,512]{1,0:T(8,128)(2,1)S(1)}, u32[]{:S(2)}, u32[]{:S(2)}) collective-permute-start(bf16[512,512]{1,0:T(8,128)(2,1)} %k_ref.1), channel_id=1, source_target_pairs={{0,8},{8,0},{16,24},{24,16},{32,40},{40,32},{48,56},{56,48},{64,72... | collective-permute-start | bytes 1572872 | tf_op jit(solution)/shard_map/ppermute | solution.py:38
  1.2 4.2 %collective-permute-start.1 = (bf16[512,512]{1,0:T(8,128)(2,1)}, bf16[512,512]{1,0:T(8,128)(2,1)S(1)}, u32[]{:S(2)}, u32[]{:S(2)}) collective-permute-start(bf16[512,512]{1,0:T(8,128)(2,1)} %v_ref.1), channel_id=1, source_target_pairs={{0,8},{8,0},{16,24},{24,16},{32,40},{40,32},{48,56},{56,48},{64,72... | collective-permute-start | bytes 1572872 | tf_op jit(solution)/shard_map/ppermute | solution.py:38
  1.4 1.0 copy-start.3
  6.3 17.4 %collective-permute-start.6 = (bf16[512,512]{1,0:T(8,128)(2,1)S(1)}, bf16[512,512]{1,0:T(8,128)(2,1)S(1)}, u32[]{:S(2)}, u32[]{:S(2)}) collective-permute-start(bf16[512,512]{1,0:T(8,128)(2,1)S(1)} %get-tuple-element.84.l1_ref), channel_id=1, source_target_pairs={{0,16},{8,24},{16,0},{24,8},{32,48},{40,56},{48,32},{56,40},{64,80... | collective-permute-start | bytes 1572872 | tf_op jit(solution)/shard_map/ppermute | solution.py:38
  7.9 16.4 %copy-start = (bf16[512,4096]{1,0:T(8,128)(2,1)S(1)}, bf16[512,4096]{1,0:T(8,128)(2,1)}, u32[]{:S(2)}) copy-start(bf16[512,4096]{1,0:T(8,128)(2,1)} %w_other.3) | copy-start | bytes 12582916
  8.9 14.7 %collective-permute-start.3 = (bf16[256,512]{1,0:T(8,128)(2,1)S(1)}, bf16[256,512]{1,0:T(8,128)(2,1)S(1)}, u32[]{:S(2)}, u32[]{:S(2)}) collective-permute-start(bf16[256,512]{1,0:T(8,128)(2,1)S(1)} %get-tuple-element.87), channel_id=1, source_target_pairs={{0,32},{8,40},{16,48},{24,56},{32,0},{40,8},{48,16},{56,24},{64,96... | collective-permute-start | bytes 786440 | tf_op jit(solution)/shard_map/ppermute | solution.py:38
  11.0 12.7 %collective-permute-start.5 = (bf16[128,512]{1,0:T(8,128)(2,1)S(1)}, bf16[128,512]{1,0:T(8,128)(2,1)S(1)}, u32[]{:S(2)}, u32[]{:S(2)}) collective-permute-start(bf16[128,512]{1,0:T(8,128)(2,1)S(1)} %get-tuple-element.88), channel_id=1, source_target_pairs={{0,64},{8,72},{16,80},{24,88},{32,96},{40,104},{48,112},{56,120},{... | collective-permute-start | bytes 393224 | tf_op jit(solution)/shard_map/ppermute | solution.py:38
  14.5 9.1 %collective-permute-start.4 = (bf16[128,512]{1,0:T(8,128)(2,1)S(1)}, bf16[128,512]{1,0:T(8,128)(2,1)S(1)}, u32[]{:S(2)}, u32[]{:S(2)}) collective-permute-start(bf16[128,512]{1,0:T(8,128)(2,1)S(1)} %get-tuple-element.88), channel_id=1, source_target_pairs={{0,96},{8,104},{16,112},{24,120},{32,64},{40,72},{48,80},{56,88},{... | collective-permute-start | bytes 393224 | tf_op jit(solution)/shard_map/ppermute | solution.py:38
  23.7 13.2 %collective-permute-start.7 = (bf16[512,512]{1,0:T(8,128)(2,1)S(1)}, bf16[512,512]{1,0:T(8,128)(2,1)S(1)}, u32[]{:S(2)}, u32[]{:S(2)}) collective-permute-start(bf16[512,512]{1,0:T(8,128)(2,1)S(1)} %pad_maximum_fusion.2.refs_1_.refs_3_.refs_4_), channel_id=1, source_target_pairs={{0,16},{8,24},{16,0},{24,8},{32,48},{40,56},{48,32},{56,40},{64,80... | collective-permute-start | bytes 1572872 | tf_op jit(solution)/shard_map/ppermute | solution.py:38
  24.3 2.2 %copy-start.1 = (bf16[512,4096]{1,0:T(8,128)(2,1)S(1)}, bf16[512,4096]{1,0:T(8,128)(2,1)}, u32[]{:S(2)}) copy-start(bf16[512,4096]{1,0:T(8,128)(2,1)} %g_own.1) | copy-start | bytes 12582916
  37.0 5.3 %collective-permute-start.10 = (bf16[512,2048]{1,0:T(8,128)(2,1)S(1)}, bf16[512,2048]{1,0:T(8,128)(2,1)S(1)}, u32[]{:S(2)}, u32[]{:S(2)}) collective-permute-start(bf16[512,2048]{1,0:T(8,128)(2,1)S(1)} %get-tuple-element.106), channel_id=1, source_target_pairs={{0,8},{8,0},{16,24},{24,16},{32,40},{40,32},{48,56},{56,48},{64,72... | collective-permute-start | bytes 6291464 | tf_op jit(solution)/shard_map/ppermute | solution.py:38
  39.3 2.9 %collective-permute-start.8 = (bf16[256,1024]{1,0:T(8,128)(2,1)S(1)}, bf16[256,1024]{1,0:T(8,128)(2,1)S(1)}, u32[]{:S(2)}, u32[]{:S(2)}) collective-permute-start(bf16[256,1024]{1,0:T(8,128)(2,1)S(1)} %get-tuple-element.127.o_ref), channel_id=1, source_target_pairs={{0,8},{8,0},{16,24},{24,16},{32,40},{40,32},{48,56},{56,48},{64,72... | collective-permute-start | bytes 1572872 | tf_op jit(solution)/shard_map/ppermute | solution.py:38
  39.9 2.3 %collective-permute-start.9 = (bf16[256,512]{1,0:T(8,128)(2,1)S(1)}, bf16[256,512]{1,0:T(8,128)(2,1)S(1)}, u32[]{:S(2)}, u32[]{:S(2)}) collective-permute-start(bf16[256,512]{1,0:T(8,128)(2,1)S(1)} %get-tuple-element.105), channel_id=1, source_target_pairs={{0,8},{8,0},{16,24},{24,16},{32,40},{40,32},{48,56},{56,48},{64,72... | collective-permute-start | bytes 786440 | tf_op jit(solution)/shard_map/ppermute | solution.py:38
  45.3 28.7 %collective-permute-start.11 = (bf16[512,512]{1,0:T(8,128)(2,1)S(1)}, bf16[512,512]{1,0:T(8,128)(2,1)S(1)}, u32[]{:S(2)}, u32[]{:S(2)}) collective-permute-start(bf16[512,512]{1,0:T(8,128)(2,1)S(1)} %get-tuple-element.118), channel_id=1, source_target_pairs={{0,6},{1,7},{2,4},{3,5},{4,2},{5,3},{6,0},{7,1},{8,14},{9,15},{10,... | collective-permute-start | bytes 1572872 | tf_op jit(solution)/shard_map/ppermute | solution.py:38
  48.3 25.7 %collective-permute-start.12 = (bf16[512,512]{1,0:T(8,128)(2,1)S(1)}, bf16[512,512]{1,0:T(8,128)(2,1)S(1)}, u32[]{:S(2)}, u32[]{:S(2)}) collective-permute-start(bf16[512,512]{1,0:T(8,128)(2,1)S(1)} %get-tuple-element.121), channel_id=1, source_target_pairs={{0,2},{1,3},{2,0},{3,1},{4,6},{5,7},{6,4},{7,5},{8,10},{9,11},{10,... | collective-permute-start | bytes 1572872 | tf_op jit(solution)/shard_map/ppermute | solution.py:38
  55.1 17.1 %collective-permute-start.18 = (bf16[256,512]{1,0:T(8,128)(2,1)S(1)}, bf16[256,512]{1,0:T(8,128)(2,1)S(1)}, u32[]{:S(2)}, u32[]{:S(2)}) collective-permute-start(bf16[256,512]{1,0:T(8,128)(2,1)S(1)} %get-tuple-element.137), channel_id=1, source_target_pairs={{0,96},{8,104},{16,112},{24,120},{32,64},{40,72},{48,80},{56,88},{... | collective-permute-start | bytes 786440 | tf_op jit(solution)/shard_map/ppermute | solution.py:38
  56.4 15.7 %collective-permute-start.19 = (bf16[256,512]{1,0:T(8,128)(2,1)S(1)}, bf16[256,512]{1,0:T(8,128)(2,1)S(1)}, u32[]{:S(2)}, u32[]{:S(2)}) collective-permute-start(bf16[256,512]{1,0:T(8,128)(2,1)S(1)} %get-tuple-element.138), channel_id=1, source_target_pairs={{0,64},{8,72},{16,80},{24,88},{32,96},{40,104},{48,112},{56,120},{... | collective-permute-start | bytes 786440 | tf_op jit(solution)/shard_map/ppermute | solution.py:38
  57.1 20.7 %collective-permute-start.22 = (bf16[512,512]{1,0:T(8,128)(2,1)S(1)}, bf16[512,512]{1,0:T(8,128)(2,1)S(1)}, u32[]{:S(2)}, u32[]{:S(2)}) collective-permute-start(bf16[512,512]{1,0:T(8,128)(2,1)S(1)} %get-tuple-element.142), channel_id=1, source_target_pairs={{0,32},{8,40},{16,48},{24,56},{32,0},{40,8},{48,16},{56,24},{64,96... | collective-permute-start | bytes 1572872 | tf_op jit(solution)/shard_map/ppermute | solution.py:38
  59.3 3.0 %copy-start.2 = (bf16[512,4096]{1,0:T(8,128)(2,1)S(1)}, bf16[512,4096]{1,0:T(8,128)(2,1)}, u32[]{:S(2)}) copy-start(bf16[512,4096]{1,0:T(8,128)(2,1)} %g_own.1) | copy-start | bytes 12582916
  72.2 15.2 %collective-permute-start.20 = (bf16[2,2,256,256]{3,2,1,0:T(8,128)(2,1)S(1)}, bf16[2,2,256,256]{3,2,1,0:T(8,128)(2,1)S(1)}, u32[]{:S(2)}, u32[]{:S(2)}) collective-permute-start(bf16[2,2,256,256]{3,2,1,0:T(8,128)(2,1)S(1)} %get-tuple-element.139), channel_id=1, source_target_pairs={{0,32},{8,40},{16,48},{24,56},{32,0},{40,8},{48,16},{56,24},{64,96... | collective-permute-start | bytes 1572872 | tf_op jit(solution)/shard_map/ppermute | solution.py:38
  72.3 15.1 %collective-permute-start.21 = (bf16[2,2,256,256]{3,2,1,0:T(8,128)(2,1)S(1)}, bf16[2,2,256,256]{3,2,1,0:T(8,128)(2,1)S(1)}, u32[]{:S(2)}, u32[]{:S(2)}) collective-permute-start(bf16[2,2,256,256]{3,2,1,0:T(8,128)(2,1)S(1)} %get-tuple-element.140), channel_id=1, source_target_pairs={{0,96},{8,104},{16,112},{24,120},{32,64},{40,72},{48,80},{56,88},{... | collective-permute-start | bytes 1572872 | tf_op jit(solution)/shard_map/ppermute | solution.py:38
  74.2 17.9 %collective-permute-start.13 = (bf16[768,512]{1,0:T(8,128)(2,1)S(1)}, bf16[768,512]{1,0:T(8,128)(2,1)S(1)}, u32[]{:S(2)}, u32[]{:S(2)}) collective-permute-start(bf16[768,512]{1,0:T(8,128)(2,1)S(1)} %pad_maximum_fusion), channel_id=1, source_target_pairs={{0,2},{1,3},{2,0},{3,1},{4,6},{5,7},{6,4},{7,5},{8,10},{9,11},{10,... | collective-permute-start | bytes 2359304 | tf_op jit(solution)/shard_map/ppermute | solution.py:38
  76.2 18.6 %collective-permute-start.14 = (bf16[768,512]{1,0:T(8,128)(2,1)S(1)}, bf16[768,512]{1,0:T(8,128)(2,1)S(1)}, u32[]{:S(2)}, u32[]{:S(2)}) collective-permute-start(bf16[768,512]{1,0:T(8,128)(2,1)S(1)} %pad_maximum_fusion.1), channel_id=1, source_target_pairs={{0,6},{1,7},{2,4},{3,5},{4,2},{5,3},{6,0},{7,1},{8,14},{9,15},{10,... | collective-permute-start | bytes 2359304 | tf_op jit(solution)/shard_map/ppermute | solution.py:38
  78.3 10.9 %collective-permute-start.23 = (bf16[512,512]{1,0:T(8,128)(2,1)S(1)}, bf16[512,512]{1,0:T(8,128)(2,1)S(1)}, u32[]{:S(2)}, u32[]{:S(2)}) collective-permute-start(bf16[512,512]{1,0:T(8,128)(2,1)S(1)} %relay.1), channel_id=1, source_target_pairs={{0,16},{8,24},{16,0},{24,8},{32,48},{40,56},{48,32},{56,40},{64,80... | collective-permute-start | bytes 1572872 | tf_op jit(solution)/shard_map/ppermute | solution.py:38
  87.5 11.2 %collective-permute-start.26 = (bf16[2,256,256]{2,1,0:T(8,128)(2,1)S(1)}, bf16[2,256,256]{2,1,0:T(8,128)(2,1)S(1)}, u32[]{:S(2)}, u32[]{:S(2)}) collective-permute-start(bf16[2,256,256]{2,1,0:T(8,128)(2,1)S(1)} %fusion), channel_id=1, source_target_pairs={{0,96},{8,104},{16,112},{24,120},{32,64},{40,72},{48,80},{56,88},{... | collective-permute-start | bytes 786440 | tf_op jit(solution)/shard_map/ppermute | solution.py:38
  90.5 23.8 %collective-permute-start.24 = (bf16[512,768]{1,0:T(8,128)(2,1)S(1)}, bf16[512,768]{1,0:T(8,128)(2,1)S(1)}, u32[]{:S(2)}, u32[]{:S(2)}) collective-permute-start(bf16[512,768]{1,0:T(8,128)(2,1)S(1)} %get-tuple-element.147), channel_id=1, source_target_pairs={{0,8},{8,0},{16,24},{24,16},{32,40},{40,32},{48,56},{56,48},{64,72... | collective-permute-start | bytes 2359304 | tf_op jit(solution)/shard_map/ppermute | solution.py:38
  90.6 8.8 %collective-permute-start.25 = (bf16[2,256,256]{2,1,0:T(8,128)(2,1)S(1)}, bf16[2,256,256]{2,1,0:T(8,128)(2,1)S(1)}, u32[]{:S(2)}, u32[]{:S(2)}) collective-permute-start(bf16[2,256,256]{2,1,0:T(8,128)(2,1)S(1)} %fusion.1), channel_id=1, source_target_pairs={{0,32},{8,40},{16,48},{24,56},{32,0},{40,8},{48,16},{56,24},{64,96... | collective-permute-start | bytes 786440 | tf_op jit(solution)/shard_map/ppermute | solution.py:38
  94.9 21.2 %collective-permute-start.17 = (bf16[512,512]{1,0:T(8,128)(2,1)S(1)}, bf16[512,512]{1,0:T(8,128)(2,1)S(1)}, u32[]{:S(2)}, u32[]{:S(2)}) collective-permute-start(bf16[512,512]{1,0:T(8,128)(2,1)S(1)} %cross.1), channel_id=1, source_target_pairs={{0,1},{1,0},{2,3},{3,2},{4,5},{5,4},{6,7},{7,6},{8,9},{9,8},{10,11... | collective-permute-start | bytes 1572872 | tf_op jit(solution)/shard_map/ppermute | solution.py:38
  98.1 18.0 %collective-permute-start.16 = (bf16[256,512]{1,0:T(8,128)(2,1)S(1)}, bf16[256,512]{1,0:T(8,128)(2,1)S(1)}, u32[]{:S(2)}, u32[]{:S(2)}) collective-permute-start(bf16[256,512]{1,0:T(8,128)(2,1)S(1)} %add_convert_fusion), channel_id=1, source_target_pairs={{0,6},{1,7},{2,4},{3,5},{4,2},{5,3},{6,0},{7,1},{8,14},{9,15},{10,... | collective-permute-start | bytes 786440 | tf_op jit(solution)/shard_map/ppermute | solution.py:38
  99.6 13.4 %collective-permute-start.27 = (bf16[2,256,256]{2,1,0:T(8,128)(2,1)S(1)}, bf16[2,256,256]{2,1,0:T(8,128)(2,1)S(1)}, u32[]{:S(2)}, u32[]{:S(2)}) collective-permute-start(bf16[2,256,256]{2,1,0:T(8,128)(2,1)S(1)} %get-tuple-element.156), channel_id=1, source_target_pairs={{0,16},{8,24},{16,0},{24,8},{32,48},{40,56},{48,32},{56,40},{64,80... | collective-permute-start | bytes 786440 | tf_op jit(solution)/shard_map/ppermute | solution.py:38
  100.8 15.3 %collective-permute-start.15 = (bf16[256,512]{1,0:T(8,128)(2,1)S(1)}, bf16[256,512]{1,0:T(8,128)(2,1)S(1)}, u32[]{:S(2)}, u32[]{:S(2)}) collective-permute-start(bf16[256,512]{1,0:T(8,128)(2,1)S(1)} %add_convert_fusion.1), channel_id=1, source_target_pairs={{0,2},{1,3},{2,0},{3,1},{4,6},{5,7},{6,4},{7,5},{8,10},{9,11},{10,... | collective-permute-start | bytes 786440 | tf_op jit(solution)/shard_map/ppermute | solution.py:38
  (2 other events, 2.1 us)

commit v2 on v1

--- a/solution.py
+++ b/solution.py
@@ -335,52 +335,29 @@
     )(pos, attn, attn_other, out_weight, out_weight)
 
 
-def weight_kernel(
-    pos, o_ref, r_ref, g_own, g_recv, keep, first_1, first_3, late_1, late_3
-):
-    dz, dx = pl.program_id(0) // 2, pl.program_id(0) % 2
+def weight_kernel(pos, o_ref, r_ref, g_own, g_recv, out_ref):
     own, far = g_own[...], g_recv[...]
-    up = (mm(o_ref[:, :512], own, NN) + mm(o_ref[:, 512:], far, NN)).astype(BF)
-    down = (mm(r_ref[:, 512:], own, NN) + mm(r_ref[:, :512], far, NN)).astype(BF)
-
-    @pl.when(dz == 0)
-    def _():
-        keep[0, dx] = up
-        keep[1, dx] = down
-
-    @pl.when(dz == 1)
-    def _():
-        first_1[1, dx] = up
-        late_1[dx] = down
-
-    @pl.when(dz == 2)
-    def _():
-        first_1[0, dx] = up
-        first_3[0, dx] = down
-
-    @pl.when(dz == 3)
-    def _():
-        first_3[1, dx] = down
-        late_3[dx] = up
-
-
-def weight_call(pos, attn, attn_other, output_grad, grad_recv):
+    out_ref[0, 0] = (mm(o_ref[:, :512], own, NN) + mm(o_ref[:, 512:], far, NN)).astype(BF)
+    out_ref[0, 1] = (mm(r_ref[:, 512:], own, NN) + mm(r_ref[:, :512], far, NN)).astype(BF)
+
+
+def weight_call(pos, attn, attn_other, output_grad, grad_recv, dx):
     return pl.pallas_call(
         weight_kernel,
         grid_spec=pltpu.PrefetchScalarGridSpec(
             num_scalar_prefetch=1,
-            grid=(8,),
+            grid=(4,),
             in_specs=[
                 whole(256, 1024),
                 whole(256, 1024),
-                pl.BlockSpec((512, 256), lambda i, pos: (0, (pos[2] ^ i) * 2 + pos[0])),
-                pl.BlockSpec((512, 256), lambda i, pos: (0, pos[2] ^ i)),
+                pl.BlockSpec((512, 256), lambda i, pos: (0, (pos[2] ^ (2 * i + dx)) * 2 + pos[0])),
+                pl.BlockSpec((512, 256), lambda i, pos: (0, pos[2] ^ (2 * i + dx))),
             ],
-            out_specs=[whole(2, 2, 256, 256)] * 3 + [whole(2, 256, 256)] * 2,
-        ),
-        out_shape=[shape((2, 2, 256, 256))] * 3 + [shape((2, 256, 256))] * 2,
-        compiler_params=params(),
-        cost_estimate=cost(5.0),
+            out_specs=pl.BlockSpec((1, 2, 256, 256), lambda i, pos: (i, 0, 0, 0)),
+        ),
+        out_shape=shape((4, 2, 256, 256)),
+        compiler_params=params(),
+        cost_estimate=cost(2.5),
         name="weight_term",
     )(pos, attn, attn_other, output_grad, grad_recv)
 
@@ -553,51 +530,59 @@
     )(side, *along)
 
 
-def collect_kernel(kv_ref, q_ref, side_ref, z1_ref, z3_ref, z2_ref, own_ref, send_ref):
-    send_ref[:, 512:] = q_ref[...]
-    for part, out in ((1, send_ref), (0, own_ref)):
-        total = kv_ref[part * 512 : (part + 1) * 512, :]
+def collect_kernel(kv_ref, q_ref, side_ref, z1_ref, z3_ref, z2_ref, own_ref, send_k, send_v):
+    send_k[:, 256:] = q_ref[:, :128]
+    send_v[:, 256:] = q_ref[:, 128:]
+    for part in (1, 0):
+        start = kv_ref[part * 512 : (part + 1) * 512, :]
         parts = spread(512, 1, [side_ref], part)
         parts += spread(512, 2, [z1_ref.at[:256]], part)
         parts += spread(512, 3, [z3_ref.at[:128], z2_ref.at[:128]], part)
-        out[:, :512] = functools.reduce(jnp.add, parts, total).astype(BF)
+        done = functools.reduce(jnp.add, parts, start).astype(BF)
+        if part:
+            send_k[:, :256] = done[:, :256]
+            send_v[:, :256] = done[:, 256:]
+        else:
+            own_ref[...] = done
 
 
 def collect_call(kv_grad, q_send, side, *along):
     return pl.pallas_call(
         collect_kernel,
-        out_shape=[shape((512, 512)), shape((512, 768))],
+        out_shape=[shape((512, 512))] + [shape((512, 384))] * 2,
         compiler_params=params(),
         cost_estimate=cost(1.3),
         name="collect",
     )(kv_grad, q_send, side, *along)
 
 
-def place_kernel(pos, q_own, kv_own, recv, q_out, k_out, v_out):
+def place_kernel(pos, q_own, kv_own, recv_k, recv_v, q_out, k_out, v_out):
     mine = pl.ds(pl.multiple_of(pos[0] * 256, 256), 256)
     other = pl.ds(pl.multiple_of((1 - pos[0]) * 256, 256), 256)
     q_out[:, mine] = q_own[...]
-    q_out[:, other] = recv[:, 512:]
+    base = pl.multiple_of((1 - pos[0]) * 256, 128)
+    q_out[:, pl.ds(base, 128)] = recv_k[:, 256:]
+    q_out[:, pl.ds(base + 128, 128)] = recv_v[:, 256:]
     k_out[:, mine] = kv_own[:, :256]
-    k_out[:, other] = recv[:, :256]
+    k_out[:, other] = recv_k[:, :256]
     v_out[:, mine] = kv_own[:, 256:]
-    v_out[:, other] = recv[:, 256:512]
-
-
-def place_call(pos, q_own, kv_own, recv):
+    v_out[:, other] = recv_v[:, :256]
+
+
+def place_call(pos, q_own, kv_own, *recv):
     return pl.pallas_call(
         place_kernel,
         grid_spec=pltpu.PrefetchScalarGridSpec(
             num_scalar_prefetch=1,
             grid=(1,),
-            in_specs=[whole(512, 256), whole(512, 512), whole(512, 768)],
+            in_specs=[whole(512, 256), whole(512, 512)] + [whole(512, 384)] * 2,
             out_specs=[whole(512, 512)] * 3,
         ),
         out_shape=[shape((512, 512))] * 3,
         compiler_params=params(),
         cost_estimate=cost(1.0),
         name="place",
-    )(pos, q_own, kv_own, recv)
+    )(pos, q_own, kv_own, *recv)
 
 
 def total(*terms):
@@ -614,20 +599,25 @@
     out_ref[256:, :] = total(keep[256:, :], o3[512:, :], end_1[...], cross[256:, :]).astype(BF)
 
 
-def weight_sum_kernel(keep, w1, w3, end_1, end_3, own_ref, send_ref):
-    up = total(keep[0], w1[1], end_3[...])
-    down = total(keep[1], w3[1], end_1[...])
-    own_ref[0] = up[0]
-    own_ref[1] = down[0]
-    send_ref[0] = up[1].astype(BF)
-    send_ref[1] = down[1].astype(BF)
-
-
-def weight_out_kernel(pos, own, back, out_ref):
-    for part in range(2):
-        row = pos[0] * 256 if part == 0 else (1 - pos[0]) * 256
-        rows = pl.ds(pl.multiple_of(row, 256), 256)
-        out_ref[rows, :] = total(own[part], back[part]).astype(BF)
+def weight_sum_kernel(own, wx, keep, first_1, first_3, late_1, late_3):
+    def part(dz, half):
+        return total(own[dz, half], wx[dz, half])
+
+    keep[0] = part(0, 0)
+    keep[1] = part(0, 1)
+    first_1[0] = part(2, 0).astype(BF)
+    first_1[1] = part(1, 0).astype(BF)
+    first_3[0] = part(2, 1).astype(BF)
+    first_3[1] = part(3, 1).astype(BF)
+    late_1[...] = part(1, 1).astype(BF)
+    late_3[...] = part(3, 0).astype(BF)
+
+
+def weight_out_kernel(pos, keep, w1, w3, we_1, we_3, out_ref):
+    up = total(keep[0], w1[1], we_3[...])
+    down = total(keep[1], w3[1], we_1[...])
+    for row, part in ((pos[0] * 256, up), ((1 - pos[0]) * 256, down)):
+        out_ref[pl.ds(pl.multiple_of(row, 256), 256), :] = part.astype(BF)
 
 
 def plain_call(kernel, out_shape, us, name, *args):
@@ -640,20 +630,20 @@
     )(*args)
 
 
-def weight_out_call(pos, own, back):
+def weight_out_call(pos, *args):
     return pl.pallas_call(
         weight_out_kernel,
         grid_spec=pltpu.PrefetchScalarGridSpec(
             num_scalar_prefetch=1,
             grid=(1,),
-            in_specs=[whole(2, 256, 256)] * 2,
+            in_specs=[whole(2, 256, 256)] * 3 + [whole(256, 256)] * 2,
             out_specs=whole(512, 256),
         ),
         out_shape=shape((512, 256)),
         compiler_params=params(),
         cost_estimate=cost(1.0),
         name="weight_out",
-    )(pos, own, back)
+    )(pos, *args)
 
 
 def add(*terms):
@@ -702,57 +692,59 @@
     )
     got_c1, got_c3 = swap(first_c1, "head", 2), swap(first_c3, "head", 6)
 
-    attn_g, qt_g = after((attn, qt), keep_c)
+    attn_v, other_v = after((attn, attn_other), keep_c)
+    w_cross = weight_call(pos, attn_v, other_v, output_grad, grad_recv, 1)
+    w_recv = swap(w_cross, "ctx", 2)
+
+    attn_g, qt_g = after((attn, qt), w_cross)
     side_grad, *level_grads, dq = far_grad_call(
         qt_g, da_own, da_recv, attn_g, scales, e_middle, e_last, far
     )
-    back = [swap(g, "ctx", mask) for g, mask in zip(level_grads, (4, 12, 8))]
+    back = [swap(g, "ctx", mask) for g, mask in zip(level_grads[:2], (4, 12))]
 
     attn_p, other_p = after((attn, attn_other), side_grad)
     keep_o, first_o1, first_o3, late_o1, late_o3 = project_call(
         pos, attn_p, other_p, out_weight, 0
     )
-    attn_w, other_w = after((attn, attn_other), keep_o)
-    keep_w, first_w1, first_w3, late_w1, late_w3 = weight_call(
-        pos, attn_w, other_w, output_grad, grad_recv
-    )
-    qt_n, da_n = after((qt, da_own), keep_w)
-    kv_grad, q_own, q_send = near_grad_call(qt_n, da_n, da_recv, attn, scales, e_near, kv_own, kv_sib, dq)
-
     send_1 = jnp.concatenate([low(late_c1, got_c3[:256]), first_o1], axis=0)
     send_3 = jnp.concatenate([low(late_c3, got_c1[:256]), first_o3], axis=0)
     send_1, send_3 = after((send_1, send_3))
     got_o1, got_o3 = swap(send_1, "head", 2), swap(send_3, "head", 6)
+    back.append(swap(after(level_grads[2], back[1]), "ctx", 8))
+    attn_w, other_w = after((attn, attn_other), (keep_o, send_1, send_3))
+    w_own = weight_call(pos, attn_w, other_w, output_grad, grad_recv, 0)
+    qt_n, da_n = after((qt, da_own), w_own)
+    kv_grad, q_own, q_send = near_grad_call(
+        qt_n, da_n, da_recv, attn, scales, e_near, kv_own, kv_sib, dq
+    )
 
     relayed = relay_call(after(side_grad, send_1, send_3, kv_grad), *back)
     side_back = swap(relayed, "ctx", 2)
-    first_w1, first_w3 = after((first_w1, first_w3), back[1:])
+    keep_w, first_w1, first_w3, late_w1, late_w3 = plain_call(
+        weight_sum_kernel,
+        [shape((2, 256, 256), F32)] + [shape((2, 256, 256))] * 2 + [shape((256, 256))] * 2,
+        0.5,
+        "weight_sum",
+        *(after(w_own, relayed), w_recv),
+    )
     got_w1, got_w3 = swap(first_w1, "ctx", 4), swap(first_w3, "ctx", 12)
 
     cross = plain_call(
         cross_kernel, shape((512, 512)), 1.0, "cross", keep_c, got_c1, got_c3, got_o1, got_o3
     )
-    got_w1, got_w3 = after((got_w1, got_w3), relayed)
+    got_w1, got_w3 = after((got_w1, got_w3), (relayed, cross))
     cross_back = swap(cross, "head", 1)
     end_1 = swap(low(late_o1, got_o3[256:512]), "head", 2)
     end_3 = swap(low(late_o3, got_o1[256:512]), "head", 6)
+    end_w1 = swap(low(late_w1, got_w3[0]), "ctx", 4)
+    end_w3 = swap(low(late_w3, got_w1[0]), "ctx", 12)
+    weight_grad = weight_out_call(pos, keep_w, got_w1, got_w3, end_w1, end_w3)
+
     layer_output = plain_call(
         output_kernel, shape((512, 512)), 1.0, "output", keep_o, got_o1, got_o3, end_1, end_3, cross_back
     )
-
-    end_w1 = swap(low(late_w1, got_w3[0]), "ctx", 4)
-    end_w3 = swap(low(late_w3, got_w1[0]), "ctx", 12)
-    w_own, w_send = plain_call(
-        weight_sum_kernel,
-        [shape((2, 256, 256), F32), shape((2, 256, 256))],
-        1.0,
-        "weight_sum",
-        *(after(keep_w, cross), got_w1, got_w3, end_w1, end_w3),
-    )
-    weight_grad = weight_out_call(pos, w_own, swap(w_send, "ctx", 2))
-
-    kv_done, send = collect_call(after(kv_grad, got_w1), q_send, side_back, *back)
-    query_grad, key_grad, value_grad = place_call(pos, q_own, kv_done, swap(send, "ctx", 1))
+    kv_done, *sends = collect_call(after(kv_grad, (end_w1, end_w3)), q_send, side_back, *back)
+    query_grad, key_grad, value_grad = place_call(pos, q_own, kv_done, *[swap(a, "ctx", 1) for a in sends])
     return (layer_output, query_grad, key_grad, value_grad, weight_grad)
 
 

time: 117 us -> 112 us (0.957)
  waiting for transfers between devices: 33.4 us -> 26.3 us
    ppermute x28 -> x29, waiting for transfers between devices: 33.4 us -> 26.3 us  [swap(): return lax.ppermute(value, axis, [(i, i ^ mask) for i in range(size)])]
    ppermute x28 -> x29, starting transfers between devices: 30 us -> 30.7 us  [swap(): return lax.ppermute(value, axis, [(i, i ^ mask) for i in range(size)])]
    pallas_call x1 -> x2, Pallas kernels: 5.1 us -> 5.42 us  [weight_call(): pl.pallas_call(weight_kernel, grid_spec=pltpu.PrefetchScalarGridSpec(num_...]
  transfers between devices with their start and end apart: 28 -> 29, of which waited for: 10 -> 11; matrix products, arithmetic and copies ran while one was open for 1% -> 0% of each run, Pallas kernels for 36% -> 38%
where the time goes in v2:
time: 112 us; the launch traced here: 111 us
  Pallas kernels  47.5 us (42%)
  starting transfers between devices  30.7 us (27%)
  waiting for transfers between devices  26.3 us (23%)
  local copies, waits for them, and re-layouts  5.32 us (5%)
    ppermute x29, starting transfers between devices, swap(): return lax.ppermute(value, axis, [(i, i ^ mask) for i in range(size)])  30.7 us
    ppermute x29, waiting for transfers between devices, swap(): return lax.ppermute(value, axis, [(i, i ^ mask) for i in range(size)])  26.3 us
    pallas_call x3, Pallas kernels, score_call(): pl.pallas_call(kernel, grid=(2,), in_specs=[per_head(128, 1024), *kv_spec...  11 us
    pallas_call x1, Pallas kernels, far_grad_call(): pl.pallas_call(far_grad_kernel, grid=(2,), in_specs=[*common_specs(), per...  6.6 us
    pallas_call x2, Pallas kernels, project_call(): pl.pallas_call(project_kernel, grid_spec=pltpu.PrefetchScalarGridSpec(num...  5.99 us
    pallas_call x2, Pallas kernels, weight_call(): pl.pallas_call(weight_kernel, grid_spec=pltpu.PrefetchScalarGridSpec(num_...  5.42 us
    unnamed x12, local copies, waits for them, and re-layouts  5.32 us
    pallas_call x1, Pallas kernels, near_grad_call(): pl.pallas_call(near_grad_kernel, grid=(2,), in_specs=[*common_specs(), pl...  4.76 us
  transfers between devices with their start and end apart: 29, of which 11 were waited for; matrix products, arithmetic and copies ran while one was open for 0% of the time, Pallas kernels for 38%

profile of v2, /device:TPU:0, one launch (start us, length us, event | category | flops | bytes accessed | tf_op | source)
XLA Modules:
  0.0 111.3 jit_solution(5186307052157438125)
XLA Ops:
  6.3 1.6 %collective-permute-start.6 = (bf16[512,512]{1,0:T(8,128)(2,1)S(1)}, bf16[512,512]{1,0:T(8,128)(2,1)S(1)}, u32[]{:S(2)}, u32[]{:S(2)}) collective-permute-start(bf16[512,512]{1,0:T(8,128)(2,1)S(1)} %get-tuple-element.84.l1_ref), channel_id=1, source_target_pairs={{0,16},{8,24},{16,0},{24,8},{32,48},{40,56},{48,32},{56,40},{64,80... | collective-permute-start | bytes 1572872 | tf_op jit(solution)/shard_map/ppermute | solution.py:38
  8.9 2.0 %collective-permute-start.3 = (bf16[256,512]{1,0:T(8,128)(2,1)S(1)}, bf16[256,512]{1,0:T(8,128)(2,1)S(1)}, u32[]{:S(2)}, u32[]{:S(2)}) collective-permute-start(bf16[256,512]{1,0:T(8,128)(2,1)S(1)} %get-tuple-element.87), channel_id=1, source_target_pairs={{0,32},{8,40},{16,48},{24,56},{32,0},{40,8},{48,16},{56,24},{64,96... | collective-permute-start | bytes 786440 | tf_op jit(solution)/shard_map/ppermute | solution.py:38
  11.0 3.6 %collective-permute-start.5 = (bf16[128,512]{1,0:T(8,128)(2,1)S(1)}, bf16[128,512]{1,0:T(8,128)(2,1)S(1)}, u32[]{:S(2)}, u32[]{:S(2)}) collective-permute-start(bf16[128,512]{1,0:T(8,128)(2,1)S(1)} %get-tuple-element.88), channel_id=1, source_target_pairs={{0,64},{8,72},{16,80},{24,88},{32,96},{40,104},{48,112},{56,120},{... | collective-permute-start | bytes 393224 | tf_op jit(solution)/shard_map/ppermute | solution.py:38
  14.5 4.2 %near_scores.1 = (bf16[2,2,512,1024]{3,2,1,0:T(8,128)(2,1)S(1)}, f32[256,1024]{1,0:T(8,128)S(1)}, f32[2,8,1024]{2,1,0:T(8,128)S(1)}) custom-call(bf16[256,1024]{1,0:T(8,128)(2,1)S(1)} %get-tuple-element.131.qt_ref, bf16[512,512]{1,0:T(8,128)(2,1)S(1)} %get-tuple-element.89.refs_0_.refs_2_.k_own.v_own, ...), custom_call_target="tpu_custom_call" | custom-call | bytes 5040000 | tf_op jit(solution)/shard_map/near_scores/pallas_call | solution.py:269
  18.8 4.9 %collective-permute-done.5 = bf16[128,512]{1,0:T(8,128)(2,1)S(1)} collective-permute-done((bf16[128,512]{1,0:T(8,128)(2,1)S(1)}, bf16[128,512]{1,0:T(8,128)(2,1)S(1)}, u32[]{:S(2)}, u32[]{:S(2)}) %collective-permute-start.5) | collective-permute-done | bytes 131104 | tf_op jit(solution)/shard_map/ppermute | solution.py:38
  24.3 2.2 %copy-done.1 = bf16[512,4096]{1,0:T(8,128)(2,1)S(1)} copy-done((bf16[512,4096]{1,0:T(8,128)(2,1)S(1)}, bf16[512,4096]{1,0:T(8,128)(2,1)}, u32[]{:S(2)}) %copy-start.1) | copy-done | bytes 4194328
  26.5 4.5 %grad_attention.1 = (bf16[256,512]{1,0:T(8,128)(2,1)S(1)}, bf16[256,512]{1,0:T(8,128)(2,1)S(1)}, bf16[512,2048]{1,0:T(8,128)(2,1)S(1)}) custom-call(s32[3]{0:T(128)S(1)} %pad_add_fusion.pos, bf16[512,4096]{1,0:T(8,128)(2,1)S(1)} %copy-done, bf16[512,4096]{1,0:T(8,128)(2,1)S(1)} %copy-done.1), custom_call_target="tpu_custom_call" | custom-call | bytes 5400000 | tf_op jit(solution)/shard_map/grad_attention/pallas_call | solution.py:67
  31.1 4.4 %middle_scores.1 = (bf16[2,2,512,1024]{3,2,1,0:T(8,128)(2,1)S(1)}, f32[256,1024]{1,0:T(8,128)S(1)}, f32[2,8,1024]{2,1,0:T(8,128)S(1)}) custom-call(bf16[256,1024]{1,0:T(8,128)(2,1)S(1)} %get-tuple-element.131.qt_ref, bf16[512,512]{1,0:T(8,128)(2,1)S(1)} %collective-permute-done.6.refs_0_.refs_2_.refs_3_, ...), custom_call_target="tpu_custom_call" | custom-call | bytes 5040000 | tf_op jit(solution)/shard_map/middle_scores/pallas_call | solution.py:269
  35.5 1.5 %collective-permute-done.7.key.value.refs_2_.refs_5_ = bf16[512,512]{1,0:T(8,128)(2,1)S(1)} collective-permute-done((bf16[512,512]{1,0:T(8,128)(2,1)S(1)}, bf16[512,512]{1,0:T(8,128)(2,1)S(1)}, u32[]{:S(2)}, u32[]{:S(2)}) %collective-permute-start.7) | collective-permute-done | bytes 524320 | tf_op jit(solution)/shard_map/ppermute | solution.py:38
  37.0 2.4 %last_scores.1 = (bf16[2,1,512,1024]{3,2,1,0:T(8,128)(2,1)S(1)}, bf16[256,1024]{1,0:T(8,128)(2,1)S(1)}, f32[2,8,1024]{2,1,0:T(8,128)S(1)}) custom-call(bf16[256,1024]{1,0:T(8,128)(2,1)S(1)} %get-tuple-element.131.qt_ref, bf16[512,512]{1,0:T(8,128)(2,1)S(1)} %collective-permute-done.7.key.value.refs_2_.refs_5_, ...), custom_call_target="tpu_custom_call" | custom-call | bytes 2640000 | tf_op jit(solution)/shard_map/last_scores/pallas_call | solution.py:269
  40.0 2.2 %collective-permute-done.9.da_recv = bf16[256,512]{1,0:T(8,128)(2,1)S(1)} collective-permute-done((bf16[256,512]{1,0:T(8,128)(2,1)S(1)}, bf16[256,512]{1,0:T(8,128)(2,1)S(1)}, u32[]{:S(2)}, u32[]{:S(2)}) %collective-permute-start.9) | collective-permute-done | bytes 262176 | tf_op jit(solution)/shard_map/ppermute | solution.py:38
  42.3 3.0 %project.2 = (bf16[512,512]{1,0:T(8,128)(2,1)S(1)}, bf16[512,512]{1,0:T(8,128)(2,1)S(1)}, bf16[512,512]{1,0:T(8,128)(2,1)S(1)}, bf16[256,512]{1,0:T(8,128)(2,1)S(1)}, bf16[256,512]{1,0:T(8,128)(2,1)S(1)}) custom-call(s32[3]{0:T(128)S(1)} %pad_add_fusion.pos, bf16[256,1024]{1,0:T(8,128)(2,1)S(1)} %get-tuple-element.129.o_ref, ...), custom_call_target="tpu_custom_call" | custom-call | bytes 3600000 | tf_op jit(solution)/shard_map/project/pallas_call | solution.py:322
  45.3 3.1 %collective-permute-start.11 = (bf16[512,512]{1,0:T(8,128)(2,1)S(1)}, bf16[512,512]{1,0:T(8,128)(2,1)S(1)}, u32[]{:S(2)}, u32[]{:S(2)}) collective-permute-start(bf16[512,512]{1,0:T(8,128)(2,1)S(1)} %get-tuple-element.120), channel_id=1, source_target_pairs={{0,6},{1,7},{2,4},{3,5},{4,2},{5,3},{6,0},{7,1},{8,14},{9,15},{10,... | collective-permute-start | bytes 1572872 | tf_op jit(solution)/shard_map/ppermute | solution.py:38
  48.5 2.7 %weight_term.2 = bf16[4,2,256,256]{3,2,1,0:T(8,128)(2,1)S(1)} custom-call(s32[3]{0:T(128)S(1)} %pad_add_fusion.pos, bf16[256,1024]{1,0:T(8,128)(2,1)S(1)} %get-tuple-element.129.o_ref, bf16[256,1024]{1,0:T(8,128)(2,1)S(1)} %collective-permute-done.8.r_ref, bf16[512,4096]{1,0:T(8,128)(2,1)S(1)} %copy-done.2, bf16[512,2048]{1,0:T(8,128)(2,1)S(1)} %collective-permute-done.10.g_recv), custom_call_target="tpu_custom_call" | custom-call | bytes 3000000 | tf_op jit(solution)/shard_map/weight_term/pallas_call | solution.py:345
  52.0 6.6 %far_grads.1 = (bf16[512,512]{1,0:T(8,128)(2,1)S(1)}, bf16[512,512]{1,0:T(8,128)(2,1)S(1)}, bf16[256,512]{1,0:T(8,128)(2,1)S(1)}, bf16[256,512]{1,0:T(8,128)(2,1)S(1)}, f32[256,1024]{1,0:T(8,128)S(1)}) custom-call(bf16[256,1024]{1,0:T(8,128)(2,1)S(1)} %get-tuple-element.131.qt_ref, bf16[256,512]{1,0:T(8,128)(2,1)S(1)} %get-tuple-element.132.da_own, ...), custom_call_target="tpu_custom_call" | custom-call | bytes 8040000 | tf_op jit(solution)/shard_map/far_grads/pallas_call | solution.py:433
  58.6 2.3 %collective-permute-start.19 = (bf16[256,512]{1,0:T(8,128)(2,1)S(1)}, bf16[256,512]{1,0:T(8,128)(2,1)S(1)}, u32[]{:S(2)}, u32[]{:S(2)}) collective-permute-start(bf16[256,512]{1,0:T(8,128)(2,1)S(1)} %get-tuple-element.138), channel_id=1, source_target_pairs={{0,96},{8,104},{16,112},{24,120},{32,64},{40,72},{48,80},{56,88},{... | collective-permute-start | bytes 786440 | tf_op jit(solution)/shard_map/ppermute | solution.py:38
  60.9 3.0 %project.3 = (bf16[512,512]{1,0:T(8,128)(2,1)S(1)}, bf16[512,512]{1,0:T(8,128)(2,1)S(1)}, bf16[512,512]{1,0:T(8,128)(2,1)S(1)}, bf16[256,512]{1,0:T(8,128)(2,1)S(1)}, bf16[256,512]{1,0:T(8,128)(2,1)S(1)}) custom-call(s32[3]{0:T(128)S(1)} %pad_add_fusion.pos, bf16[256,1024]{1,0:T(8,128)(2,1)S(1)} %get-tuple-element.129.o_ref, ...), custom_call_target="tpu_custom_call" | custom-call | bytes 3600000 | tf_op jit(solution)/shard_map/project/pallas_call | solution.py:322
  64.2 2.0 %collective-permute-start.13 = (bf16[768,512]{1,0:T(8,128)(2,1)S(1)}, bf16[768,512]{1,0:T(8,128)(2,1)S(1)}, u32[]{:S(2)}, u32[]{:S(2)}) collective-permute-start(bf16[768,512]{1,0:T(8,128)(2,1)S(1)} %pad_maximum_fusion), channel_id=1, source_target_pairs={{0,2},{1,3},{2,0},{3,1},{4,6},{5,7},{6,4},{7,5},{8,10},{9,11},{10,... | collective-permute-start | bytes 2359304 | tf_op jit(solution)/shard_map/ppermute | solution.py:38
  67.6 1.3 %collective-permute-start.20 = (bf16[256,512]{1,0:T(8,128)(2,1)S(1)}, bf16[256,512]{1,0:T(8,128)(2,1)S(1)}, u32[]{:S(2)}, u32[]{:S(2)}) collective-permute-start(bf16[256,512]{1,0:T(8,128)(2,1)S(1)} %get-tuple-element.140), channel_id=1, source_target_pairs={{0,64},{8,72},{16,80},{24,88},{32,96},{40,104},{48,112},{56,120},{... | collective-permute-start | bytes 786440 | tf_op jit(solution)/shard_map/ppermute | solution.py:38
  68.9 2.7 %weight_term.3.own = bf16[4,2,256,256]{3,2,1,0:T(8,128)(2,1)S(1)} custom-call(s32[3]{0:T(128)S(1)} %pad_add_fusion.pos, bf16[256,1024]{1,0:T(8,128)(2,1)S(1)} %get-tuple-element.129.o_ref, bf16[256,1024]{1,0:T(8,128)(2,1)S(1)} %collective-permute-done.8.r_ref, bf16[512,4096]{1,0:T(8,128)(2,1)S(1)} %copy-done.2, ...), custom_call_target="tpu_custom_call" | custom-call | bytes 3000000 | tf_op jit(solution)/shard_map/weight_term/pallas_call | solution.py:345
  71.6 4.8 %near_grads.1 = (f32[1024,512]{1,0:T(8,128)S(1)}, bf16[512,256]{1,0:T(8,128)(2,1)S(1)}, bf16[512,256]{1,0:T(8,128)(2,1)S(1)}) custom-call(bf16[256,1024]{1,0:T(8,128)(2,1)S(1)} %get-tuple-element.131.qt_ref, bf16[256,512]{1,0:T(8,128)(2,1)S(1)} %get-tuple-element.132.da_own, bf16[256,512]{1,0:T(8,128)(2,1)S(1)} %collective-permute-done.9.da_recv, ...), custom_call_target="tpu_custom_call" | custom-call | bytes 5760000 | tf_op jit(solution)/shard_map/near_grads/pallas_call | solution.py:490
  76.4 3.6 %collective-permute-done.20.z2_ref = bf16[256,512]{1,0:T(8,128)(2,1)S(1)} collective-permute-done((bf16[256,512]{1,0:T(8,128)(2,1)S(1)}, bf16[256,512]{1,0:T(8,128)(2,1)S(1)}, u32[]{:S(2)}, u32[]{:S(2)}) %collective-permute-start.20) | collective-permute-done | bytes 262176 | tf_op jit(solution)/shard_map/ppermute | solution.py:38
  80.9 2.3 %collective-permute-start.23 = (bf16[2,256,256]{2,1,0:T(8,128)(2,1)S(1)}, bf16[2,256,256]{2,1,0:T(8,128)(2,1)S(1)}, u32[]{:S(2)}, u32[]{:S(2)}) collective-permute-start(bf16[2,256,256]{2,1,0:T(8,128)(2,1)S(1)} %get-tuple-element.144), channel_id=1, source_target_pairs={{0,96},{8,104},{16,112},{24,120},{32,64},{40,72},{48,80},{56,88},{... | collective-permute-start | bytes 786440 | tf_op jit(solution)/shard_map/ppermute | solution.py:38
  83.7 1.8 %collective-permute-done.14.o3 = bf16[768,512]{1,0:T(8,128)(2,1)S(1)} collective-permute-done((bf16[768,512]{1,0:T(8,128)(2,1)S(1)}, bf16[768,512]{1,0:T(8,128)(2,1)S(1)}, u32[]{:S(2)}, u32[]{:S(2)}) %collective-permute-start.14) | collective-permute-done | bytes 786464 | tf_op jit(solution)/shard_map/ppermute | solution.py:38
  85.8 2.8 %collective-permute-start.17 = (bf16[512,512]{1,0:T(8,128)(2,1)S(1)}, bf16[512,512]{1,0:T(8,128)(2,1)S(1)}, u32[]{:S(2)}, u32[]{:S(2)}) collective-permute-start(bf16[512,512]{1,0:T(8,128)(2,1)S(1)} %cross.1), channel_id=1, source_target_pairs={{0,1},{1,0},{2,3},{3,2},{4,5},{5,4},{6,7},{7,6},{8,9},{9,8},{10,11... | collective-permute-start | bytes 1572872 | tf_op jit(solution)/shard_map/ppermute | solution.py:38
  88.7 2.3 %collective-permute-start.25 = (bf16[256,256]{1,0:T(8,128)(2,1)S(1)}, bf16[256,256]{1,0:T(8,128)(2,1)S(1)}, u32[]{:S(2)}, u32[]{:S(2)}) collective-permute-start(bf16[256,256]{1,0:T(8,128)(2,1)S(1)} %fusion), channel_id=1, source_target_pairs={{0,96},{8,104},{16,112},{24,120},{32,64},{40,72},{48,80},{56,88},{... | collective-permute-start | bytes 393224 | tf_op jit(solution)/shard_map/ppermute | solution.py:38
  92.4 2.5 %collective-permute-done.25.we_3 = bf16[256,256]{1,0:T(8,128)(2,1)S(1)} collective-permute-done((bf16[256,256]{1,0:T(8,128)(2,1)S(1)}, bf16[256,256]{1,0:T(8,128)(2,1)S(1)}, u32[]{:S(2)}, u32[]{:S(2)}) %collective-permute-start.25) | collective-permute-done | bytes 131104 | tf_op jit(solution)/shard_map/ppermute | solution.py:38
  96.0 2.0 %collective-permute-done.26.side_ref = bf16[512,512]{1,0:T(8,128)(2,1)S(1)} collective-permute-done((bf16[512,512]{1,0:T(8,128)(2,1)S(1)}, bf16[512,512]{1,0:T(8,128)(2,1)S(1)}, u32[]{:S(2)}, u32[]{:S(2)}) %collective-permute-start.26) | collective-permute-done | bytes 524320 | tf_op jit(solution)/shard_map/ppermute | solution.py:38
  100.0 1.8 %collective-permute-start.15 = (bf16[256,512]{1,0:T(8,128)(2,1)S(1)}, bf16[256,512]{1,0:T(8,128)(2,1)S(1)}, u32[]{:S(2)}, u32[]{:S(2)}) collective-permute-start(bf16[256,512]{1,0:T(8,128)(2,1)S(1)} %add_convert_fusion.1), channel_id=1, source_target_pairs={{0,2},{1,3},{2,0},{3,1},{4,6},{5,7},{6,4},{7,5},{8,10},{9,11},{10,... | collective-permute-start | bytes 786440 | tf_op jit(solution)/shard_map/ppermute | solution.py:38
  101.8 1.3 %weight_out.1 = bf16[512,256]{1,0:T(8,128)(2,1)} custom-call(s32[3]{0:T(128)S(1)} %pad_add_fusion.pos, f32[2,256,256]{2,1,0:T(8,128)S(1)} %get-tuple-element.156.keep, bf16[2,256,256]{2,1,0:T(8,128)(2,1)S(1)} %collective-permute-done.22.w1, bf16[2,256,256]{2,1,0:T(8,128)(2,1)S(1)} %collective-permute-done.23.w3, ...), custom_call_target="tpu_custom_call" | custom-call | bytes 1200000 | tf_op jit(solution)/shard_map/weight_out/pallas_call | solution.py:634
  103.1 5.2 %collective-permute-done.15.end_1 = bf16[256,512]{1,0:T(8,128)(2,1)S(1)} collective-permute-done((bf16[256,512]{1,0:T(8,128)(2,1)S(1)}, bf16[256,512]{1,0:T(8,128)(2,1)S(1)}, u32[]{:S(2)}, u32[]{:S(2)}) %collective-permute-start.15) | collective-permute-done | bytes 262176 | tf_op jit(solution)/shard_map/ppermute | solution.py:38
  109.4 1.8 %place.1 = (bf16[512,512]{1,0:T(8,128)(2,1)}, bf16[512,512]{1,0:T(8,128)(2,1)}, bf16[512,512]{1,0:T(8,128)(2,1)}) custom-call(s32[3]{0:T(128)S(1)} %pad_add_fusion.pos, bf16[512,256]{1,0:T(8,128)(2,1)S(1)} %get-tuple-element.134.q_own, bf16[512,512]{1,0:T(8,128)(2,1)S(1)} %get-tuple-element.150.kv_own, bf16[512,384]{1,0:T(8,128)(2,1)S(1)} %collective-permute-done.27.recv_k, ...), custom_call_target="tpu_custom_call" | custom-call | bytes 1200000 | tf_op jit(solution)/shard_map/place/pallas_call | solution.py:573
  (68 shorter events, 17.8 us)
Async XLA Ops:
  0.6 4.8 %collective-permute-start.2 = (bf16[512,512]{1,0:T(8,128)(2,1)}, bf16[512,512]{1,0:T(8,128)(2,1)S(1)}, u32[]{:S(2)}, u32[]{:S(2)}) collective-permute-start(bf16[512,512]{1,0:T(8,128)(2,1)} %q_ref.1), channel_id=1, source_target_pairs={{0,8},{8,0},{16,24},{24,16},{32,40},{40,32},{48,56},{56,48},{64,72... | collective-permute-start | bytes 1572872 | tf_op jit(solution)/shard_map/ppermute | solution.py:38
  0.7 4.7 %collective-permute-start = (bf16[512,512]{1,0:T(8,128)(2,1)}, bf16[512,512]{1,0:T(8,128)(2,1)S(1)}, u32[]{:S(2)}, u32[]{:S(2)}) collective-permute-start(bf16[512,512]{1,0:T(8,128)(2,1)} %k_ref.1), channel_id=1, source_target_pairs={{0,8},{8,0},{16,24},{24,16},{32,40},{40,32},{48,56},{56,48},{64,72... | collective-permute-start | bytes 1572872 | tf_op jit(solution)/shard_map/ppermute | solution.py:38
  1.2 4.2 %collective-permute-start.1 = (bf16[512,512]{1,0:T(8,128)(2,1)}, bf16[512,512]{1,0:T(8,128)(2,1)S(1)}, u32[]{:S(2)}, u32[]{:S(2)}) collective-permute-start(bf16[512,512]{1,0:T(8,128)(2,1)} %v_ref.1), channel_id=1, source_target_pairs={{0,8},{8,0},{16,24},{24,16},{32,40},{40,32},{48,56},{56,48},{64,72... | collective-permute-start | bytes 1572872 | tf_op jit(solution)/shard_map/ppermute | solution.py:38
  6.3 17.4 %collective-permute-start.6 = (bf16[512,512]{1,0:T(8,128)(2,1)S(1)}, bf16[512,512]{1,0:T(8,128)(2,1)S(1)}, u32[]{:S(2)}, u32[]{:S(2)}) collective-permute-start(bf16[512,512]{1,0:T(8,128)(2,1)S(1)} %get-tuple-element.84.l1_ref), channel_id=1, source_target_pairs={{0,16},{8,24},{16,0},{24,8},{32,48},{40,56},{48,32},{56,40},{64,80... | collective-permute-start | bytes 1572872 | tf_op jit(solution)/shard_map/ppermute | solution.py:38
  7.9 16.4 %copy-start = (bf16[512,4096]{1,0:T(8,128)(2,1)S(1)}, bf16[512,4096]{1,0:T(8,128)(2,1)}, u32[]{:S(2)}) copy-start(bf16[512,4096]{1,0:T(8,128)(2,1)} %w_other.3) | copy-start | bytes 12582916
  8.9 14.7 %collective-permute-start.3 = (bf16[256,512]{1,0:T(8,128)(2,1)S(1)}, bf16[256,512]{1,0:T(8,128)(2,1)S(1)}, u32[]{:S(2)}, u32[]{:S(2)}) collective-permute-start(bf16[256,512]{1,0:T(8,128)(2,1)S(1)} %get-tuple-element.87), channel_id=1, source_target_pairs={{0,32},{8,40},{16,48},{24,56},{32,0},{40,8},{48,16},{56,24},{64,96... | collective-permute-start | bytes 786440 | tf_op jit(solution)/shard_map/ppermute | solution.py:38
  11.0 12.7 %collective-permute-start.5 = (bf16[128,512]{1,0:T(8,128)(2,1)S(1)}, bf16[128,512]{1,0:T(8,128)(2,1)S(1)}, u32[]{:S(2)}, u32[]{:S(2)}) collective-permute-start(bf16[128,512]{1,0:T(8,128)(2,1)S(1)} %get-tuple-element.88), channel_id=1, source_target_pairs={{0,64},{8,72},{16,80},{24,88},{32,96},{40,104},{48,112},{56,120},{... | collective-permute-start | bytes 393224 | tf_op jit(solution)/shard_map/ppermute | solution.py:38
  14.5 9.1 %collective-permute-start.4 = (bf16[128,512]{1,0:T(8,128)(2,1)S(1)}, bf16[128,512]{1,0:T(8,128)(2,1)S(1)}, u32[]{:S(2)}, u32[]{:S(2)}) collective-permute-start(bf16[128,512]{1,0:T(8,128)(2,1)S(1)} %get-tuple-element.88), channel_id=1, source_target_pairs={{0,96},{8,104},{16,112},{24,120},{32,64},{40,72},{48,80},{56,88},{... | collective-permute-start | bytes 393224 | tf_op jit(solution)/shard_map/ppermute | solution.py:38
  23.7 13.2 %collective-permute-start.7 = (bf16[512,512]{1,0:T(8,128)(2,1)S(1)}, bf16[512,512]{1,0:T(8,128)(2,1)S(1)}, u32[]{:S(2)}, u32[]{:S(2)}) collective-permute-start(bf16[512,512]{1,0:T(8,128)(2,1)S(1)} %pad_maximum_fusion.2.refs_1_.refs_3_.refs_4_), channel_id=1, source_target_pairs={{0,16},{8,24},{16,0},{24,8},{32,48},{40,56},{48,32},{56,40},{64,80... | collective-permute-start | bytes 1572872 | tf_op jit(solution)/shard_map/ppermute | solution.py:38
  24.3 2.2 %copy-start.1 = (bf16[512,4096]{1,0:T(8,128)(2,1)S(1)}, bf16[512,4096]{1,0:T(8,128)(2,1)}, u32[]{:S(2)}) copy-start(bf16[512,4096]{1,0:T(8,128)(2,1)} %g_own.3) | copy-start | bytes 12582916
  37.0 5.3 %collective-permute-start.10 = (bf16[512,2048]{1,0:T(8,128)(2,1)S(1)}, bf16[512,2048]{1,0:T(8,128)(2,1)S(1)}, u32[]{:S(2)}, u32[]{:S(2)}) collective-permute-start(bf16[512,2048]{1,0:T(8,128)(2,1)S(1)} %get-tuple-element.106), channel_id=1, source_target_pairs={{0,8},{8,0},{16,24},{24,16},{32,40},{40,32},{48,56},{56,48},{64,72... | collective-permute-start | bytes 6291464 | tf_op jit(solution)/shard_map/ppermute | solution.py:38
  39.3 2.9 %collective-permute-start.8 = (bf16[256,1024]{1,0:T(8,128)(2,1)S(1)}, bf16[256,1024]{1,0:T(8,128)(2,1)S(1)}, u32[]{:S(2)}, u32[]{:S(2)}) collective-permute-start(bf16[256,1024]{1,0:T(8,128)(2,1)S(1)} %get-tuple-element.129.o_ref), channel_id=1, source_target_pairs={{0,8},{8,0},{16,24},{24,16},{32,40},{40,32},{48,56},{56,48},{64,72... | collective-permute-start | bytes 1572872 | tf_op jit(solution)/shard_map/ppermute | solution.py:38
  39.9 2.3 %collective-permute-start.9 = (bf16[256,512]{1,0:T(8,128)(2,1)S(1)}, bf16[256,512]{1,0:T(8,128)(2,1)S(1)}, u32[]{:S(2)}, u32[]{:S(2)}) collective-permute-start(bf16[256,512]{1,0:T(8,128)(2,1)S(1)} %get-tuple-element.105), channel_id=1, source_target_pairs={{0,8},{8,0},{16,24},{24,16},{32,40},{40,32},{48,56},{56,48},{64,72... | collective-permute-start | bytes 786440 | tf_op jit(solution)/shard_map/ppermute | solution.py:38
  42.3 6.2 %copy-start.2 = (bf16[512,4096]{1,0:T(8,128)(2,1)S(1)}, bf16[512,4096]{1,0:T(8,128)(2,1)}, u32[]{:S(2)}) copy-start(bf16[512,4096]{1,0:T(8,128)(2,1)} %g_own.3) | copy-start | bytes 12582916
  45.3 18.6 %collective-permute-start.11 = (bf16[512,512]{1,0:T(8,128)(2,1)S(1)}, bf16[512,512]{1,0:T(8,128)(2,1)S(1)}, u32[]{:S(2)}, u32[]{:S(2)}) collective-permute-start(bf16[512,512]{1,0:T(8,128)(2,1)S(1)} %get-tuple-element.120), channel_id=1, source_target_pairs={{0,6},{1,7},{2,4},{3,5},{4,2},{5,3},{6,0},{7,1},{8,14},{9,15},{10,... | collective-permute-start | bytes 1572872 | tf_op jit(solution)/shard_map/ppermute | solution.py:38
  48.4 15.7 %collective-permute-start.12 = (bf16[512,512]{1,0:T(8,128)(2,1)S(1)}, bf16[512,512]{1,0:T(8,128)(2,1)S(1)}, u32[]{:S(2)}, u32[]{:S(2)}) collective-permute-start(bf16[512,512]{1,0:T(8,128)(2,1)S(1)} %get-tuple-element.123), channel_id=1, source_target_pairs={{0,2},{1,3},{2,0},{3,1},{4,6},{5,7},{6,4},{7,5},{8,10},{9,11},{10,... | collective-permute-start | bytes 1572872 | tf_op jit(solution)/shard_map/ppermute | solution.py:38
  51.2 29.3 %collective-permute-start.21 = (bf16[4,2,256,256]{3,2,1,0:T(8,128)(2,1)S(1)}, bf16[4,2,256,256]{3,2,1,0:T(8,128)(2,1)S(1)}, u32[]{:S(2)}, u32[]{:S(2)}) collective-permute-start(bf16[4,2,256,256]{3,2,1,0:T(8,128)(2,1)S(1)} %weight_term.2), channel_id=1, source_target_pairs={{0,16},{8,24},{16,0},{24,8},{32,48},{40,56},{48,32},{56,40},{64,80... | collective-permute-start | bytes 3145736 | tf_op jit(solution)/shard_map/ppermute | solution.py:38
  58.6 8.9 %collective-permute-start.19 = (bf16[256,512]{1,0:T(8,128)(2,1)S(1)}, bf16[256,512]{1,0:T(8,128)(2,1)S(1)}, u32[]{:S(2)}, u32[]{:S(2)}) collective-permute-start(bf16[256,512]{1,0:T(8,128)(2,1)S(1)} %get-tuple-element.138), channel_id=1, source_target_pairs={{0,96},{8,104},{16,112},{24,120},{32,64},{40,72},{48,80},{56,88},{... | collective-permute-start | bytes 786440 | tf_op jit(solution)/shard_map/ppermute | solution.py:38
  60.9 15.4 %collective-permute-start.18 = (bf16[512,512]{1,0:T(8,128)(2,1)S(1)}, bf16[512,512]{1,0:T(8,128)(2,1)S(1)}, u32[]{:S(2)}, u32[]{:S(2)}) collective-permute-start(bf16[512,512]{1,0:T(8,128)(2,1)S(1)} %get-tuple-element.137), channel_id=1, source_target_pairs={{0,32},{8,40},{16,48},{24,56},{32,0},{40,8},{48,16},{56,24},{64,96... | collective-permute-start | bytes 1572872 | tf_op jit(solution)/shard_map/ppermute | solution.py:38
  64.2 19.5 %collective-permute-start.13 = (bf16[768,512]{1,0:T(8,128)(2,1)S(1)}, bf16[768,512]{1,0:T(8,128)(2,1)S(1)}, u32[]{:S(2)}, u32[]{:S(2)}) collective-permute-start(bf16[768,512]{1,0:T(8,128)(2,1)S(1)} %pad_maximum_fusion), channel_id=1, source_target_pairs={{0,2},{1,3},{2,0},{3,1},{4,6},{5,7},{6,4},{7,5},{8,10},{9,11},{10,... | collective-permute-start | bytes 2359304 | tf_op jit(solution)/shard_map/ppermute | solution.py:38
  66.2 19.4 %collective-permute-start.14 = (bf16[768,512]{1,0:T(8,128)(2,1)S(1)}, bf16[768,512]{1,0:T(8,128)(2,1)S(1)}, u32[]{:S(2)}, u32[]{:S(2)}) collective-permute-start(bf16[768,512]{1,0:T(8,128)(2,1)S(1)} %pad_maximum_fusion.1), channel_id=1, source_target_pairs={{0,6},{1,7},{2,4},{3,5},{4,2},{5,3},{6,0},{7,1},{8,14},{9,15},{10,... | collective-permute-start | bytes 2359304 | tf_op jit(solution)/shard_map/ppermute | solution.py:38
  67.6 12.4 %collective-permute-start.20 = (bf16[256,512]{1,0:T(8,128)(2,1)S(1)}, bf16[256,512]{1,0:T(8,128)(2,1)S(1)}, u32[]{:S(2)}, u32[]{:S(2)}) collective-permute-start(bf16[256,512]{1,0:T(8,128)(2,1)S(1)} %get-tuple-element.140), channel_id=1, source_target_pairs={{0,64},{8,72},{16,80},{24,88},{32,96},{40,104},{48,112},{56,120},{... | collective-permute-start | bytes 786440 | tf_op jit(solution)/shard_map/ppermute | solution.py:38
  80.8 7.8 %collective-permute-start.22 = (bf16[2,256,256]{2,1,0:T(8,128)(2,1)S(1)}, bf16[2,256,256]{2,1,0:T(8,128)(2,1)S(1)}, u32[]{:S(2)}, u32[]{:S(2)}) collective-permute-start(bf16[2,256,256]{2,1,0:T(8,128)(2,1)S(1)} %get-tuple-element.143), channel_id=1, source_target_pairs={{0,32},{8,40},{16,48},{24,56},{32,0},{40,8},{48,16},{56,24},{64,96... | collective-permute-start | bytes 786440 | tf_op jit(solution)/shard_map/ppermute | solution.py:38
  80.9 7.7 %collective-permute-start.23 = (bf16[2,256,256]{2,1,0:T(8,128)(2,1)S(1)}, bf16[2,256,256]{2,1,0:T(8,128)(2,1)S(1)}, u32[]{:S(2)}, u32[]{:S(2)}) collective-permute-start(bf16[2,256,256]{2,1,0:T(8,128)(2,1)S(1)} %get-tuple-element.144), channel_id=1, source_target_pairs={{0,96},{8,104},{16,112},{24,120},{32,64},{40,72},{48,80},{56,88},{... | collective-permute-start | bytes 786440 | tf_op jit(solution)/shard_map/ppermute | solution.py:38
  83.2 14.9 %collective-permute-start.26 = (bf16[512,512]{1,0:T(8,128)(2,1)S(1)}, bf16[512,512]{1,0:T(8,128)(2,1)S(1)}, u32[]{:S(2)}, u32[]{:S(2)}) collective-permute-start(bf16[512,512]{1,0:T(8,128)(2,1)S(1)} %relay.1), channel_id=1, source_target_pairs={{0,16},{8,24},{16,0},{24,8},{32,48},{40,56},{48,32},{56,40},{64,80... | collective-permute-start | bytes 1572872 | tf_op jit(solution)/shard_map/ppermute | solution.py:38
  85.8 22.6 %collective-permute-start.17 = (bf16[512,512]{1,0:T(8,128)(2,1)S(1)}, bf16[512,512]{1,0:T(8,128)(2,1)S(1)}, u32[]{:S(2)}, u32[]{:S(2)}) collective-permute-start(bf16[512,512]{1,0:T(8,128)(2,1)S(1)} %cross.1), channel_id=1, source_target_pairs={{0,1},{1,0},{2,3},{3,2},{4,5},{5,4},{6,7},{7,6},{8,9},{9,8},{10,11... | collective-permute-start | bytes 1572872 | tf_op jit(solution)/shard_map/ppermute | solution.py:38
  88.7 6.3 %collective-permute-start.25 = (bf16[256,256]{1,0:T(8,128)(2,1)S(1)}, bf16[256,256]{1,0:T(8,128)(2,1)S(1)}, u32[]{:S(2)}, u32[]{:S(2)}) collective-permute-start(bf16[256,256]{1,0:T(8,128)(2,1)S(1)} %fusion), channel_id=1, source_target_pairs={{0,96},{8,104},{16,112},{24,120},{32,64},{40,72},{48,80},{56,88},{... | collective-permute-start | bytes 393224 | tf_op jit(solution)/shard_map/ppermute | solution.py:38
  91.0 5.0 %collective-permute-start.24 = (bf16[256,256]{1,0:T(8,128)(2,1)S(1)}, bf16[256,256]{1,0:T(8,128)(2,1)S(1)}, u32[]{:S(2)}, u32[]{:S(2)}) collective-permute-start(bf16[256,256]{1,0:T(8,128)(2,1)S(1)} %fusion.1), channel_id=1, source_target_pairs={{0,32},{8,40},{16,48},{24,56},{32,0},{40,8},{48,16},{56,24},{64,96... | collective-permute-start | bytes 393224 | tf_op jit(solution)/shard_map/ppermute | solution.py:38
  91.3 11.8 %collective-permute-start.16 = (bf16[256,512]{1,0:T(8,128)(2,1)S(1)}, bf16[256,512]{1,0:T(8,128)(2,1)S(1)}, u32[]{:S(2)}, u32[]{:S(2)}) collective-permute-start(bf16[256,512]{1,0:T(8,128)(2,1)S(1)} %add_convert_fusion), channel_id=1, source_target_pairs={{0,6},{1,7},{2,4},{3,5},{4,2},{5,3},{6,0},{7,1},{8,14},{9,15},{10,... | collective-permute-start | bytes 786440 | tf_op jit(solution)/shard_map/ppermute | solution.py:38
  99.3 10.1 %collective-permute-start.27 = (bf16[512,384]{1,0:T(8,128)(2,1)S(1)}, bf16[512,384]{1,0:T(8,128)(2,1)S(1)}, u32[]{:S(2)}, u32[]{:S(2)}) collective-permute-start(bf16[512,384]{1,0:T(8,128)(2,1)S(1)} %get-tuple-element.151), channel_id=1, source_target_pairs={{0,8},{8,0},{16,24},{24,16},{32,40},{40,32},{48,56},{56,48},{64,72... | collective-permute-start | bytes 1179656 | tf_op jit(solution)/shard_map/ppermute | solution.py:38
  99.4 10.0 %collective-permute-start.28 = (bf16[512,384]{1,0:T(8,128)(2,1)S(1)}, bf16[512,384]{1,0:T(8,128)(2,1)S(1)}, u32[]{:S(2)}, u32[]{:S(2)}) collective-permute-start(bf16[512,384]{1,0:T(8,128)(2,1)S(1)} %get-tuple-element.152), channel_id=1, source_target_pairs={{0,8},{8,0},{16,24},{24,16},{32,40},{40,32},{48,56},{56,48},{64,72... | collective-permute-start | bytes 1179656 | tf_op jit(solution)/shard_map/ppermute | solution.py:38
  100.0 8.4 %collective-permute-start.15 = (bf16[256,512]{1,0:T(8,128)(2,1)S(1)}, bf16[256,512]{1,0:T(8,128)(2,1)S(1)}, u32[]{:S(2)}, u32[]{:S(2)}) collective-permute-start(bf16[256,512]{1,0:T(8,128)(2,1)S(1)} %add_convert_fusion.1), channel_id=1, source_target_pairs={{0,2},{1,3},{2,0},{3,1},{4,6},{5,7},{6,4},{7,5},{8,10},{9,11},{10,... | collective-permute-start | bytes 786440 | tf_op jit(solution)/shard_map/ppermute | solution.py:38
  (3 other events, 3.1 us)

commit v3 on v2

--- a/solution.py
+++ b/solution.py
@@ -332,6 +332,79 @@
         compiler_params=params(),
         cost_estimate=cost(3.0),
         name="project",
+    )(pos, attn, attn_other, out_weight, out_weight)
+
+
+def project_away_kernel(
+    pos, o_ref, r_ref, w_mine, w_other, first_1, first_3, late_1, late_3, mine, other
+):
+    step = pl.program_id(0) + 1
+
+    @pl.when(step == 1)
+    def _():
+        mine[...] = o_ref[:, :512].T
+        other[...] = r_ref[:, 512:].T
+
+    out = (mm(mine[...], w_mine[...], NN) + mm(other[...], w_other[...], NN)).astype(BF)
+    top, low = out[:256], out[256:]
+
+    @pl.when(step == 1)
+    def _():
+        first_1[256:] = top
+        late_1[...] = low
+
+    @pl.when(step == 2)
+    def _():
+        first_1[:256] = top
+        first_3[:256] = low
+
+    @pl.when(step == 3)
+    def _():
+        first_3[256:] = low
+        late_3[...] = top
+
+
+def project_away_call(pos, attn, attn_other, out_weight, dx):
+    def weight(flip):
+        return pl.BlockSpec((256, 512), lambda i, pos: (pos[0] ^ flip, pos[1] ^ (i * 2 + 2 + dx)))
+
+    return pl.pallas_call(
+        project_away_kernel,
+        grid_spec=pltpu.PrefetchScalarGridSpec(
+            num_scalar_prefetch=1,
+            grid=(3,),
+            in_specs=[whole(256, 1024), whole(256, 1024), weight(0), weight(1)],
+            out_specs=[whole(512, 512)] * 2 + [whole(256, 512)] * 2,
+            scratch_shapes=[pltpu.VMEM((512, 256), BF), pltpu.VMEM((512, 256), BF)],
+        ),
+        out_shape=[shape((512, 512))] * 2 + [shape((256, 512))] * 2,
+        compiler_params=params(),
+        cost_estimate=cost(3.0),
+        name="project_away",
+    )(pos, attn, attn_other, out_weight, out_weight)
+
+
+def project_keep_kernel(pos, o_ref, r_ref, w_mine, w_other, keep):
+    out = mm(o_ref[:, :512], w_mine[...], TN) + mm(r_ref[:, 512:], w_other[...], TN)
+    keep[...] = out.astype(BF)
+
+
+def project_keep_call(pos, attn, attn_other, out_weight, dx):
+    def weight(flip):
+        return pl.BlockSpec((256, 512), lambda i, pos: (pos[0] ^ flip, pos[1] ^ dx))
+
+    return pl.pallas_call(
+        project_keep_kernel,
+        grid_spec=pltpu.PrefetchScalarGridSpec(
+            num_scalar_prefetch=1,
+            grid=(1,),
+            in_specs=[whole(256, 1024), whole(256, 1024), weight(0), weight(1)],
+            out_specs=whole(512, 512),
+        ),
+        out_shape=shape((512, 512)),
+        compiler_params=params(),
+        cost_estimate=cost(1.0),
+        name="project_keep",
     )(pos, attn, attn_other, out_weight, out_weight)
 
 
@@ -687,12 +760,12 @@
     far = (side, level, cross_level)
 
     attn_other = after(swap(attn, "ctx", 1), da_recv, grad_recv)
-    keep_c, first_c1, first_c3, late_c1, late_c3 = project_call(
+    first_c1, first_c3, late_c1, late_c3 = project_away_call(
         pos, attn, attn_other, out_weight, 1
     )
     got_c1, got_c3 = swap(first_c1, "head", 2), swap(first_c3, "head", 6)
 
-    attn_v, other_v = after((attn, attn_other), keep_c)
+    attn_v, other_v = after((attn, attn_other), first_c1)
     w_cross = weight_call(pos, attn_v, other_v, output_grad, grad_recv, 1)
     w_recv = swap(w_cross, "ctx", 2)
 
@@ -718,7 +791,9 @@
         qt_n, da_n, da_recv, attn, scales, e_near, kv_own, kv_sib, dq
     )
 
-    relayed = relay_call(after(side_grad, send_1, send_3, kv_grad), *back)
+    attn_k, other_k = after((attn, attn_other), kv_grad)
+    keep_c = project_keep_call(pos, attn_k, other_k, out_weight, 1)
+    relayed = relay_call(after(side_grad, send_1, send_3, keep_c), *back)
     side_back = swap(relayed, "ctx", 2)
     keep_w, first_w1, first_w3, late_w1, late_w3 = plain_call(
         weight_sum_kernel,

time: 112 us -> 111 us (level)
  waiting for transfers between devices: 26.3 us -> 25.1 us
    pallas_call x0 -> x2, Pallas kernels: none -> 3.46 us  [the longest x1 2.43 us: project_away_call(): pl.pallas_call(project_away_kernel, grid_spec=pltpu.PrefetchScalarGridSpe...]
    pallas_call x2 -> x1, Pallas kernels: 5.99 us -> 2.99 us  [project_call(): pl.pallas_call(project_kernel, grid_spec=pltpu.PrefetchScalarGridSpec(num...]
  transfers between devices with their start and end apart: 29 -> 29, of which waited for: 11 -> 11; matrix products, arithmetic and copies ran while one was open for 0% -> 0% of each run, Pallas kernels for 38% -> 39%
where the time goes in v3:
time: 111 us
  Pallas kernels  47.9 us (43%)
  starting transfers between devices  30.8 us (28%)
  waiting for transfers between devices  25.1 us (23%)
  local copies, waits for them, and re-layouts  5.32 us (5%)
    ppermute x29, starting transfers between devices, swap(): return lax.ppermute(value, axis, [(i, i ^ mask) for i in range(size)])  30.8 us
    ppermute x29, waiting for transfers between devices, swap(): return lax.ppermute(value, axis, [(i, i ^ mask) for i in range(size)])  25.1 us
    pallas_call x3, Pallas kernels, score_call(): pl.pallas_call(kernel, grid=(2,), in_specs=[per_head(128, 1024), *kv_spec...  11 us
    pallas_call x1, Pallas kernels, far_grad_call(): pl.pallas_call(far_grad_kernel, grid=(2,), in_specs=[*common_specs(), per...  6.6 us
    pallas_call x2, Pallas kernels, weight_call(): pl.pallas_call(weight_kernel, grid_spec=pltpu.PrefetchScalarGridSpec(num_...  5.43 us
    unnamed x12, local copies, waits for them, and re-layouts  5.32 us
    pallas_call x1, Pallas kernels, near_grad_call(): pl.pallas_call(near_grad_kernel, grid=(2,), in_specs=[*common_specs(), pl...  4.77 us
    pallas_call x1, Pallas kernels, grad_attention_call(): pl.pallas_call(grad_attention_kernel, grid_spec=pltpu.PrefetchScalarGridS...  4.53 us
  transfers between devices with their start and end apart: 29, of which 11 were waited for; matrix products, arithmetic and copies ran while one was open for 0% of the time, Pallas kernels for 39%

profile of v3, /device:TPU:0, one launch (start us, length us, event | category | flops | bytes accessed | tf_op | source)
XLA Modules:
  0.0 110.7 jit_solution(8517050410646624190)
XLA Ops:
  6.3 1.6 %collective-permute-start.6 = (bf16[512,512]{1,0:T(8,128)(2,1)S(1)}, bf16[512,512]{1,0:T(8,128)(2,1)S(1)}, u32[]{:S(2)}, u32[]{:S(2)}) collective-permute-start(bf16[512,512]{1,0:T(8,128)(2,1)S(1)} %get-tuple-element.85.l1_ref), channel_id=1, source_target_pairs={{0,16},{8,24},{16,0},{24,8},{32,48},{40,56},{48,32},{56,40},{64,80... | collective-permute-start | bytes 1572872 | tf_op jit(solution)/shard_map/ppermute | solution.py:38
  8.9 2.0 %collective-permute-start.3 = (bf16[256,512]{1,0:T(8,128)(2,1)S(1)}, bf16[256,512]{1,0:T(8,128)(2,1)S(1)}, u32[]{:S(2)}, u32[]{:S(2)}) collective-permute-start(bf16[256,512]{1,0:T(8,128)(2,1)S(1)} %get-tuple-element.88), channel_id=1, source_target_pairs={{0,32},{8,40},{16,48},{24,56},{32,0},{40,8},{48,16},{56,24},{64,96... | collective-permute-start | bytes 786440 | tf_op jit(solution)/shard_map/ppermute | solution.py:38
  11.0 3.6 %collective-permute-start.5 = (bf16[128,512]{1,0:T(8,128)(2,1)S(1)}, bf16[128,512]{1,0:T(8,128)(2,1)S(1)}, u32[]{:S(2)}, u32[]{:S(2)}) collective-permute-start(bf16[128,512]{1,0:T(8,128)(2,1)S(1)} %get-tuple-element.89), channel_id=1, source_target_pairs={{0,64},{8,72},{16,80},{24,88},{32,96},{40,104},{48,112},{56,120},{... | collective-permute-start | bytes 393224 | tf_op jit(solution)/shard_map/ppermute | solution.py:38
  14.5 4.2 %near_scores.1 = (bf16[2,2,512,1024]{3,2,1,0:T(8,128)(2,1)S(1)}, f32[256,1024]{1,0:T(8,128)S(1)}, f32[2,8,1024]{2,1,0:T(8,128)S(1)}) custom-call(bf16[256,1024]{1,0:T(8,128)(2,1)S(1)} %get-tuple-element.131.qt_ref, bf16[512,512]{1,0:T(8,128)(2,1)S(1)} %get-tuple-element.90.refs_0_.refs_2_.k_own.v_own, ...), custom_call_target="tpu_custom_call" | custom-call | bytes 5040000 | tf_op jit(solution)/shard_map/near_scores/pallas_call | solution.py:269
  18.8 4.9 %collective-permute-done.5 = bf16[128,512]{1,0:T(8,128)(2,1)S(1)} collective-permute-done((bf16[128,512]{1,0:T(8,128)(2,1)S(1)}, bf16[128,512]{1,0:T(8,128)(2,1)S(1)}, u32[]{:S(2)}, u32[]{:S(2)}) %collective-permute-start.5) | collective-permute-done | bytes 131104 | tf_op jit(solution)/shard_map/ppermute | solution.py:38
  24.3 2.2 %copy-done.1 = bf16[512,4096]{1,0:T(8,128)(2,1)S(1)} copy-done((bf16[512,4096]{1,0:T(8,128)(2,1)S(1)}, bf16[512,4096]{1,0:T(8,128)(2,1)}, u32[]{:S(2)}) %copy-start.1) | copy-done | bytes 4194328
  26.5 4.5 %grad_attention.1 = (bf16[256,512]{1,0:T(8,128)(2,1)S(1)}, bf16[256,512]{1,0:T(8,128)(2,1)S(1)}, bf16[512,2048]{1,0:T(8,128)(2,1)S(1)}) custom-call(s32[3]{0:T(128)S(1)} %pad_add_fusion.pos, bf16[512,4096]{1,0:T(8,128)(2,1)S(1)} %copy-done, bf16[512,4096]{1,0:T(8,128)(2,1)S(1)} %copy-done.1), custom_call_target="tpu_custom_call" | custom-call | bytes 5400000 | tf_op jit(solution)/shard_map/grad_attention/pallas_call | solution.py:67
  31.1 4.4 %middle_scores.1 = (bf16[2,2,512,1024]{3,2,1,0:T(8,128)(2,1)S(1)}, f32[256,1024]{1,0:T(8,128)S(1)}, f32[2,8,1024]{2,1,0:T(8,128)S(1)}) custom-call(bf16[256,1024]{1,0:T(8,128)(2,1)S(1)} %get-tuple-element.131.qt_ref, bf16[512,512]{1,0:T(8,128)(2,1)S(1)} %collective-permute-done.6.refs_0_.refs_2_.refs_3_, ...), custom_call_target="tpu_custom_call" | custom-call | bytes 5040000 | tf_op jit(solution)/shard_map/middle_scores/pallas_call | solution.py:269
  35.5 1.5 %collective-permute-done.7.key.value.refs_2_.refs_5_ = bf16[512,512]{1,0:T(8,128)(2,1)S(1)} collective-permute-done((bf16[512,512]{1,0:T(8,128)(2,1)S(1)}, bf16[512,512]{1,0:T(8,128)(2,1)S(1)}, u32[]{:S(2)}, u32[]{:S(2)}) %collective-permute-start.7) | collective-permute-done | bytes 524320 | tf_op jit(solution)/shard_map/ppermute | solution.py:38
  37.0 2.4 %last_scores.1 = (bf16[2,1,512,1024]{3,2,1,0:T(8,128)(2,1)S(1)}, bf16[256,1024]{1,0:T(8,128)(2,1)S(1)}, f32[2,8,1024]{2,1,0:T(8,128)S(1)}) custom-call(bf16[256,1024]{1,0:T(8,128)(2,1)S(1)} %get-tuple-element.131.qt_ref, bf16[512,512]{1,0:T(8,128)(2,1)S(1)} %collective-permute-done.7.key.value.refs_2_.refs_5_, ...), custom_call_target="tpu_custom_call" | custom-call | bytes 2640000 | tf_op jit(solution)/shard_map/last_scores/pallas_call | solution.py:269
  40.0 2.2 %collective-permute-done.9.da_recv = bf16[256,512]{1,0:T(8,128)(2,1)S(1)} collective-permute-done((bf16[256,512]{1,0:T(8,128)(2,1)S(1)}, bf16[256,512]{1,0:T(8,128)(2,1)S(1)}, u32[]{:S(2)}, u32[]{:S(2)}) %collective-permute-start.9) | collective-permute-done | bytes 262176 | tf_op jit(solution)/shard_map/ppermute | solution.py:38
  42.3 2.4 %project_away.1 = (bf16[512,512]{1,0:T(8,128)(2,1)S(1)}, bf16[512,512]{1,0:T(8,128)(2,1)S(1)}, bf16[256,512]{1,0:T(8,128)(2,1)S(1)}, bf16[256,512]{1,0:T(8,128)(2,1)S(1)}) custom-call(s32[3]{0:T(128)S(1)} %pad_add_fusion.pos, bf16[256,1024]{1,0:T(8,128)(2,1)S(1)} %get-tuple-element.135.o_ref, bf16[256,1024]{1,0:T(8,128)(2,1)S(1)} %collective-permute-done.8.r_ref, ...), custom_call_target="tpu_custom_call" | custom-call | bytes 3600000 | tf_op jit(solution)/shard_map/project_away/pallas_call | solution.py:371
  44.7 3.1 %collective-permute-start.11 = (bf16[512,512]{1,0:T(8,128)(2,1)S(1)}, bf16[512,512]{1,0:T(8,128)(2,1)S(1)}, u32[]{:S(2)}, u32[]{:S(2)}) collective-permute-start(bf16[512,512]{1,0:T(8,128)(2,1)S(1)} %get-tuple-element.121), channel_id=1, source_target_pairs={{0,6},{1,7},{2,4},{3,5},{4,2},{5,3},{6,0},{7,1},{8,14},{9,15},{10,... | collective-permute-start | bytes 1572872 | tf_op jit(solution)/shard_map/ppermute | solution.py:38
  47.9 2.7 %weight_term.2 = bf16[4,2,256,256]{3,2,1,0:T(8,128)(2,1)S(1)} custom-call(s32[3]{0:T(128)S(1)} %pad_add_fusion.pos, bf16[256,1024]{1,0:T(8,128)(2,1)S(1)} %get-tuple-element.135.o_ref, bf16[256,1024]{1,0:T(8,128)(2,1)S(1)} %collective-permute-done.8.r_ref, bf16[512,4096]{1,0:T(8,128)(2,1)S(1)} %copy-done.2, bf16[512,2048]{1,0:T(8,128)(2,1)S(1)} %collective-permute-done.10.g_recv), custom_call_target="tpu_custom_call" | custom-call | bytes 3000000 | tf_op jit(solution)/shard_map/weight_term/pallas_call | solution.py:418
  51.5 6.6 %far_grads.1 = (bf16[512,512]{1,0:T(8,128)(2,1)S(1)}, bf16[512,512]{1,0:T(8,128)(2,1)S(1)}, bf16[256,512]{1,0:T(8,128)(2,1)S(1)}, bf16[256,512]{1,0:T(8,128)(2,1)S(1)}, f32[256,1024]{1,0:T(8,128)S(1)}) custom-call(bf16[256,1024]{1,0:T(8,128)(2,1)S(1)} %get-tuple-element.131.qt_ref, bf16[256,512]{1,0:T(8,128)(2,1)S(1)} %get-tuple-element.132.da_own, ...), custom_call_target="tpu_custom_call" | custom-call | bytes 8040000 | tf_op jit(solution)/shard_map/far_grads/pallas_call | solution.py:506
  58.1 2.3 %collective-permute-start.19 = (bf16[256,512]{1,0:T(8,128)(2,1)S(1)}, bf16[256,512]{1,0:T(8,128)(2,1)S(1)}, u32[]{:S(2)}, u32[]{:S(2)}) collective-permute-start(bf16[256,512]{1,0:T(8,128)(2,1)S(1)} %get-tuple-element.140), channel_id=1, source_target_pairs={{0,96},{8,104},{16,112},{24,120},{32,64},{40,72},{48,80},{56,88},{... | collective-permute-start | bytes 786440 | tf_op jit(solution)/shard_map/ppermute | solution.py:38
  60.4 3.0 %project.1 = (bf16[512,512]{1,0:T(8,128)(2,1)S(1)}, bf16[512,512]{1,0:T(8,128)(2,1)S(1)}, bf16[512,512]{1,0:T(8,128)(2,1)S(1)}, bf16[256,512]{1,0:T(8,128)(2,1)S(1)}, bf16[256,512]{1,0:T(8,128)(2,1)S(1)}) custom-call(s32[3]{0:T(128)S(1)} %pad_add_fusion.pos, bf16[256,1024]{1,0:T(8,128)(2,1)S(1)} %get-tuple-element.135.o_ref, ...), custom_call_target="tpu_custom_call" | custom-call | bytes 3600000 | tf_op jit(solution)/shard_map/project/pallas_call | solution.py:322
  63.6 2.0 %collective-permute-start.13 = (bf16[768,512]{1,0:T(8,128)(2,1)S(1)}, bf16[768,512]{1,0:T(8,128)(2,1)S(1)}, u32[]{:S(2)}, u32[]{:S(2)}) collective-permute-start(bf16[768,512]{1,0:T(8,128)(2,1)S(1)} %pad_maximum_fusion), channel_id=1, source_target_pairs={{0,2},{1,3},{2,0},{3,1},{4,6},{5,7},{6,4},{7,5},{8,10},{9,11},{10,... | collective-permute-start | bytes 2359304 | tf_op jit(solution)/shard_map/ppermute | solution.py:38
  67.0 1.3 %collective-permute-start.20 = (bf16[256,512]{1,0:T(8,128)(2,1)S(1)}, bf16[256,512]{1,0:T(8,128)(2,1)S(1)}, u32[]{:S(2)}, u32[]{:S(2)}) collective-permute-start(bf16[256,512]{1,0:T(8,128)(2,1)S(1)} %get-tuple-element.142), channel_id=1, source_target_pairs={{0,64},{8,72},{16,80},{24,88},{32,96},{40,104},{48,112},{56,120},{... | collective-permute-start | bytes 786440 | tf_op jit(solution)/shard_map/ppermute | solution.py:38
  68.3 2.7 %weight_term.3.own = bf16[4,2,256,256]{3,2,1,0:T(8,128)(2,1)S(1)} custom-call(s32[3]{0:T(128)S(1)} %pad_add_fusion.pos, bf16[256,1024]{1,0:T(8,128)(2,1)S(1)} %get-tuple-element.135.o_ref, bf16[256,1024]{1,0:T(8,128)(2,1)S(1)} %collective-permute-done.8.r_ref, bf16[512,4096]{1,0:T(8,128)(2,1)S(1)} %copy-done.2, ...), custom_call_target="tpu_custom_call" | custom-call | bytes 3000000 | tf_op jit(solution)/shard_map/weight_term/pallas_call | solution.py:418
  71.0 4.8 %near_grads.1 = (f32[1024,512]{1,0:T(8,128)S(1)}, bf16[512,256]{1,0:T(8,128)(2,1)S(1)}, bf16[512,256]{1,0:T(8,128)(2,1)S(1)}) custom-call(bf16[256,1024]{1,0:T(8,128)(2,1)S(1)} %get-tuple-element.131.qt_ref, bf16[256,512]{1,0:T(8,128)(2,1)S(1)} %get-tuple-element.132.da_own, bf16[256,512]{1,0:T(8,128)(2,1)S(1)} %collective-permute-done.9.da_recv, ...), custom_call_target="tpu_custom_call" | custom-call | bytes 5760000 | tf_op jit(solution)/shard_map/near_grads/pallas_call | solution.py:563
  76.8 2.6 %collective-permute-done.20.z2_ref = bf16[256,512]{1,0:T(8,128)(2,1)S(1)} collective-permute-done((bf16[256,512]{1,0:T(8,128)(2,1)S(1)}, bf16[256,512]{1,0:T(8,128)(2,1)S(1)}, u32[]{:S(2)}, u32[]{:S(2)}) %collective-permute-start.20) | collective-permute-done | bytes 262176 | tf_op jit(solution)/shard_map/ppermute | solution.py:38
  80.3 2.3 %collective-permute-start.23 = (bf16[2,256,256]{2,1,0:T(8,128)(2,1)S(1)}, bf16[2,256,256]{2,1,0:T(8,128)(2,1)S(1)}, u32[]{:S(2)}, u32[]{:S(2)}) collective-permute-start(bf16[2,256,256]{2,1,0:T(8,128)(2,1)S(1)} %get-tuple-element.146), channel_id=1, source_target_pairs={{0,96},{8,104},{16,112},{24,120},{32,64},{40,72},{48,80},{56,88},{... | collective-permute-start | bytes 786440 | tf_op jit(solution)/shard_map/ppermute | solution.py:38
  83.2 1.8 %collective-permute-done.14.o3 = bf16[768,512]{1,0:T(8,128)(2,1)S(1)} collective-permute-done((bf16[768,512]{1,0:T(8,128)(2,1)S(1)}, bf16[768,512]{1,0:T(8,128)(2,1)S(1)}, u32[]{:S(2)}, u32[]{:S(2)}) %collective-permute-start.14) | collective-permute-done | bytes 786464 | tf_op jit(solution)/shard_map/ppermute | solution.py:38
  85.2 2.8 %collective-permute-start.17 = (bf16[512,512]{1,0:T(8,128)(2,1)S(1)}, bf16[512,512]{1,0:T(8,128)(2,1)S(1)}, u32[]{:S(2)}, u32[]{:S(2)}) collective-permute-start(bf16[512,512]{1,0:T(8,128)(2,1)S(1)} %cross.1), channel_id=1, source_target_pairs={{0,1},{1,0},{2,3},{3,2},{4,5},{5,4},{6,7},{7,6},{8,9},{9,8},{10,11... | collective-permute-start | bytes 1572872 | tf_op jit(solution)/shard_map/ppermute | solution.py:38
  88.1 2.3 %collective-permute-start.25 = (bf16[256,256]{1,0:T(8,128)(2,1)S(1)}, bf16[256,256]{1,0:T(8,128)(2,1)S(1)}, u32[]{:S(2)}, u32[]{:S(2)}) collective-permute-start(bf16[256,256]{1,0:T(8,128)(2,1)S(1)} %fusion), channel_id=1, source_target_pairs={{0,96},{8,104},{16,112},{24,120},{32,64},{40,72},{48,80},{56,88},{... | collective-permute-start | bytes 393224 | tf_op jit(solution)/shard_map/ppermute | solution.py:38
  91.9 2.5 %collective-permute-done.25.we_3 = bf16[256,256]{1,0:T(8,128)(2,1)S(1)} collective-permute-done((bf16[256,256]{1,0:T(8,128)(2,1)S(1)}, bf16[256,256]{1,0:T(8,128)(2,1)S(1)}, u32[]{:S(2)}, u32[]{:S(2)}) %collective-permute-start.25) | collective-permute-done | bytes 131104 | tf_op jit(solution)/shard_map/ppermute | solution.py:38
  95.5 2.0 %collective-permute-done.26.side_ref = bf16[512,512]{1,0:T(8,128)(2,1)S(1)} collective-permute-done((bf16[512,512]{1,0:T(8,128)(2,1)S(1)}, bf16[512,512]{1,0:T(8,128)(2,1)S(1)}, u32[]{:S(2)}, u32[]{:S(2)}) %collective-permute-start.26) | collective-permute-done | bytes 524320 | tf_op jit(solution)/shard_map/ppermute | solution.py:38
  99.4 1.8 %collective-permute-start.15 = (bf16[256,512]{1,0:T(8,128)(2,1)S(1)}, bf16[256,512]{1,0:T(8,128)(2,1)S(1)}, u32[]{:S(2)}, u32[]{:S(2)}) collective-permute-start(bf16[256,512]{1,0:T(8,128)(2,1)S(1)} %add_convert_fusion.1), channel_id=1, source_target_pairs={{0,2},{1,3},{2,0},{3,1},{4,6},{5,7},{6,4},{7,5},{8,10},{9,11},{10,... | collective-permute-start | bytes 786440 | tf_op jit(solution)/shard_map/ppermute | solution.py:38
  101.2 1.3 %weight_out.1 = bf16[512,256]{1,0:T(8,128)(2,1)} custom-call(s32[3]{0:T(128)S(1)} %pad_add_fusion.pos, f32[2,256,256]{2,1,0:T(8,128)S(1)} %get-tuple-element.158.keep, bf16[2,256,256]{2,1,0:T(8,128)(2,1)S(1)} %collective-permute-done.22.w1, bf16[2,256,256]{2,1,0:T(8,128)(2,1)S(1)} %collective-permute-done.23.w3, ...), custom_call_target="tpu_custom_call" | custom-call | bytes 1200000 | tf_op jit(solution)/shard_map/weight_out/pallas_call | solution.py:707
  102.6 5.2 %collective-permute-done.15.end_1 = bf16[256,512]{1,0:T(8,128)(2,1)S(1)} collective-permute-done((bf16[256,512]{1,0:T(8,128)(2,1)S(1)}, bf16[256,512]{1,0:T(8,128)(2,1)S(1)}, u32[]{:S(2)}, u32[]{:S(2)}) %collective-permute-start.15) | collective-permute-done | bytes 262176 | tf_op jit(solution)/shard_map/ppermute | solution.py:38
  108.9 1.8 %place.1 = (bf16[512,512]{1,0:T(8,128)(2,1)}, bf16[512,512]{1,0:T(8,128)(2,1)}, bf16[512,512]{1,0:T(8,128)(2,1)}) custom-call(s32[3]{0:T(128)S(1)} %pad_add_fusion.pos, bf16[512,256]{1,0:T(8,128)(2,1)S(1)} %get-tuple-element.137.q_own, bf16[512,512]{1,0:T(8,128)(2,1)S(1)} %get-tuple-element.152.kv_own, bf16[512,384]{1,0:T(8,128)(2,1)S(1)} %collective-permute-done.27.recv_k, ...), custom_call_target="tpu_custom_call" | custom-call | bytes 1200000 | tf_op jit(solution)/shard_map/place/pallas_call | solution.py:646
  (69 shorter events, 18.9 us)
Async XLA Ops:
  0.6 4.8 %collective-permute-start.2 = (bf16[512,512]{1,0:T(8,128)(2,1)}, bf16[512,512]{1,0:T(8,128)(2,1)S(1)}, u32[]{:S(2)}, u32[]{:S(2)}) collective-permute-start(bf16[512,512]{1,0:T(8,128)(2,1)} %q_ref.1), channel_id=1, source_target_pairs={{0,8},{8,0},{16,24},{24,16},{32,40},{40,32},{48,56},{56,48},{64,72... | collective-permute-start | bytes 1572872 | tf_op jit(solution)/shard_map/ppermute | solution.py:38
  0.7 4.7 %collective-permute-start = (bf16[512,512]{1,0:T(8,128)(2,1)}, bf16[512,512]{1,0:T(8,128)(2,1)S(1)}, u32[]{:S(2)}, u32[]{:S(2)}) collective-permute-start(bf16[512,512]{1,0:T(8,128)(2,1)} %k_ref.1), channel_id=1, source_target_pairs={{0,8},{8,0},{16,24},{24,16},{32,40},{40,32},{48,56},{56,48},{64,72... | collective-permute-start | bytes 1572872 | tf_op jit(solution)/shard_map/ppermute | solution.py:38
  1.2 4.2 %collective-permute-start.1 = (bf16[512,512]{1,0:T(8,128)(2,1)}, bf16[512,512]{1,0:T(8,128)(2,1)S(1)}, u32[]{:S(2)}, u32[]{:S(2)}) collective-permute-start(bf16[512,512]{1,0:T(8,128)(2,1)} %v_ref.1), channel_id=1, source_target_pairs={{0,8},{8,0},{16,24},{24,16},{32,40},{40,32},{48,56},{56,48},{64,72... | collective-permute-start | bytes 1572872 | tf_op jit(solution)/shard_map/ppermute | solution.py:38
  6.3 17.4 %collective-permute-start.6 = (bf16[512,512]{1,0:T(8,128)(2,1)S(1)}, bf16[512,512]{1,0:T(8,128)(2,1)S(1)}, u32[]{:S(2)}, u32[]{:S(2)}) collective-permute-start(bf16[512,512]{1,0:T(8,128)(2,1)S(1)} %get-tuple-element.85.l1_ref), channel_id=1, source_target_pairs={{0,16},{8,24},{16,0},{24,8},{32,48},{40,56},{48,32},{56,40},{64,80... | collective-permute-start | bytes 1572872 | tf_op jit(solution)/shard_map/ppermute | solution.py:38
  7.9 16.4 %copy-start = (bf16[512,4096]{1,0:T(8,128)(2,1)S(1)}, bf16[512,4096]{1,0:T(8,128)(2,1)}, u32[]{:S(2)}) copy-start(bf16[512,4096]{1,0:T(8,128)(2,1)} %w_other.5) | copy-start | bytes 12582916
  8.9 14.7 %collective-permute-start.3 = (bf16[256,512]{1,0:T(8,128)(2,1)S(1)}, bf16[256,512]{1,0:T(8,128)(2,1)S(1)}, u32[]{:S(2)}, u32[]{:S(2)}) collective-permute-start(bf16[256,512]{1,0:T(8,128)(2,1)S(1)} %get-tuple-element.88), channel_id=1, source_target_pairs={{0,32},{8,40},{16,48},{24,56},{32,0},{40,8},{48,16},{56,24},{64,96... | collective-permute-start | bytes 786440 | tf_op jit(solution)/shard_map/ppermute | solution.py:38
  11.0 12.7 %collective-permute-start.5 = (bf16[128,512]{1,0:T(8,128)(2,1)S(1)}, bf16[128,512]{1,0:T(8,128)(2,1)S(1)}, u32[]{:S(2)}, u32[]{:S(2)}) collective-permute-start(bf16[128,512]{1,0:T(8,128)(2,1)S(1)} %get-tuple-element.89), channel_id=1, source_target_pairs={{0,64},{8,72},{16,80},{24,88},{32,96},{40,104},{48,112},{56,120},{... | collective-permute-start | bytes 393224 | tf_op jit(solution)/shard_map/ppermute | solution.py:38
  14.5 9.1 %collective-permute-start.4 = (bf16[128,512]{1,0:T(8,128)(2,1)S(1)}, bf16[128,512]{1,0:T(8,128)(2,1)S(1)}, u32[]{:S(2)}, u32[]{:S(2)}) collective-permute-start(bf16[128,512]{1,0:T(8,128)(2,1)S(1)} %get-tuple-element.89), channel_id=1, source_target_pairs={{0,96},{8,104},{16,112},{24,120},{32,64},{40,72},{48,80},{56,88},{... | collective-permute-start | bytes 393224 | tf_op jit(solution)/shard_map/ppermute | solution.py:38
  23.7 13.2 %collective-permute-start.7 = (bf16[512,512]{1,0:T(8,128)(2,1)S(1)}, bf16[512,512]{1,0:T(8,128)(2,1)S(1)}, u32[]{:S(2)}, u32[]{:S(2)}) collective-permute-start(bf16[512,512]{1,0:T(8,128)(2,1)S(1)} %pad_maximum_fusion.2.refs_1_.refs_3_.refs_4_), channel_id=1, source_target_pairs={{0,16},{8,24},{16,0},{24,8},{32,48},{40,56},{48,32},{56,40},{64,80... | collective-permute-start | bytes 1572872 | tf_op jit(solution)/shard_map/ppermute | solution.py:38
  24.3 2.2 %copy-start.1 = (bf16[512,4096]{1,0:T(8,128)(2,1)S(1)}, bf16[512,4096]{1,0:T(8,128)(2,1)}, u32[]{:S(2)}) copy-start(bf16[512,4096]{1,0:T(8,128)(2,1)} %g_own.3) | copy-start | bytes 12582916
  37.0 5.3 %collective-permute-start.10 = (bf16[512,2048]{1,0:T(8,128)(2,1)S(1)}, bf16[512,2048]{1,0:T(8,128)(2,1)S(1)}, u32[]{:S(2)}, u32[]{:S(2)}) collective-permute-start(bf16[512,2048]{1,0:T(8,128)(2,1)S(1)} %get-tuple-element.107), channel_id=1, source_target_pairs={{0,8},{8,0},{16,24},{24,16},{32,40},{40,32},{48,56},{56,48},{64,72... | collective-permute-start | bytes 6291464 | tf_op jit(solution)/shard_map/ppermute | solution.py:38
  39.3 2.9 %collective-permute-start.8 = (bf16[256,1024]{1,0:T(8,128)(2,1)S(1)}, bf16[256,1024]{1,0:T(8,128)(2,1)S(1)}, u32[]{:S(2)}, u32[]{:S(2)}) collective-permute-start(bf16[256,1024]{1,0:T(8,128)(2,1)S(1)} %get-tuple-element.135.o_ref), channel_id=1, source_target_pairs={{0,8},{8,0},{16,24},{24,16},{32,40},{40,32},{48,56},{56,48},{64,72... | collective-permute-start | bytes 1572872 | tf_op jit(solution)/shard_map/ppermute | solution.py:38
  39.9 2.3 %collective-permute-start.9 = (bf16[256,512]{1,0:T(8,128)(2,1)S(1)}, bf16[256,512]{1,0:T(8,128)(2,1)S(1)}, u32[]{:S(2)}, u32[]{:S(2)}) collective-permute-start(bf16[256,512]{1,0:T(8,128)(2,1)S(1)} %get-tuple-element.106), channel_id=1, source_target_pairs={{0,8},{8,0},{16,24},{24,16},{32,40},{40,32},{48,56},{56,48},{64,72... | collective-permute-start | bytes 786440 | tf_op jit(solution)/shard_map/ppermute | solution.py:38
  42.3 5.7 %copy-start.2 = (bf16[512,4096]{1,0:T(8,128)(2,1)S(1)}, bf16[512,4096]{1,0:T(8,128)(2,1)}, u32[]{:S(2)}) copy-start(bf16[512,4096]{1,0:T(8,128)(2,1)} %g_own.3) | copy-start | bytes 12582916
  44.7 18.7 %collective-permute-start.11 = (bf16[512,512]{1,0:T(8,128)(2,1)S(1)}, bf16[512,512]{1,0:T(8,128)(2,1)S(1)}, u32[]{:S(2)}, u32[]{:S(2)}) collective-permute-start(bf16[512,512]{1,0:T(8,128)(2,1)S(1)} %get-tuple-element.121), channel_id=1, source_target_pairs={{0,6},{1,7},{2,4},{3,5},{4,2},{5,3},{6,0},{7,1},{8,14},{9,15},{10,... | collective-permute-start | bytes 1572872 | tf_op jit(solution)/shard_map/ppermute | solution.py:38
  47.8 15.7 %collective-permute-start.12 = (bf16[512,512]{1,0:T(8,128)(2,1)S(1)}, bf16[512,512]{1,0:T(8,128)(2,1)S(1)}, u32[]{:S(2)}, u32[]{:S(2)}) collective-permute-start(bf16[512,512]{1,0:T(8,128)(2,1)S(1)} %get-tuple-element.109), channel_id=1, source_target_pairs={{0,2},{1,3},{2,0},{3,1},{4,6},{5,7},{6,4},{7,5},{8,10},{9,11},{10,... | collective-permute-start | bytes 1572872 | tf_op jit(solution)/shard_map/ppermute | solution.py:38
  50.6 29.3 %collective-permute-start.21 = (bf16[4,2,256,256]{3,2,1,0:T(8,128)(2,1)S(1)}, bf16[4,2,256,256]{3,2,1,0:T(8,128)(2,1)S(1)}, u32[]{:S(2)}, u32[]{:S(2)}) collective-permute-start(bf16[4,2,256,256]{3,2,1,0:T(8,128)(2,1)S(1)} %weight_term.2), channel_id=1, source_target_pairs={{0,16},{8,24},{16,0},{24,8},{32,48},{40,56},{48,32},{56,40},{64,80... | collective-permute-start | bytes 3145736 | tf_op jit(solution)/shard_map/ppermute | solution.py:38
  58.1 8.9 %collective-permute-start.19 = (bf16[256,512]{1,0:T(8,128)(2,1)S(1)}, bf16[256,512]{1,0:T(8,128)(2,1)S(1)}, u32[]{:S(2)}, u32[]{:S(2)}) collective-permute-start(bf16[256,512]{1,0:T(8,128)(2,1)S(1)} %get-tuple-element.140), channel_id=1, source_target_pairs={{0,96},{8,104},{16,112},{24,120},{32,64},{40,72},{48,80},{56,88},{... | collective-permute-start | bytes 786440 | tf_op jit(solution)/shard_map/ppermute | solution.py:38
  60.4 16.5 %collective-permute-start.18 = (bf16[512,512]{1,0:T(8,128)(2,1)S(1)}, bf16[512,512]{1,0:T(8,128)(2,1)S(1)}, u32[]{:S(2)}, u32[]{:S(2)}) collective-permute-start(bf16[512,512]{1,0:T(8,128)(2,1)S(1)} %get-tuple-element.139), channel_id=1, source_target_pairs={{0,32},{8,40},{16,48},{24,56},{32,0},{40,8},{48,16},{56,24},{64,96... | collective-permute-start | bytes 1572872 | tf_op jit(solution)/shard_map/ppermute | solution.py:38
  63.6 19.5 %collective-permute-start.13 = (bf16[768,512]{1,0:T(8,128)(2,1)S(1)}, bf16[768,512]{1,0:T(8,128)(2,1)S(1)}, u32[]{:S(2)}, u32[]{:S(2)}) collective-permute-start(bf16[768,512]{1,0:T(8,128)(2,1)S(1)} %pad_maximum_fusion), channel_id=1, source_target_pairs={{0,2},{1,3},{2,0},{3,1},{4,6},{5,7},{6,4},{7,5},{8,10},{9,11},{10,... | collective-permute-start | bytes 2359304 | tf_op jit(solution)/shard_map/ppermute | solution.py:38
  65.6 19.4 %collective-permute-start.14 = (bf16[768,512]{1,0:T(8,128)(2,1)S(1)}, bf16[768,512]{1,0:T(8,128)(2,1)S(1)}, u32[]{:S(2)}, u32[]{:S(2)}) collective-permute-start(bf16[768,512]{1,0:T(8,128)(2,1)S(1)} %pad_maximum_fusion.1), channel_id=1, source_target_pairs={{0,6},{1,7},{2,4},{3,5},{4,2},{5,3},{6,0},{7,1},{8,14},{9,15},{10,... | collective-permute-start | bytes 2359304 | tf_op jit(solution)/shard_map/ppermute | solution.py:38
  67.0 12.4 %collective-permute-start.20 = (bf16[256,512]{1,0:T(8,128)(2,1)S(1)}, bf16[256,512]{1,0:T(8,128)(2,1)S(1)}, u32[]{:S(2)}, u32[]{:S(2)}) collective-permute-start(bf16[256,512]{1,0:T(8,128)(2,1)S(1)} %get-tuple-element.142), channel_id=1, source_target_pairs={{0,64},{8,72},{16,80},{24,88},{32,96},{40,104},{48,112},{56,120},{... | collective-permute-start | bytes 786440 | tf_op jit(solution)/shard_map/ppermute | solution.py:38
  80.2 7.8 %collective-permute-start.22 = (bf16[2,256,256]{2,1,0:T(8,128)(2,1)S(1)}, bf16[2,256,256]{2,1,0:T(8,128)(2,1)S(1)}, u32[]{:S(2)}, u32[]{:S(2)}) collective-permute-start(bf16[2,256,256]{2,1,0:T(8,128)(2,1)S(1)} %get-tuple-element.145), channel_id=1, source_target_pairs={{0,32},{8,40},{16,48},{24,56},{32,0},{40,8},{48,16},{56,24},{64,96... | collective-permute-start | bytes 786440 | tf_op jit(solution)/shard_map/ppermute | solution.py:38
  80.3 7.7 %collective-permute-start.23 = (bf16[2,256,256]{2,1,0:T(8,128)(2,1)S(1)}, bf16[2,256,256]{2,1,0:T(8,128)(2,1)S(1)}, u32[]{:S(2)}, u32[]{:S(2)}) collective-permute-start(bf16[2,256,256]{2,1,0:T(8,128)(2,1)S(1)} %get-tuple-element.146), channel_id=1, source_target_pairs={{0,96},{8,104},{16,112},{24,120},{32,64},{40,72},{48,80},{56,88},{... | collective-permute-start | bytes 786440 | tf_op jit(solution)/shard_map/ppermute | solution.py:38
  82.6 14.9 %collective-permute-start.26 = (bf16[512,512]{1,0:T(8,128)(2,1)S(1)}, bf16[512,512]{1,0:T(8,128)(2,1)S(1)}, u32[]{:S(2)}, u32[]{:S(2)}) collective-permute-start(bf16[512,512]{1,0:T(8,128)(2,1)S(1)} %relay.1), channel_id=1, source_target_pairs={{0,16},{8,24},{16,0},{24,8},{32,48},{40,56},{48,32},{56,40},{64,80... | collective-permute-start | bytes 1572872 | tf_op jit(solution)/shard_map/ppermute | solution.py:38
  85.2 22.6 %collective-permute-start.17 = (bf16[512,512]{1,0:T(8,128)(2,1)S(1)}, bf16[512,512]{1,0:T(8,128)(2,1)S(1)}, u32[]{:S(2)}, u32[]{:S(2)}) collective-permute-start(bf16[512,512]{1,0:T(8,128)(2,1)S(1)} %cross.1), channel_id=1, source_target_pairs={{0,1},{1,0},{2,3},{3,2},{4,5},{5,4},{6,7},{7,6},{8,9},{9,8},{10,11... | collective-permute-start | bytes 1572872 | tf_op jit(solution)/shard_map/ppermute | solution.py:38
  88.1 6.3 %collective-permute-start.25 = (bf16[256,256]{1,0:T(8,128)(2,1)S(1)}, bf16[256,256]{1,0:T(8,128)(2,1)S(1)}, u32[]{:S(2)}, u32[]{:S(2)}) collective-permute-start(bf16[256,256]{1,0:T(8,128)(2,1)S(1)} %fusion), channel_id=1, source_target_pairs={{0,96},{8,104},{16,112},{24,120},{32,64},{40,72},{48,80},{56,88},{... | collective-permute-start | bytes 393224 | tf_op jit(solution)/shard_map/ppermute | solution.py:38
  90.4 5.0 %collective-permute-start.24 = (bf16[256,256]{1,0:T(8,128)(2,1)S(1)}, bf16[256,256]{1,0:T(8,128)(2,1)S(1)}, u32[]{:S(2)}, u32[]{:S(2)}) collective-permute-start(bf16[256,256]{1,0:T(8,128)(2,1)S(1)} %fusion.1), channel_id=1, source_target_pairs={{0,32},{8,40},{16,48},{24,56},{32,0},{40,8},{48,16},{56,24},{64,96... | collective-permute-start | bytes 393224 | tf_op jit(solution)/shard_map/ppermute | solution.py:38
  90.8 11.8 %collective-permute-start.16 = (bf16[256,512]{1,0:T(8,128)(2,1)S(1)}, bf16[256,512]{1,0:T(8,128)(2,1)S(1)}, u32[]{:S(2)}, u32[]{:S(2)}) collective-permute-start(bf16[256,512]{1,0:T(8,128)(2,1)S(1)} %add_convert_fusion), channel_id=1, source_target_pairs={{0,6},{1,7},{2,4},{3,5},{4,2},{5,3},{6,0},{7,1},{8,14},{9,15},{10,... | collective-permute-start | bytes 786440 | tf_op jit(solution)/shard_map/ppermute | solution.py:38
  98.8 10.1 %collective-permute-start.27 = (bf16[512,384]{1,0:T(8,128)(2,1)S(1)}, bf16[512,384]{1,0:T(8,128)(2,1)S(1)}, u32[]{:S(2)}, u32[]{:S(2)}) collective-permute-start(bf16[512,384]{1,0:T(8,128)(2,1)S(1)} %get-tuple-element.153), channel_id=1, source_target_pairs={{0,8},{8,0},{16,24},{24,16},{32,40},{40,32},{48,56},{56,48},{64,72... | collective-permute-start | bytes 1179656 | tf_op jit(solution)/shard_map/ppermute | solution.py:38
  98.8 10.0 %collective-permute-start.28 = (bf16[512,384]{1,0:T(8,128)(2,1)S(1)}, bf16[512,384]{1,0:T(8,128)(2,1)S(1)}, u32[]{:S(2)}, u32[]{:S(2)}) collective-permute-start(bf16[512,384]{1,0:T(8,128)(2,1)S(1)} %get-tuple-element.154), channel_id=1, source_target_pairs={{0,8},{8,0},{16,24},{24,16},{32,40},{40,32},{48,56},{56,48},{64,72... | collective-permute-start | bytes 1179656 | tf_op jit(solution)/shard_map/ppermute | solution.py:38
  99.4 8.4 %collective-permute-start.15 = (bf16[256,512]{1,0:T(8,128)(2,1)S(1)}, bf16[256,512]{1,0:T(8,128)(2,1)S(1)}, u32[]{:S(2)}, u32[]{:S(2)}) collective-permute-start(bf16[256,512]{1,0:T(8,128)(2,1)S(1)} %add_convert_fusion.1), channel_id=1, source_target_pairs={{0,2},{1,3},{2,0},{3,1},{4,6},{5,7},{6,4},{7,5},{8,10},{9,11},{10,... | collective-permute-start | bytes 786440 | tf_op jit(solution)/shard_map/ppermute | solution.py:38
  (3 other events, 3.1 us)
